TPU v7x, 256 devices: a whole 4x4x8 slice. The times are simulated.
256 devices in a mesh: gx: 8 (over z), gy: 8 (over x, core), gz: 4 (over y).
Axes of the slice: x: 4, y: 4, z: 8, core: 2. Of those that a mesh axis runs over, the one named last changes fastest.
Arguments:
- tri_geom: float32 [10, 2097152], P(None, ('gx', 'gy', 'gz')), as said below
- send_index: int32 [16384, 128], P(('gx', 'gy', 'gz')), may hold values from -1 to 8191, as said below
- near_index: int32 [64, 256, 512], P('gx', 'gy', 'gz'), may hold values from 0 to 8191, as said below
- return_cell: int32 [3, 2097152], P(None, ('gx', 'gy', 'gz')), may hold values from -1 to 32767, as said below
- velocity: float32 [3, 64, 256, 512], P(None, 'gx', 'gy', 'gz'), may hold values from -6 to 6
Outputs:
- new_velocity: float32 [3, 64, 256, 512], P(None, 'gx', 'gy', 'gz')
- indicator: float32 [64, 256, 512], P('gx', 'gy', 'gz')
- vertex_velocity: float32 [9, 2097152], P(None, ('gx', 'gy', 'gz'))
Inputs may be any that keep to these rules, and one draw needn't show every extreme that they name: `send_index`: each row lists distinct local triangle indices of its owner in its first entries and -1 in the rest; every row has at least one triangle; an owner lists each of its triangles at most once over all its rows; for some bricks every owner fills all 128 slots. `near_index`: A value j * 128 + k names a slot that holds a triangle: k is below the number of triangles that owner j of the cell's row along gz lists for the cell's brick. `return_cell`: -1 where the vertex lies outside the brick. `tri_geom`: row 9 lies between 0.25 and 3.
All inputs are finite; a program needn't handle non-finite values.
Results may differ from a plain program's by a relative error of at most 0.0003.
Values sent between devices are 32-bit elements; how exact they have to be, the bound alone decides.
No kernel may reach another device: no remote copies, remote signals or barrier semaphores. Data moves between devices by JAX's collectives and lax.ppermute only.
A program may use at most 128 MiB of HBM per device.

v0:
```python
import jax
import jax.numpy as jnp
from jax import lax
from jax.sharding import PartitionSpec as P

CAP = 128
NSWEEP = 4


time_step = 0.04
smear_width = 4.0
rho_liquid = 1.0
rho_gas = 0.05
mu_liquid = 2.0
mu_gas = 0.2


def extended(cells, sides, width):
    for axis, dim in sides:
        count = lax.axis_size(axis)
        head = lax.slice_in_dim(cells, 0, width, axis=dim)
        tail = lax.slice_in_dim(cells, cells.shape[dim] - width, cells.shape[dim], axis=dim)
        cells = jnp.concatenate(
            [
                lax.ppermute(tail, axis, [(i, (i + 1) % count) for i in range(count)]),
                cells,
                lax.ppermute(head, axis, [((i + 1) % count, i) for i in range(count)]),
            ],
            axis=dim,
        )
    return cells


def slot_table(slots):
    first = slots[0:3]
    second = slots[3:6]
    third = slots[6:9]
    edge_one = second - first
    edge_two = third - first
    normal_x = edge_one[1] * edge_two[2] - edge_one[2] * edge_two[1]
    normal_y = edge_one[2] * edge_two[0] - edge_one[0] * edge_two[2]
    normal_z = edge_one[0] * edge_two[1] - edge_one[1] * edge_two[0]
    length = jnp.sqrt(normal_x * normal_x + normal_y * normal_y + normal_z * normal_z)
    scale = jnp.maximum(length, 1.0)
    centre = (first + second + third) / 3.0
    return jnp.stack(
        [
            normal_x / scale,
            normal_y / scale,
            normal_z / scale,
            centre[0],
            centre[1],
            centre[2],
            slots[9],
        ]
    )


def coefficients(padded_ind, tension):
    gradient = jnp.stack(
        [
            (padded_ind[2:, 1:-1, 1:-1] - padded_ind[:-2, 1:-1, 1:-1]) * 0.5,
            (padded_ind[1:-1, 2:, 1:-1] - padded_ind[1:-1, :-2, 1:-1]) * 0.5,
            (padded_ind[1:-1, 1:-1, 2:] - padded_ind[1:-1, 1:-1, :-2]) * 0.5,
        ]
    )
    core_ind = padded_ind[1:-1, 1:-1, 1:-1]
    density = rho_liquid + (rho_gas - rho_liquid) * core_ind
    viscosity = mu_liquid + (mu_gas - mu_liquid) * core_ind
    return (viscosity / density, tension * gradient / density)


def stencil(padded):
    laplace = padded[:, 2:, 1:-1, 1:-1] + padded[:, :-2, 1:-1, 1:-1]
    laplace = laplace + padded[:, 1:-1, 2:, 1:-1] + padded[:, 1:-1, :-2, 1:-1]
    laplace = laplace + padded[:, 1:-1, 1:-1, 2:] + padded[:, 1:-1, 1:-1, :-2]
    return laplace - 6.0 * padded[:, 1:-1, 1:-1, 1:-1]


def per_device(tri_geom, send_index, near_index, return_cell, velocity):
    count_x = lax.axis_size("gx")
    count_y = lax.axis_size("gy")
    group_size = count_x * count_y
    tri_dev = tri_geom.shape[1]
    filled = send_index >= 0
    outgoing = jnp.take(tri_geom, jnp.maximum(send_index, 0).reshape(-1), axis=1).reshape(
        10, group_size, CAP
    )
    outgoing = jnp.where(filled[None], outgoing, 0.0)
    arrived = lax.all_to_all(outgoing, ("gx", "gy"), split_axis=1, concat_axis=1, tiled=True)
    lookup = slot_table(arrived.reshape(10, group_size * CAP))
    size_x, size_y, size_z = near_index.shape
    picked = jnp.take(lookup, near_index.reshape(-1), axis=1).reshape(7, size_x, size_y, size_z)
    pos_x = (lax.axis_index("gx") * size_x + jnp.arange(size_x)).astype(jnp.float32)[
        :, None, None
    ] + 0.5
    pos_y = (lax.axis_index("gy") * size_y + jnp.arange(size_y)).astype(jnp.float32)[
        None, :, None
    ] + 0.5
    pos_z = (lax.axis_index("gz") * size_z + jnp.arange(size_z)).astype(jnp.float32)[
        None, None, :
    ] + 0.5
    distance = (
        picked[0] * (pos_x - picked[3])
        + picked[1] * (pos_y - picked[4])
        + picked[2] * (pos_z - picked[5])
    )
    indicator = 0.5 * (1.0 + jnp.tanh(distance / smear_width))
    tension = picked[6]
    padded_ind = extended(indicator, (("gx", 0), ("gy", 1), ("gz", 2)), 1)
    diffusion, forcing = coefficients(padded_ind, tension)
    current = velocity
    for repeat in range(NSWEEP):
        padded = extended(current, (("gx", 1), ("gy", 2), ("gz", 3)), 1)
        laplace = stencil(padded)
        current = current + time_step * (diffusion * laplace + forcing)
    flat_field = current.reshape(3, -1)
    slot_count = return_cell.shape[1]
    taken = jnp.take(flat_field, jnp.maximum(return_cell, 0).reshape(-1), axis=1).reshape(
        3, 3, slot_count
    )
    samples = jnp.where(return_cell[None] >= 0, taken, 0.0).reshape(9, slot_count)
    returned = lax.all_to_all(
        samples.reshape(9, group_size, CAP), ("gx", "gy"), split_axis=1, concat_axis=1, tiled=True
    )
    target = jnp.where(filled, send_index, tri_dev).reshape(-1)
    vertex_velocity = (
        jnp.zeros((9, tri_dev), jnp.float32).at[:, target].add(returned.reshape(9, -1), mode="drop")
    )
    return (current, indicator, vertex_velocity)


def solution(mesh):
    placed = (
        P(None, ("gx", "gy", "gz")),
        P(("gx", "gy", "gz"), None),
        P("gx", "gy", "gz"),
        P(None, ("gx", "gy", "gz")),
        P(None, "gx", "gy", "gz"),
    )
    return jax.shard_map(
        per_device,
        mesh=mesh,
        in_specs=placed,
        out_specs=(P(None, "gx", "gy", "gz"), P("gx", "gy", "gz"), P(None, ("gx", "gy", "gz"))),
        check_vma=False,
    )
```

profile of v0, /device:TPU:1, one launch (start us, length us, event | category | flops | bytes accessed | tf_op | source)
XLA Modules:
  0.0 539.5 jit_solution(3968862753052948591)
XLA Ops:
  0.7 1.4 broadcast_select_fusion
  2.1 0.8 broadcast_compare_fusion.2
  2.9 3.6 copy.41
  6.5 30.0 %gather_fusion = f32[8192,10]{1,0:T(8,128)} fusion(f32[10,8192]{0,1:T(8,128)} %copy.41, s32[8192]{0:T(1024)S(1)} %broadcast_clamp_fusion.2), kind=kCustom, calls=%fused_computation | custom fusion | bytes 688128 | tf_op jit(solution)/shard_map/jit(_take)/gather | solution.py:86
  36.4 2.8 copy.42
  39.3 0.9 select_select_fusion
  40.2 13.0 %all-to-all-start = ((f32[10,64,128]{2,0,1:T(8,128)}), f32[10,64,128]{2,0,1:T(8,128)S(1)}, u32[]{:S(2)}, u32[]{:S(2)}) async-start(f32[10,64,128]{2,0,1:T(8,128)} %select_select_fusion), calls=%async_computation | async-start | bytes 1048576 | tf_op jit(solution)/shard_map/all_to_all | solution.py:90
  53.2 1.5 collective-permute-start.1
  54.7 2.0 collective-permute-start
  57.0 11.4 %collective-permute-done.1 = f32[3,1,32,128]{3,2,1,0:T(8,128)S(1)} collective-permute-done((f32[3,1,32,128]{3,2,1,0:T(8,128)S(1)}, f32[3,1,32,128]{3,2,1,0:T(8,128)S(1)}, u32[]{:S(2)}, u32[]{:S(2)}) %collective-permute-start.1) | collective-permute-done | bytes 49184 | tf_op jit(solution)/shard_map/ppermute | solution.py:25
  68.5 1.2 collective-permute-start.2
  69.7 0.8 collective-permute-start.3
  70.5 1.4 collective-permute-done.2
  72.0 0.5 copy-done.8
  73.3 2.7 copy.43
  76.0 110.7 %gather_fusion.1 = f32[32768,7]{1,0:T(8,128)} fusion(f32[7,8192]{0,1:T(8,128)} %copy.43, s32[32768]{0:T(1024)S(1)} %broadcast_clamp_fusion), kind=kCustom, calls=%fused_computation.1 | custom fusion | bytes 1966080 | tf_op jit(solution)/shard_map/jit(_take)/gather | solution.py:93
  186.6 19.1 %select_bitcast_fusion = f32[7,32768]{0,1:T(8,128)} fusion(f32[32768,7]{1,0:T(8,128)} %gather_fusion.1, pred[32768]{0:T(1024)(128)(4,1)S(1)} %compare_and_fusion), kind=kLoop, calls=%fused_computation.11 | loop fusion | flops 229376 | bytes 1867776 | tf_op jit(solution)/shard_map/jit(_take)/select_n | solution.py:93
  205.7 67.6 %slice_reduce_fusion = (f32[32768]{0:T(1024)S(1)}, f32[32768]{0:T(1024)S(1)}, f32[32768]{0:T(1024)S(1)}, f32[32768]{0:T(1024)S(1)}, f32[32768]{0:T(1024)S(1)}, /*index=5*/f32[32768]{0:T(1024)S(1)}, f32[32768]{0:T(1024)S(1)}) fusion(f32[7,32768]{0,1:T(8,128)} %select_bitcast_fusion), kind=kLoop, calls=%fused_computation.4 | loop fusion | bytes 1835008 | tf_op jit(solution)/shard_map/slice | solution.py:109
  273.4 1.5 collective-permute-start.6
  275.5 2.8 collective-permute-start.4
  279.5 3.1 collective-permute-done.5
  283.0 5.5 %collective-permute-start.8 = (f32[10,1,128]{2,1,0:T(1,128)S(1)}, f32[10,1,128]{2,1,0:T(1,128)S(1)}, u32[]{:S(2)}, u32[]{:S(2)}) collective-permute-start(f32[10,1,128]{2,1,0:T(1,128)S(1)} %get-tuple-element.60), channel_id=1, source_target_pairs={{4,0},{8,4},{12,8},{16,12},{20,16},{24,20},{28,24},{0,28},{5,1},{9... | collective-permute-start | bytes 15368 | tf_op jit(solution)/shard_map/ppermute | solution.py:27
  288.5 0.8 collective-permute-done.8
  289.9 1.5 collective-permute-start.11
  291.4 3.1 collective-permute-done.10
  294.5 1.3 collective-permute-done.11
  296.0 2.0 fusion.37
  298.0 2.7 collective-permute-start.12
  300.7 1.2 collective-permute-done.12
  301.9 3.0 collective-permute-done.13
  304.9 5.7 %collective-permute-start.14 = (f32[3,10,1,128]{3,2,1,0:T(1,128)S(1)}, f32[3,10,1,128]{3,2,1,0:T(1,128)S(1)}, u32[]{:S(2)}, u32[]{:S(2)}) collective-permute-start(f32[3,10,1,128]{3,2,1,0:T(1,128)S(1)} %get-tuple-element.44), channel_id=1, source_target_pairs={{4,0},{8,4},{12,8},{16,12},{20,16},{24,20},{28,24},{0,28},{5,1},{9... | collective-permute-start | bytes 46088 | tf_op jit(solution)/shard_map/ppermute | solution.py:27
  310.6 0.8 collective-permute-done.14
  311.4 0.3 collective-permute-done.15
  312.7 1.5 collective-permute-start.17
  314.2 0.8 collective-permute-done.16
  315.3 1.2 collective-permute-done.17
  316.9 0.5 fusion.27
  317.6 1.5 collective-permute-start.19
  319.0 1.5 collective-permute-done.18
  320.5 1.3 collective-permute-done.19
  321.8 5.5 %collective-permute-start.20 = (f32[3,10,1,128]{3,2,1,0:T(1,128)S(1)}, f32[3,10,1,128]{3,2,1,0:T(1,128)S(1)}, u32[]{:S(2)}, u32[]{:S(2)}) collective-permute-start(f32[3,10,1,128]{3,2,1,0:T(1,128)S(1)} %get-tuple-element.42), channel_id=1, source_target_pairs={{4,0},{8,4},{12,8},{16,12},{20,16},{24,20},{28,24},{0,28},{5,1},{9... | collective-permute-start | bytes 46088 | tf_op jit(solution)/shard_map/ppermute | solution.py:27
  327.3 0.8 collective-permute-done.20
  329.5 1.5 collective-permute-start.23
  331.2 0.6 collective-permute-done.22
  332.1 1.2 collective-permute-done.23
  333.7 0.5 fusion.17
  334.5 1.5 collective-permute-start.25
  336.1 1.4 collective-permute-done.24
  337.5 1.5 collective-permute-done.25
  339.0 5.6 %collective-permute-start.26 = (f32[3,10,1,128]{3,2,1,0:T(1,128)S(1)}, f32[3,10,1,128]{3,2,1,0:T(1,128)S(1)}, u32[]{:S(2)}, u32[]{:S(2)}) collective-permute-start(f32[3,10,1,128]{3,2,1,0:T(1,128)S(1)} %get-tuple-element.40), channel_id=1, source_target_pairs={{4,0},{8,4},{12,8},{16,12},{20,16},{24,20},{28,24},{0,28},{5,1},{9... | collective-permute-start | bytes 46088 | tf_op jit(solution)/shard_map/ppermute | solution.py:27
  344.7 0.7 collective-permute-done.26
  346.4 0.6 collective-permute-start.28
  347.2 1.0 collective-permute-start.29
  349.3 1.8 collective-permute-done.29
  351.4 0.5 fusion.7
  352.0 8.7 %copy.60 = f32[3,8,32,128]{0,3,2,1:T(8,128)} copy(f32[3,8,32,128]{3,2,1,0:T(8,128)S(1)} %fusion.7) | data formatting | bytes 786432 | tf_op jit(solution)/shard_map/add | solution.py:116
  360.7 87.3 %gather_fusion.2 = f32[24576,3]{1,0:T(8,128)} fusion(f32[3,32768]{0,1:T(8,128)} %bitcast.62, s32[24576]{0:T(1024)S(1)} %broadcast_clamp_fusion.1), kind=kCustom, calls=%fused_computation.2 | custom fusion | bytes 688128 | tf_op jit(solution)/shard_map/jit(_take)/gather | solution.py:119
  447.9 7.7 %copy.61 = f32[3,24576]{1,0:T(4,128)S(1)} copy(f32[3,24576]{0,1:T(8,128)} %bitcast.63) | data formatting | bytes 589824 | tf_op jit(solution)/shard_map/jit(_take)/gather | solution.py:119
  456.0 1.0 copy.62
  456.9 11.4 %all-to-all-start.1 = ((f32[9,64,128]{2,0,1:T(8,128)}), f32[9,64,128]{2,0,1:T(8,128)S(1)}, u32[]{:S(2)}, u32[]{:S(2)}) async-start(f32[9,64,128]{2,0,1:T(8,128)} %copy.62), calls=%async_computation.1 | async-start | bytes 1048576 | tf_op jit(solution)/shard_map/all_to_all | solution.py:123
  468.4 17.7 %all-to-all-done.1 = f32[9,64,128]{2,0,1:T(8,128)S(1)} async-done(((f32[9,64,128]{2,0,1:T(8,128)}), f32[9,64,128]{2,0,1:T(8,128)S(1)}, u32[]{:S(2)}, u32[]{:S(2)}) %all-to-all-start.1) | async-done | bytes 294944 | tf_op jit(solution)/shard_map/all_to_all | solution.py:123
  486.5 2.7 copy.64
  489.2 46.5 %scatter_custom_fusion = f32[9,8192]{0,1:T(8,128)} fusion(s32[8192]{0:T(1024)S(1)} %bitcast.85, f32[8192,9]{1,0:T(8,128)} %copy.64, f32[]{:T(128)} %constant.41.clone.1), kind=kCustom, calls=%fused_computation.12 | custom fusion | flops 73728 | bytes 295424 | tf_op jit(solution)/shard_map/scatter-add | solution.py:128
  535.8 3.5 copy.65
  (112 shorter events, 12.1 us)
Async XLA Ops:
  0.6 52.6 %copy-start.1 = (f32[3,8,32,128]{3,2,1,0:T(8,128)S(1)}, f32[3,8,32,128]{3,2,1,0:T(8,128)}, u32[]{:S(2)}) copy-start(f32[3,8,32,128]{3,2,1,0:T(8,128)} %param.9) | copy-start | bytes 1179652
  0.6 56.1 %copy-start.3 = (s32[8,32,128]{2,1,0:T(8,128)S(1)}, s32[8,32,128]{2,1,0:T(8,128)}, u32[]{:S(2)}) copy-start(s32[8,32,128]{2,1,0:T(8,128)} %param.7) | copy-start | bytes 393220
  40.2 32.3 %all-to-all-start = ((f32[10,64,128]{2,0,1:T(8,128)}), f32[10,64,128]{2,0,1:T(8,128)S(1)}, u32[]{:S(2)}, u32[]{:S(2)}) async-start(f32[10,64,128]{2,0,1:T(8,128)} %select_select_fusion), calls=%async_computation | async-start | bytes 1048576 | tf_op jit(solution)/shard_map/all_to_all | solution.py:90
  53.2 15.2 %collective-permute-start.1 = (f32[3,1,32,128]{3,2,1,0:T(8,128)S(1)}, f32[3,1,32,128]{3,2,1,0:T(8,128)S(1)}, u32[]{:S(2)}, u32[]{:S(2)}) collective-permute-start(f32[3,1,32,128]{3,2,1,0:T(8,128)S(1)} %get-tuple-element.54), channel_id=1, source_target_pairs={{0,32},{32,64},{64,96},{96,128},{128,160},{160,192},{192,224},{224... | collective-permute-start | bytes 147464 | tf_op jit(solution)/shard_map/ppermute | solution.py:25
  54.7 13.7 %collective-permute-start = (f32[3,1,32,128]{3,2,1,0:T(8,128)S(1)}, f32[3,1,32,128]{3,2,1,0:T(8,128)S(1)}, u32[]{:S(2)}, u32[]{:S(2)}) collective-permute-start(f32[3,1,32,128]{3,2,1,0:T(8,128)S(1)} %get-tuple-element.53), channel_id=1, source_target_pairs={{32,0},{64,32},{96,64},{128,96},{160,128},{192,160},{224,192},{0,2... | collective-permute-start | bytes 147464 | tf_op jit(solution)/shard_map/ppermute | solution.py:27
  68.4 3.5 copy-start.5
  68.4 3.5 copy-start.6
  68.5 3.4 collective-permute-start.2
  69.7 2.2 collective-permute-start.3
  71.9 0.6 copy-start.8
  71.9 0.6 copy-start.9
  273.4 55.4 %copy-start = (f32[8,32,128]{2,1,0:T(8,128)}, f32[8,32,128]{2,1,0:T(8,128)S(1)}, u32[]{:S(2)}) copy-start(f32[8,32,128]{2,1,0:T(8,128)S(1)} %get-tuple-element.22) | copy-start | bytes 393220
  273.4 9.5 %collective-permute-start.6 = (f32[1,32,128]{2,1,0:T(8,128)S(1)}, f32[1,32,128]{2,1,0:T(8,128)S(1)}, u32[]{:S(2)}, u32[]{:S(2)}) collective-permute-start(f32[1,32,128]{2,1,0:T(8,128)S(1)} %get-tuple-element.64), channel_id=1, source_target_pairs={{32,0},{64,32},{96,64},{128,96},{160,128},{192,160},{224,192},{0,2... | collective-permute-start | bytes 49160 | tf_op jit(solution)/shard_map/ppermute | solution.py:27
  274.9 8.0 %collective-permute-start.7 = (f32[1,32,128]{2,1,0:T(8,128)S(1)}, f32[1,32,128]{2,1,0:T(8,128)S(1)}, u32[]{:S(2)}, u32[]{:S(2)}) collective-permute-start(f32[1,32,128]{2,1,0:T(8,128)S(1)} %get-tuple-element.63), channel_id=1, source_target_pairs={{0,32},{32,64},{64,96},{96,128},{128,160},{160,192},{192,224},{224... | collective-permute-start | bytes 49160 | tf_op jit(solution)/shard_map/ppermute | solution.py:25
  275.2 55.8 %copy-start.4 = (s32[3,8192]{1,0:T(4,128)S(1)}, s32[3,8192]{1,0:T(4,128)}, u32[]{:S(2)}) copy-start(s32[3,8192]{1,0:T(4,128)} %param.8) | copy-start | bytes 294916
  275.5 3.7 collective-permute-start.4
  278.6 4.0 collective-permute-start.5
  283.0 6.3 %collective-permute-start.8 = (f32[10,1,128]{2,1,0:T(1,128)S(1)}, f32[10,1,128]{2,1,0:T(1,128)S(1)}, u32[]{:S(2)}, u32[]{:S(2)}) collective-permute-start(f32[10,1,128]{2,1,0:T(1,128)S(1)} %get-tuple-element.60), channel_id=1, source_target_pairs={{4,0},{8,4},{12,8},{16,12},{20,16},{24,20},{28,24},{0,28},{5,1},{9... | collective-permute-start | bytes 15368 | tf_op jit(solution)/shard_map/ppermute | solution.py:27
  288.5 1.2 collective-permute-start.9
  289.8 4.7 collective-permute-start.10
  289.9 5.9 %collective-permute-start.11 = (f32[10,34,1]{2,1,0:T(8,128)S(1)}, f32[10,34,1]{2,1,0:T(8,128)S(1)}, u32[]{:S(2)}, u32[]{:S(2)}) collective-permute-start(f32[10,34,1]{2,1,0:T(8,128)S(1)} %get-tuple-element.56), channel_id=1, source_target_pairs={{0,1},{1,2},{2,3},{3,0},{4,5},{5,6},{6,7},{7,4},{8,9},{9,10},{10,1... | collective-permute-start | bytes 4088 | tf_op jit(solution)/shard_map/ppermute | solution.py:25
  298.0 3.9 collective-permute-start.12
  300.7 4.2 collective-permute-start.13
  304.9 6.5 %collective-permute-start.14 = (f32[3,10,1,128]{3,2,1,0:T(1,128)S(1)}, f32[3,10,1,128]{3,2,1,0:T(1,128)S(1)}, u32[]{:S(2)}, u32[]{:S(2)}) collective-permute-start(f32[3,10,1,128]{3,2,1,0:T(1,128)S(1)} %get-tuple-element.44), channel_id=1, source_target_pairs={{4,0},{8,4},{12,8},{16,12},{20,16},{24,20},{28,24},{0,28},{5,1},{9... | collective-permute-start | bytes 46088 | tf_op jit(solution)/shard_map/ppermute | solution.py:27
  310.6 1.2 collective-permute-start.15
  312.4 2.6 collective-permute-start.16
  312.7 3.8 collective-permute-start.17
  317.5 3.1 collective-permute-start.18
  317.6 4.2 collective-permute-start.19
  321.8 6.4 %collective-permute-start.20 = (f32[3,10,1,128]{3,2,1,0:T(1,128)S(1)}, f32[3,10,1,128]{3,2,1,0:T(1,128)S(1)}, u32[]{:S(2)}, u32[]{:S(2)}) collective-permute-start(f32[3,10,1,128]{3,2,1,0:T(1,128)S(1)} %get-tuple-element.42), channel_id=1, source_target_pairs={{4,0},{8,4},{12,8},{16,12},{20,16},{24,20},{28,24},{0,28},{5,1},{9... | collective-permute-start | bytes 46088 | tf_op jit(solution)/shard_map/ppermute | solution.py:27
  327.3 1.2 collective-permute-start.21
  329.1 2.6 collective-permute-start.22
  329.5 3.8 collective-permute-start.23
  334.2 3.2 collective-permute-start.24
  334.5 4.4 collective-permute-start.25
  339.0 6.4 %collective-permute-start.26 = (f32[3,10,1,128]{3,2,1,0:T(1,128)S(1)}, f32[3,10,1,128]{3,2,1,0:T(1,128)S(1)}, u32[]{:S(2)}, u32[]{:S(2)}) collective-permute-start(f32[3,10,1,128]{3,2,1,0:T(1,128)S(1)} %get-tuple-element.40), channel_id=1, source_target_pairs={{4,0},{8,4},{12,8},{16,12},{20,16},{24,20},{28,24},{0,28},{5,1},{9... | collective-permute-start | bytes 46088 | tf_op jit(solution)/shard_map/ppermute | solution.py:27
  344.6 1.2 collective-permute-start.27
  346.4 2.6 collective-permute-start.28
  347.2 3.8 collective-permute-start.29
  352.0 103.7 %copy-start.2 = (f32[3,8,32,128]{3,2,1,0:T(8,128)}, f32[3,8,32,128]{3,2,1,0:T(8,128)S(1)}, u32[]{:S(2)}) copy-start(f32[3,8,32,128]{3,2,1,0:T(8,128)S(1)} %fusion.7) | copy-start | bytes 1179652
  360.7 107.7 %copy-start.7 = (s32[64,128]{1,0:T(8,128)S(1)}, s32[64,128]{1,0:T(8,128)}, u32[]{:S(2)}) copy-start(s32[64,128]{1,0:T(8,128)} %get-tuple-element.67) | copy-start | bytes 98308
  456.9 29.2 %all-to-all-start.1 = ((f32[9,64,128]{2,0,1:T(8,128)}), f32[9,64,128]{2,0,1:T(8,128)S(1)}, u32[]{:S(2)}, u32[]{:S(2)}) async-start(f32[9,64,128]{2,0,1:T(8,128)} %copy.62), calls=%async_computation.1 | async-start | bytes 1048576 | tf_op jit(solution)/shard_map/all_to_all | solution.py:123
where the time goes:
time: 543 us; the launch traced here: 540 us
  local copies, waits for them, and re-layouts  337 us (62%)
  other arithmetic  74.2 us (14%)
  starting transfers between devices  69.1 us (13%)
  waiting for transfers between devices  58.4 us (11%)
    gather x1, local copies, waits for them, and re-layouts, per_device(): jnp.take(lookup, near_index.reshape(-1), axis=1)  111 us
    gather x3, local copies, waits for them, and re-layouts, per_device(): jnp.take(flat_field, jnp.maximum(return_cell, 0).reshape(-1), axis=1)  95.2 us
    slice x1, local copies, waits for them, and re-layouts, per_device(): tension = picked[6]  67.6 us
    scatter-add x1, other arithmetic, per_device(): jnp.zeros((9, tri_dev), jnp.float32).at[:, target]  46.5 us
    ppermute x15, starting transfers between devices, extended(): lax.ppermute(head, axis, [((i + 1) % count, i) for i in range(count)])  33.7 us
    gather x2, local copies, waits for them, and re-layouts, per_device(): jnp.take(tri_geom, jnp.maximum(send_index, 0).reshape(-1), axis=1)  32.8 us
    ppermute x15, waiting for transfers between devices, extended(): lax.ppermute(tail, axis, [(i, (i + 1) % count) for i in range(count)])  27.1 us
    select_n x2, other arithmetic, per_device(): jnp.take(lookup, near_index.reshape(-1), axis=1)  19.2 us
  transfers between devices with their start and end apart: 32, of which 27 were waited for; matrix products, arithmetic and copies ran while one was open for 1% of the time, Pallas kernels for 0%

commit v1 on v0

v1 whole, which is shorter than its diff:
```python
import jax
import jax.numpy as jnp
from jax import lax
from jax.experimental import pallas as pl
from jax.experimental.pallas import tpu as pltpu
from jax.sharding import PartitionSpec as P

NSWEEP = 4

time_step = 0.04
rho_liquid = 1.0
rho_gas = 0.05
mu_liquid = 2.0
mu_gas = 0.2

F32, BF16, I32 = jnp.float32, jnp.bfloat16, jnp.int32
LANE = 128
VMEM = pl.BlockSpec(memory_space=pltpu.VMEM)


def one_hot(rows, index):
    level = lax.broadcasted_iota(I32, (rows, index.shape[1]), 0)
    return jnp.where(level == index, 1.0, 0.0).astype(BF16)


def fold_lines(lines):
    sub = lax.broadcasted_iota(I32, (8, LANE), 0)
    step = 1
    while step < 8:
        low = (sub & step) == 0
        lines = [
            jnp.where(low, even, odd) + pltpu.roll(jnp.where(low, odd, even), step, 0)
            for even, odd in zip(lines[0::2], lines[1::2])
        ]
        step *= 2
    return lines[0]


def parts_of(value, count):
    out = []
    for _ in range(count - 1):
        head = value.astype(BF16)
        out.append(head)
        value = value - head.astype(F32)
    out.append(value.astype(BF16))
    return out


def put_table(table_ref, columns, halves):
    for q, column in enumerate(columns):
        table_ref[q * halves:(q + 1) * halves, 0:LANE] = column[0:halves]
        table_ref[q * halves:(q + 1) * halves, LANE:2 * LANE] = column[halves:2 * halves]


def look_up(table_ref, groups, half, lines):
    shift = half.bit_length() - 1
    tiles = half // 8
    sub = lax.broadcasted_iota(I32, (8, LANE), 0)
    count = sum(groups)
    found = [[] for _ in groups]
    for pair in range(4):
        index = jnp.concatenate([lines[2 * pair], lines[2 * pair + 1]], axis=1)
        row = index >> 7
        hot = one_hot(2 * LANE, ((row >> shift) << 7) + (index & 127))
        product = jnp.dot(table_ref[...], hot, preferred_element_type=F32)
        place = jnp.where(index < 0, -1, row & (half - 1))
        for side in range(2):
            here = place[:, side * LANE:(side + 1) * LANE]
            masks = [sub + 8 * t == here for t in range(tiles)]
            picked = []
            for q in range(count):
                total = jnp.zeros((8, LANE), F32)
                for t in range(tiles):
                    start = q * half + 8 * t
                    total = jnp.where(masks[t], product[start:start + 8, side * LANE:(side + 1) * LANE], total)
                picked.append(total)
            at = 0
            for g, size in enumerate(groups):
                total = picked[at]
                for other in picked[at + 1:at + size]:
                    total = total + other
                found[g].append(total)
                at += size
    return [fold_lines(column) for column in found]


def send_kernel(geom_ref, send_ref, origin_ref, out_ref, dense_ref, table_ref):
    rows = geom_ref.shape[1] // LANE
    half = rows // 2
    for h in range(rows):
        dense_ref[pl.ds(h, 10, stride=rows), :] = geom_ref[:, h * LANE:(h + 1) * LANE]
    geom = [dense_ref[r * rows:(r + 1) * rows, :] for r in range(10)]
    one = [geom[3 + a] - geom[a] for a in range(3)]
    two = [geom[6 + a] - geom[a] for a in range(3)]
    normal = [
        one[1] * two[2] - one[2] * two[1],
        one[2] * two[0] - one[0] * two[2],
        one[0] * two[1] - one[1] * two[0],
    ]
    length = jnp.sqrt(normal[0] * normal[0] + normal[1] * normal[1] + normal[2] * normal[2])
    scale = jnp.maximum(length, 1.0)
    columns = []
    offset = jnp.zeros_like(length)
    for a in range(3):
        head, tail = parts_of(normal[a] / scale, 2)
        columns += [head, tail]
        centre = (geom[a] + geom[3 + a] + geom[6 + a]) / 3.0 - origin_ref[a]
        offset = offset + (head.astype(F32) + tail.astype(F32)) * centre
    columns += parts_of(offset, 3) + parts_of(geom[9], 2)
    put_table(table_ref, columns, half)

    @pl.loop(0, send_ref.shape[0] // 8)
    def _(tile):
        index = send_ref[pl.ds(tile * 8, 8), :]
        found = look_up(table_ref, (2, 2, 2, 3, 2), half, [index[s:s + 1] for s in range(8)])
        for q, value in enumerate(found):
            out_ref[pl.ds(tile * 64 + q, 8, stride=8), :] = value


def send_tables(geom, send, origin):
    rows = geom.shape[1] // LANE
    dests = send.shape[0]
    return pl.pallas_call(
        send_kernel,
        name="send_tables",
        out_shape=jax.ShapeDtypeStruct((dests * 8, LANE), F32),
        in_specs=[VMEM, VMEM, pl.BlockSpec(memory_space=pltpu.SMEM)],
        out_specs=VMEM,
        scratch_shapes=[pltpu.VMEM((10 * rows, LANE), F32), pltpu.VMEM((11 * rows // 2, 2 * LANE), BF16)],
        compiler_params=pltpu.CompilerParams(vmem_limit_bytes=40 << 20),
        cost_estimate=pl.CostEstimate(flops=2 << 40, bytes_accessed=1 << 20, transcendentals=0),
    )(geom, send, origin)


def cell_kernel(tab_ref, near_ref, origin_ref, ind_ref, ten_ref, table_ref):
    sources = tab_ref.shape[0] // 8
    half = sources // 2
    size_x, size_y, _ = near_ref.shape
    value = [tab_ref[pl.ds(q, sources, stride=8), :] for q in range(5)]
    columns = []
    offset = value[3]
    for a in range(3):
        columns += parts_of(value[a], 2)
        offset = offset - value[a] * origin_ref[a]
    columns += parts_of(offset, 3) + parts_of(value[4], 2)
    put_table(table_ref, columns, half)
    mid_x, mid_y, mid_z = 0.5 * size_x, 0.5 * size_y, 0.5 * LANE
    sub = lax.broadcasted_iota(I32, (8, LANE), 0).astype(F32)
    at_z = lax.broadcasted_iota(I32, (8, LANE), 1).astype(F32) + (0.5 - mid_z)
    tiles = size_y // 8

    @pl.loop(0, size_x * tiles)
    def _(step):
        x = lax.shift_right_logical(step, tiles.bit_length() - 1)
        y = pl.multiple_of((step & (tiles - 1)) * 8, 8)
        index = near_ref[x, pl.ds(y, 8), :]
        found = look_up(table_ref, (2, 2, 2, 3, 2), half, [index[s:s + 1] for s in range(8)])
        at_x = x.astype(F32) + (0.5 - mid_x)
        at_y = sub + (y.astype(F32) + (0.5 - mid_y))
        distance = found[0] * at_x + found[1] * at_y + found[2] * at_z - found[3]
        ind_ref[x, pl.ds(y, 8), :] = 0.5 * (1.0 + jnp.tanh(distance / 4.0))
        ten_ref[x, pl.ds(y, 8), :] = found[4]


def cell_fields(tab, near, origin):
    sources = tab.shape[0] // 8
    out = jax.ShapeDtypeStruct(near.shape, F32)
    return pl.pallas_call(
        cell_kernel,
        name="cell_fields",
        out_shape=(out, out),
        in_specs=[VMEM, VMEM, pl.BlockSpec(memory_space=pltpu.SMEM)],
        out_specs=(VMEM, VMEM),
        scratch_shapes=[pltpu.VMEM((11 * sources // 2, 2 * LANE), BF16)],
        compiler_params=pltpu.CompilerParams(vmem_limit_bytes=40 << 20),
        cost_estimate=pl.CostEstimate(flops=6 << 40, bytes_accessed=1 << 20, transcendentals=0),
    )(tab, near, origin)


def vertex_kernel(field_ref, cell_ref, out_ref, table_ref):
    comps, rows, _ = field_ref.shape
    half = rows // 2
    columns = []
    for c in range(comps):
        columns += parts_of(field_ref[c], 2)
    put_table(table_ref, columns, half)
    sources = cell_ref.shape[1] // LANE

    @pl.loop(0, sources // 8)
    def _(tile):
        for v in range(3):
            lines = [
                cell_ref[v:v + 1, pl.ds(pl.multiple_of((tile * 8 + s) * LANE, LANE), LANE)] for s in range(8)
            ]
            found = look_up(table_ref, (2, 2, 2), half, lines)
            for c in range(3):
                out_ref[pl.ds(tile * 72 + 3 * c + v, 8, stride=9), :] = found[c]


def vertex_samples(field, cells):
    comps, rows, _ = field.shape
    sources = cells.shape[1] // LANE
    return pl.pallas_call(
        vertex_kernel,
        name="vertex_samples",
        out_shape=jax.ShapeDtypeStruct((sources * 9, LANE), F32),
        in_specs=[VMEM, VMEM],
        out_specs=VMEM,
        scratch_shapes=[pltpu.VMEM((6 * rows // 2, 2 * LANE), BF16)],
        compiler_params=pltpu.CompilerParams(vmem_limit_bytes=40 << 20),
        cost_estimate=pl.CostEstimate(flops=10 << 40, bytes_accessed=1 << 20, transcendentals=0),
    )(field, cells)


def home_kernel(back_ref, send_ref, out_ref, left_ref, right_ref, total_ref):
    dests = send_ref.shape[0]
    blocks = out_ref.shape[1] // (2 * LANE)
    chunk = left_ref.shape[1] // (2 * LANE)
    total_ref[...] = jnp.zeros_like(total_ref)

    @pl.loop(0, dests // chunk)
    def _(step):
        for line in range(chunk):
            d = step * chunk + line
            index = send_ref[pl.ds(d, 1), :]
            low = slice(line * LANE, (line + 1) * LANE)
            high = slice((chunk + line) * LANE, (chunk + line + 1) * LANE)
            hot = one_hot(2 * LANE, index & (2 * LANE - 1))
            right_ref[:, low] = hot
            right_ref[:, high] = hot
            mine = lax.broadcasted_iota(I32, (blocks, LANE), 0) == (index >> 8)
            for r in range(9):
                value = back_ref[pl.ds(d * 9 + r, 1), :]
                head = value.astype(BF16).astype(F32)
                tail = value - head
                rows = slice(r * blocks, (r + 1) * blocks)
                left_ref[rows, low] = jnp.where(mine, head, 0.0).astype(BF16)
                left_ref[rows, high] = jnp.where(mine, tail, 0.0).astype(BF16)
        total_ref[...] += lax.dot_general(
            left_ref[...], right_ref[...], (((1,), (1,)), ((), ())), preferred_element_type=F32
        )

    for r in range(9):
        for b in range(blocks):
            at = r * blocks + b
            out_ref[r:r + 1, b * 2 * LANE:(b + 1) * 2 * LANE] = total_ref[at:at + 1, :]


def bring_home(back, send, triangles):
    blocks = triangles // (2 * LANE)
    chunk = 4
    return pl.pallas_call(
        home_kernel,
        name="bring_home",
        out_shape=jax.ShapeDtypeStruct((9, triangles), F32),
        in_specs=[VMEM, VMEM],
        out_specs=VMEM,
        scratch_shapes=[
            pltpu.VMEM((9 * blocks, 2 * chunk * LANE), BF16),
            pltpu.VMEM((2 * LANE, 2 * chunk * LANE), BF16),
            pltpu.VMEM((9 * blocks, 2 * LANE), F32),
        ],
        compiler_params=pltpu.CompilerParams(vmem_limit_bytes=40 << 20),
        cost_estimate=pl.CostEstimate(flops=2 << 40, bytes_accessed=1 << 20, transcendentals=0),
    )(back, send)


def extended(cells, sides, width):
    for axis, dim in sides:
        count = lax.axis_size(axis)
        head = lax.slice_in_dim(cells, 0, width, axis=dim)
        tail = lax.slice_in_dim(cells, cells.shape[dim] - width, cells.shape[dim], axis=dim)
        cells = jnp.concatenate(
            [
                lax.ppermute(tail, axis, [(i, (i + 1) % count) for i in range(count)]),
                cells,
                lax.ppermute(head, axis, [((i + 1) % count, i) for i in range(count)]),
            ],
            axis=dim,
        )
    return cells


def coefficients(padded_ind, tension):
    gradient = jnp.stack(
        [
            (padded_ind[2:, 1:-1, 1:-1] - padded_ind[:-2, 1:-1, 1:-1]) * 0.5,
            (padded_ind[1:-1, 2:, 1:-1] - padded_ind[1:-1, :-2, 1:-1]) * 0.5,
            (padded_ind[1:-1, 1:-1, 2:] - padded_ind[1:-1, 1:-1, :-2]) * 0.5,
        ]
    )
    core_ind = padded_ind[1:-1, 1:-1, 1:-1]
    density = rho_liquid + (rho_gas - rho_liquid) * core_ind
    viscosity = mu_liquid + (mu_gas - mu_liquid) * core_ind
    return (viscosity / density, tension * gradient / density)


def stencil(padded):
    laplace = padded[:, 2:, 1:-1, 1:-1] + padded[:, :-2, 1:-1, 1:-1]
    laplace = laplace + padded[:, 1:-1, 2:, 1:-1] + padded[:, 1:-1, :-2, 1:-1]
    laplace = laplace + padded[:, 1:-1, 1:-1, 2:] + padded[:, 1:-1, 1:-1, :-2]
    return laplace - 6.0 * padded[:, 1:-1, 1:-1, 1:-1]


def per_device(tri_geom, send_index, near_index, return_cell, velocity):
    size_x, size_y, size_z = near_index.shape
    group_x, group_y = lax.axis_size("gx"), lax.axis_size("gy")
    mid_z = (lax.axis_index("gz") * size_z + size_z // 2).astype(F32)
    mid_x, mid_y = 0.5 * group_x * size_x, 0.5 * group_y * size_y
    outgoing = send_tables(tri_geom, send_index, jnp.stack([jnp.float32(mid_x), jnp.float32(mid_y), mid_z]))
    arrived = lax.all_to_all(
        outgoing.reshape(-1, 8, LANE), ("gx", "gy"), split_axis=0, concat_axis=0, tiled=True
    ).reshape(-1, LANE)
    own_x = (lax.axis_index("gx") * size_x + size_x // 2).astype(F32) - mid_x
    own_y = (lax.axis_index("gy") * size_y + size_y // 2).astype(F32) - mid_y
    indicator, tension = cell_fields(arrived, near_index, jnp.stack([own_x, own_y, jnp.float32(0.0)]))
    padded_ind = extended(indicator, (("gx", 0), ("gy", 1), ("gz", 2)), 1)
    diffusion, forcing = coefficients(padded_ind, tension)
    current = velocity
    for repeat in range(NSWEEP):
        padded = extended(current, (("gx", 1), ("gy", 2), ("gz", 3)), 1)
        laplace = stencil(padded)
        current = current + time_step * (diffusion * laplace + forcing)
    samples = vertex_samples(current.reshape(3, size_x * size_y, size_z), return_cell)
    returned = lax.all_to_all(
        samples.reshape(-1, 9 * LANE), ("gx", "gy"), split_axis=0, concat_axis=0, tiled=True
    ).reshape(-1, LANE)
    return (current, indicator, bring_home(returned, send_index, tri_geom.shape[1]))


def solution(mesh):
    placed = (
        P(None, ("gx", "gy", "gz")),
        P(("gx", "gy", "gz"), None),
        P("gx", "gy", "gz"),
        P(None, ("gx", "gy", "gz")),
        P(None, "gx", "gy", "gz"),
    )
    return jax.shard_map(
        per_device,
        mesh=mesh,
        in_specs=placed,
        out_specs=(P(None, "gx", "gy", "gz"), P("gx", "gy", "gz"), P(None, ("gx", "gy", "gz"))),
        check_vma=False,
    )
```

time: 543 us -> 169 us (0.31)
  local copies, waits for them, and re-layouts: 337 us -> 12.8 us
  other arithmetic: 74.2 us -> 5.48 us
  Pallas kernels: 0 us -> 38.4 us
  waiting for transfers between devices: 58.4 us -> 28.2 us
  blocking collectives: 0 us -> 21.9 us
  starting transfers between devices: 69.1 us -> 60.3 us
    gather x6 -> x0, local copies, waits for them, and re-layouts: 239 us -> none  [the longest x1 111 us: per_device(): jnp.take(lookup, near_index.reshape(-1), axis=1)]
    slice x2 -> x0, local copies, waits for them, and re-layouts: 67.6 us -> none  [the longest x1 67.6 us: per_device(): tension = picked[6]]
    scatter-add x1 -> x0, other arithmetic: 46.5 us -> none  [per_device(): jnp.zeros((9, tri_dev), jnp.float32).at[:, target]]
    pallas_call x0 -> x4, Pallas kernels: none -> 38.4 us  [the longest x1 14 us: cell_fields(): pl.pallas_call(cell_kernel, name='cell_fields', out_shape=(out, out), in_...]
    all_to_all x0 -> x1, blocking collectives: none -> 21.9 us  [per_device(): lax.all_to_all(samples.reshape(-1, 9 * LANE), ('gx', 'gy'), split_axis=0,...]
    select_n x8 -> x0, other arithmetic: 21.8 us -> none  [the longest x2 19.2 us: per_device(): jnp.take(lookup, near_index.reshape(-1), axis=1)]
    ppermute x15, waiting for transfers between devices: 27.1 us -> 11.3 us  [extended(): lax.ppermute(tail, axis, [(i, (i + 1) % count) for i in range(count)])]
    all_to_all x2 -> x1, starting transfers between devices: 24.4 us -> 9.94 us  [per_device(): lax.all_to_all(outgoing.reshape(-1, 8, LANE), ('gx', 'gy'), split_axis=0,...]
  transfers between devices with their start and end apart: 32 -> 31, of which waited for: 27 -> 20; matrix products, arithmetic and copies ran while one was open for 1% -> 5% of each run, Pallas kernels for 0% -> 11%
where the time goes in v1:
time: 169 us; the launch traced here: 168 us
  starting transfers between devices  60.3 us (36%)
  Pallas kernels  38.4 us (23%)
  waiting for transfers between devices  28.2 us (17%)
  blocking collectives  21.9 us (13%)
  local copies, waits for them, and re-layouts  12.8 us (8%)
  other arithmetic  5.48 us (3%)
    ppermute x15, starting transfers between devices, extended(): lax.ppermute(head, axis, [((i + 1) % count, i) for i in range(count)])  35.7 us
    all_to_all x1, blocking collectives, per_device(): lax.all_to_all(samples.reshape(-1, 9 * LANE), ('gx', 'gy'), split_axis=0,...  21.9 us
    ppermute x15, starting transfers between devices, extended(): lax.ppermute(tail, axis, [(i, (i + 1) % count) for i in range(count)])  14.7 us
    pallas_call x1, Pallas kernels, cell_fields(): pl.pallas_call(cell_kernel, name='cell_fields', out_shape=(out, out), in_...  14 us
    pallas_call x1, Pallas kernels, vertex_samples(): pl.pallas_call(vertex_kernel, name='vertex_samples', out_shape=jax.ShapeD...  11.9 us
    ppermute x15, waiting for transfers between devices, extended(): lax.ppermute(tail, axis, [(i, (i + 1) % count) for i in range(count)])  11.3 us
    all_to_all x1, starting transfers between devices, per_device(): lax.all_to_all(outgoing.reshape(-1, 8, LANE), ('gx', 'gy'), split_axis=0,...  9.94 us
    all_to_all x1, waiting for transfers between devices, per_device(): lax.all_to_all(outgoing.reshape(-1, 8, LANE), ('gx', 'gy'), split_axis=0,...  8.92 us
  transfers between devices with their start and end apart: 31, of which 20 were waited for; matrix products, arithmetic and copies ran while one was open for 5% of the time, Pallas kernels for 11%

profile of v1, /device:TPU:1, one launch (start us, length us, event | category | flops | bytes accessed | tf_op | source)
XLA Modules:
  0.0 168.0 jit_solution(3083467672745792160)
XLA Ops:
  0.6 1.5 fusion.58
  2.1 2.5 %collective-permute-start.1 = (f32[3,1,32,128]{3,2,1,0:T(8,128)}, f32[3,1,32,128]{3,2,1,0:T(8,128)}, u32[]{:S(2)}, u32[]{:S(2)}) collective-permute-start(f32[3,1,32,128]{3,2,1,0:T(8,128)} %get-tuple-element.30), channel_id=1, source_target_pairs={{0,32},{32,64},{64,96},{96,128},{128,160},{160,192},{192,224},{224... | collective-permute-start | bytes 147464 | tf_op jit(solution)/shard_map/ppermute | solution.py:275
  4.6 3.9 %collective-permute-start = (f32[3,1,32,128]{3,2,1,0:T(8,128)}, f32[3,1,32,128]{3,2,1,0:T(8,128)}, u32[]{:S(2)}, u32[]{:S(2)}) collective-permute-start(f32[3,1,32,128]{3,2,1,0:T(8,128)} %get-tuple-element.29), channel_id=1, source_target_pairs={{32,0},{64,32},{96,64},{128,96},{160,128},{192,160},{224,192},{0,2... | collective-permute-start | bytes 147464 | tf_op jit(solution)/shard_map/ppermute | solution.py:277
  8.6 1.0 copy-done.1
  9.6 4.8 %send_tables.1 = f32[512,128]{1,0:T(8,128)} custom-call(f32[10,8192]{1,0:T(8,128)S(1)} %copy-done.1, s32[64,128]{1,0:T(8,128)S(1)} %copy-done.4, f32[3]{0:T(128)S(1)} %pad_maximum_fusion.88.origin_ref), custom_call_target="tpu_custom_call" | custom-call | flops 2199023255552 | bytes 1048576 | tf_op jit(solution)/shard_map/send_tables/pallas_call | solution.py:123
  14.5 9.9 %all-to-all-start = ((f32[64,8,128]{2,1,0:T(8,128)}), f32[64,8,128]{2,1,0:T(8,128)S(1)}, u32[]{:S(2)}, u32[]{:S(2)}) async-start(f32[64,8,128]{2,1,0:T(8,128)} %bitcast.1), calls=%async_computation | async-start | bytes 524288 | tf_op jit(solution)/shard_map/all_to_all | solution.py:311
  24.5 0.8 constant_dynamic-update-slice_fusion.2
  25.4 0.8 constant_dynamic-update-slice_fusion
  26.2 0.7 fusion.54
  26.9 0.5 collective-permute-start.2
  27.4 1.3 collective-permute-start.3
  28.7 8.9 %all-to-all-done = f32[64,8,128]{2,1,0:T(8,128)S(1)} async-done(((f32[64,8,128]{2,1,0:T(8,128)}), f32[64,8,128]{2,1,0:T(8,128)S(1)}, u32[]{:S(2)}, u32[]{:S(2)}) %all-to-all-start) | async-done | bytes 262176 | tf_op jit(solution)/shard_map/all_to_all | solution.py:311
  37.6 14.0 %cell_fields.1 = (f32[8,32,128]{2,1,0:T(8,128)}, f32[8,32,128]{2,1,0:T(8,128)S(1)}) custom-call(f32[512,128]{1,0:T(8,128)S(1)} %bitcast.17, s32[8,32,128]{2,1,0:T(8,128)S(1)} %copy-done.2, f32[3]{0:T(128)S(1)} %pad_maximum_fusion.89.origin_ref), custom_call_target="tpu_custom_call" | custom-call | flops 6597069766656 | bytes 1048576 | tf_op jit(solution)/shard_map/cell_fields/pallas_call | solution.py:168
  51.6 0.7 fusion.61
  52.4 0.8 collective-permute-start.7
  53.2 0.8 pad_maximum_fusion
  54.0 1.9 %collective-permute-start.6 = (f32[1,32,128]{2,1,0:T(8,128)S(1)}, f32[1,32,128]{2,1,0:T(8,128)S(1)}, u32[]{:S(2)}, u32[]{:S(2)}) collective-permute-start(f32[1,32,128]{2,1,0:T(8,128)S(1)} %get-tuple-element.41), channel_id=1, source_target_pairs={{32,0},{64,32},{96,64},{128,96},{160,128},{192,160},{224,192},{0,2... | collective-permute-start | bytes 49160 | tf_op jit(solution)/shard_map/ppermute | solution.py:277
  56.2 0.8 collective-permute-done.6
  57.0 1.7 %collective-permute-start.9 = (f32[10,1,128]{2,1,0:T(1,128)S(1)}, f32[10,1,128]{2,1,0:T(1,128)S(1)}, u32[]{:S(2)}, u32[]{:S(2)}) collective-permute-start(f32[10,1,128]{2,1,0:T(1,128)S(1)} %get-tuple-element.35), channel_id=1, source_target_pairs={{0,4},{4,8},{8,12},{12,16},{16,20},{20,24},{24,28},{28,0},{1,5},{5... | collective-permute-start | bytes 15368 | tf_op jit(solution)/shard_map/ppermute | solution.py:275
  59.3 1.4 collective-permute-start.5
  60.9 1.6 collective-permute-start.4
  62.5 0.8 fusion.59
  63.3 0.9 collective-permute-start.11
  64.2 1.8 %collective-permute-start.10 = (f32[10,34,1]{2,1,0:T(8,128)S(1)}, f32[10,34,1]{2,1,0:T(8,128)}, u32[]{:S(2)}, u32[]{:S(2)}) collective-permute-start(f32[10,34,1]{2,1,0:T(8,128)S(1)} %get-tuple-element.31), channel_id=1, source_target_pairs={{1,0},{2,1},{3,2},{0,3},{5,4},{6,5},{7,6},{4,7},{9,8},{10,9},{11,1... | collective-permute-start | bytes 4088 | tf_op jit(solution)/shard_map/ppermute | solution.py:277
  66.0 0.3 copy.11
  66.7 2.7 %collective-permute-done.11 = f32[10,34,1]{2,1,0:T(8,128)S(1)} collective-permute-done((f32[10,34,1]{2,1,0:T(8,128)}, f32[10,34,1]{2,1,0:T(8,128)S(1)}, u32[]{:S(2)}, u32[]{:S(2)}) %collective-permute-start.11) | collective-permute-done | bytes 1392 | tf_op jit(solution)/shard_map/ppermute | solution.py:275
  69.4 1.1 fusion.46
  70.5 1.4 fusion.35
  72.0 3.3 %collective-permute-start.12 = (f32[3,1,32,128]{3,2,1,0:T(8,128)S(1)}, f32[3,1,32,128]{3,2,1,0:T(8,128)S(1)}, u32[]{:S(2)}, u32[]{:S(2)}) collective-permute-start(f32[3,1,32,128]{3,2,1,0:T(8,128)S(1)} %get-tuple-element.28), channel_id=1, source_target_pairs={{32,0},{64,32},{96,64},{128,96},{160,128},{192,160},{224,192},{0,2... | collective-permute-start | bytes 147464 | tf_op jit(solution)/shard_map/ppermute | solution.py:277
  75.2 1.2 collective-permute-done.12
  76.4 3.0 %collective-permute-done.13 = f32[3,1,32,128]{3,2,1,0:T(8,128)S(1)} collective-permute-done((f32[3,1,32,128]{3,2,1,0:T(8,128)S(1)}, f32[3,1,32,128]{3,2,1,0:T(8,128)S(1)}, u32[]{:S(2)}, u32[]{:S(2)}) %collective-permute-start.13) | collective-permute-done | bytes 49184 | tf_op jit(solution)/shard_map/ppermute | solution.py:275
  79.4 5.6 %collective-permute-start.14 = (f32[3,10,1,128]{3,2,1,0:T(1,128)S(1)}, f32[3,10,1,128]{3,2,1,0:T(1,128)S(1)}, u32[]{:S(2)}, u32[]{:S(2)}) collective-permute-start(f32[3,10,1,128]{3,2,1,0:T(1,128)S(1)} %get-tuple-element.20), channel_id=1, source_target_pairs={{4,0},{8,4},{12,8},{16,12},{20,16},{24,20},{28,24},{0,28},{5,1},{9... | collective-permute-start | bytes 46088 | tf_op jit(solution)/shard_map/ppermute | solution.py:277
  85.0 1.0 collective-permute-done.14
  86.7 0.6 collective-permute-start.17
  87.7 2.3 %collective-permute-start.16 = (f32[3,10,34,1]{2,3,1,0:T(1,128)S(1)}, f32[3,10,34,1]{2,3,1,0:T(1,128)S(1)}, u32[]{:S(2)}, u32[]{:S(2)}) collective-permute-start(f32[3,10,34,1]{2,3,1,0:T(1,128)S(1)} %copy.12), channel_id=1, source_target_pairs={{1,0},{2,1},{3,2},{0,3},{5,4},{6,5},{7,6},{4,7},{9,8},{10,9},{11,1... | collective-permute-start | bytes 12248 | tf_op jit(solution)/shard_map/ppermute | solution.py:277
  90.0 0.7 collective-permute-done.17
  90.8 0.3 copy.15
  91.4 0.5 fusion.25
  92.1 1.5 collective-permute-start.19
  93.5 1.5 collective-permute-done.18
  95.0 1.3 collective-permute-done.19
  96.3 5.7 %collective-permute-start.20 = (f32[3,10,1,128]{3,2,1,0:T(1,128)S(1)}, f32[3,10,1,128]{3,2,1,0:T(1,128)S(1)}, u32[]{:S(2)}, u32[]{:S(2)}) collective-permute-start(f32[3,10,1,128]{3,2,1,0:T(1,128)S(1)} %get-tuple-element.18), channel_id=1, source_target_pairs={{4,0},{8,4},{12,8},{16,12},{20,16},{24,20},{28,24},{0,28},{5,1},{9... | collective-permute-start | bytes 46088 | tf_op jit(solution)/shard_map/ppermute | solution.py:277
  102.0 0.8 collective-permute-done.20
  102.8 0.3 collective-permute-done.21
  103.8 1.1 collective-permute-start.23
  105.2 1.8 %collective-permute-start.22 = (f32[3,10,34,1]{2,3,1,0:T(1,128)S(1)}, f32[3,10,34,1]{2,3,1,0:T(1,128)S(1)}, u32[]{:S(2)}, u32[]{:S(2)}) collective-permute-start(f32[3,10,34,1]{2,3,1,0:T(1,128)S(1)} %copy.16), channel_id=1, source_target_pairs={{1,0},{2,1},{3,2},{0,3},{5,4},{6,5},{7,6},{4,7},{9,8},{10,9},{11,1... | collective-permute-start | bytes 12248 | tf_op jit(solution)/shard_map/ppermute | solution.py:277
  106.9 0.7 collective-permute-done.23
  107.7 0.3 copy.19
  108.4 0.5 fusion.15
  109.0 1.5 collective-permute-start.25
  110.5 1.6 collective-permute-done.24
  112.0 1.2 collective-permute-done.25
  113.3 5.5 %collective-permute-start.26 = (f32[3,10,1,128]{3,2,1,0:T(1,128)S(1)}, f32[3,10,1,128]{3,2,1,0:T(1,128)S(1)}, u32[]{:S(2)}, u32[]{:S(2)}) collective-permute-start(f32[3,10,1,128]{3,2,1,0:T(1,128)S(1)} %get-tuple-element.16), channel_id=1, source_target_pairs={{4,0},{8,4},{12,8},{16,12},{20,16},{24,20},{28,24},{0,28},{5,1},{9... | collective-permute-start | bytes 46088 | tf_op jit(solution)/shard_map/ppermute | solution.py:277
  118.8 0.8 collective-permute-done.26
  119.7 0.3 collective-permute-done.27
  120.6 1.5 collective-permute-start.29
  122.4 1.7 %collective-permute-start.28 = (f32[3,10,34,1]{2,3,1,0:T(1,128)S(1)}, f32[3,10,34,1]{2,3,1,0:T(1,128)S(1)}, u32[]{:S(2)}, u32[]{:S(2)}) collective-permute-start(f32[3,10,34,1]{2,3,1,0:T(1,128)S(1)} %copy.20), channel_id=1, source_target_pairs={{1,0},{2,1},{3,2},{0,3},{5,4},{6,5},{7,6},{4,7},{9,8},{10,9},{11,1... | collective-permute-start | bytes 12248 | tf_op jit(solution)/shard_map/ppermute | solution.py:277
  124.1 0.5 collective-permute-done.29
  124.7 0.3 copy.23
  125.6 0.5 fusion.5
  126.2 0.3 copy-done.3
  126.5 11.9 %vertex_samples.1 = f32[576,128]{1,0:T(8,128)S(1)} custom-call(f32[3,256,128]{2,1,0:T(8,128)S(1)} %bitcast.14, s32[3,8192]{1,0:T(4,128)S(1)} %copy-done.3), custom_call_target="tpu_custom_call" | custom-call | flops 10995116277760 | bytes 1048576 | tf_op jit(solution)/shard_map/vertex_samples/pallas_call | solution.py:203
  138.4 21.9 %all_to_all.14 = f32[64,1,1152]{2,1,0:T(1,128)S(1)} all-to-all(f32[64,1,1152]{2,1,0:T(1,128)S(1)} %bitcast.16), channel_id=1, replica_groups=mesh['gx'=8,'gy'=8,'gz'=4] {'gx','gy'}, dimensions={0} | all-to-all | bytes 589824 | tf_op jit(solution)/shard_map/all_to_all | solution.py:325
  160.3 7.7 %bring_home.1 = f32[9,8192]{1,0:T(8,128)} custom-call(f32[576,128]{1,0:T(8,128)S(1)} %bitcast.15, s32[64,128]{1,0:T(8,128)S(1)} %copy-done.5), custom_call_target="tpu_custom_call" | custom-call | flops 2199023255552 | bytes 1048576 | tf_op jit(solution)/shard_map/bring_home/pallas_call | solution.py:252
  (74 shorter events, 6.2 us)
Async XLA Ops:
  0.6 8.0 %copy-start.4 = (s32[64,128]{1,0:T(8,128)S(1)}, s32[64,128]{1,0:T(8,128)}, u32[]{:S(2)}) copy-start(s32[64,128]{1,0:T(8,128)} %send_ref.3) | copy-start | bytes 98308
  2.1 22.4 %collective-permute-start.1 = (f32[3,1,32,128]{3,2,1,0:T(8,128)}, f32[3,1,32,128]{3,2,1,0:T(8,128)}, u32[]{:S(2)}, u32[]{:S(2)}) collective-permute-start(f32[3,1,32,128]{3,2,1,0:T(8,128)} %get-tuple-element.30), channel_id=1, source_target_pairs={{0,32},{32,64},{64,96},{96,128},{128,160},{160,192},{192,224},{224... | collective-permute-start | bytes 147464 | tf_op jit(solution)/shard_map/ppermute | solution.py:275
  4.6 20.8 %collective-permute-start = (f32[3,1,32,128]{3,2,1,0:T(8,128)}, f32[3,1,32,128]{3,2,1,0:T(8,128)}, u32[]{:S(2)}, u32[]{:S(2)}) collective-permute-start(f32[3,1,32,128]{3,2,1,0:T(8,128)} %get-tuple-element.29), channel_id=1, source_target_pairs={{32,0},{64,32},{96,64},{128,96},{160,128},{192,160},{224,192},{0,2... | collective-permute-start | bytes 147464 | tf_op jit(solution)/shard_map/ppermute | solution.py:277
  8.6 1.0 copy-start.1
  14.5 10.9 %copy-start.8 = (f32[3,8,32,128]{3,2,1,0:T(8,128)S(1)}, f32[3,8,32,128]{3,2,1,0:T(8,128)}, u32[]{:S(2)}) copy-start(f32[3,8,32,128]{3,2,1,0:T(8,128)} %param.9) | copy-start | bytes 1179652
  14.5 23.1 %all-to-all-start = ((f32[64,8,128]{2,1,0:T(8,128)}), f32[64,8,128]{2,1,0:T(8,128)S(1)}, u32[]{:S(2)}, u32[]{:S(2)}) async-start(f32[64,8,128]{2,1,0:T(8,128)} %bitcast.1), calls=%async_computation | async-start | bytes 524288 | tf_op jit(solution)/shard_map/all_to_all | solution.py:311
  25.3 12.2 %copy-start.2 = (s32[8,32,128]{2,1,0:T(8,128)S(1)}, s32[8,32,128]{2,1,0:T(8,128)}, u32[]{:S(2)}) copy-start(s32[8,32,128]{2,1,0:T(8,128)} %near_ref.1) | copy-start | bytes 393220
  26.2 1.2 copy-start.6
  26.9 26.3 %collective-permute-start.2 = (f32[3,10,1,128]{3,2,1,0:T(1,128)}, f32[3,10,1,128]{3,2,1,0:T(1,128)}, u32[]{:S(2)}, u32[]{:S(2)}) collective-permute-start(f32[3,10,1,128]{3,2,1,0:T(1,128)} %get-tuple-element.22), channel_id=1, source_target_pairs={{4,0},{8,4},{12,8},{16,12},{20,16},{24,20},{28,24},{0,28},{5,1},{9... | collective-permute-start | bytes 46088 | tf_op jit(solution)/shard_map/ppermute | solution.py:277
  27.4 25.8 %collective-permute-start.3 = (f32[3,10,1,128]{3,2,1,0:T(1,128)}, f32[3,10,1,128]{3,2,1,0:T(1,128)}, u32[]{:S(2)}, u32[]{:S(2)}) collective-permute-start(f32[3,10,1,128]{3,2,1,0:T(1,128)} %get-tuple-element.21), channel_id=1, source_target_pairs={{0,4},{4,8},{8,12},{12,16},{16,20},{20,24},{24,28},{28,0},{1,5},{5... | collective-permute-start | bytes 46088 | tf_op jit(solution)/shard_map/ppermute | solution.py:275
  37.6 15.6 %copy-start.7 = (f32[3,10,32,128]{3,2,1,0:T(8,128)S(1)}, f32[3,10,32,128]{3,2,1,0:T(8,128)}, u32[]{:S(2)}) copy-start(f32[3,10,32,128]{3,2,1,0:T(8,128)} %copy-done.6) | copy-start | bytes 1474564
  52.4 4.6 %copy-start.10 = (f32[8,32,128]{2,1,0:T(8,128)S(1)}, f32[8,32,128]{2,1,0:T(8,128)}, u32[]{:S(2)}) copy-start(f32[8,32,128]{2,1,0:T(8,128)} %get-tuple-element.3) | copy-start | bytes 393220
  52.4 3.8 %collective-permute-start.7 = (f32[1,32,128]{2,1,0:T(8,128)S(1)}, f32[1,32,128]{2,1,0:T(8,128)S(1)}, u32[]{:S(2)}, u32[]{:S(2)}) collective-permute-start(f32[1,32,128]{2,1,0:T(8,128)S(1)} %get-tuple-element.42), channel_id=1, source_target_pairs={{0,32},{32,64},{64,96},{96,128},{128,160},{160,192},{192,224},{224... | collective-permute-start | bytes 49160 | tf_op jit(solution)/shard_map/ppermute | solution.py:275
  54.0 3.0 %collective-permute-start.6 = (f32[1,32,128]{2,1,0:T(8,128)S(1)}, f32[1,32,128]{2,1,0:T(8,128)S(1)}, u32[]{:S(2)}, u32[]{:S(2)}) collective-permute-start(f32[1,32,128]{2,1,0:T(8,128)S(1)} %get-tuple-element.41), channel_id=1, source_target_pairs={{32,0},{64,32},{96,64},{128,96},{160,128},{192,160},{224,192},{0,2... | collective-permute-start | bytes 49160 | tf_op jit(solution)/shard_map/ppermute | solution.py:277
  57.0 5.5 %collective-permute-start.9 = (f32[10,1,128]{2,1,0:T(1,128)S(1)}, f32[10,1,128]{2,1,0:T(1,128)S(1)}, u32[]{:S(2)}, u32[]{:S(2)}) collective-permute-start(f32[10,1,128]{2,1,0:T(1,128)S(1)} %get-tuple-element.35), channel_id=1, source_target_pairs={{0,4},{4,8},{8,12},{12,16},{16,20},{20,24},{24,28},{28,0},{1,5},{5... | collective-permute-start | bytes 15368 | tf_op jit(solution)/shard_map/ppermute | solution.py:275
  58.8 3.7 %collective-permute-start.8 = (f32[10,1,128]{2,1,0:T(1,128)S(1)}, f32[10,1,128]{2,1,0:T(1,128)S(1)}, u32[]{:S(2)}, u32[]{:S(2)}) collective-permute-start(f32[10,1,128]{2,1,0:T(1,128)S(1)} %get-tuple-element.36), channel_id=1, source_target_pairs={{4,0},{8,4},{12,8},{16,12},{20,16},{24,20},{28,24},{0,28},{5,1},{9... | collective-permute-start | bytes 15368 | tf_op jit(solution)/shard_map/ppermute | solution.py:277
  59.3 6.7 %collective-permute-start.5 = (f32[3,10,34,1]{2,3,1,0:T(1,128)S(1)}, f32[3,10,34,1]{2,3,1,0:T(1,128)S(1)}, u32[]{:S(2)}, u32[]{:S(2)}) collective-permute-start(f32[3,10,34,1]{2,3,1,0:T(1,128)S(1)} %copy.10), channel_id=1, source_target_pairs={{0,1},{1,2},{2,3},{3,0},{4,5},{5,6},{6,7},{7,4},{8,9},{9,10},{10,1... | collective-permute-start | bytes 12248 | tf_op jit(solution)/shard_map/ppermute | solution.py:275
  60.9 5.4 %collective-permute-start.4 = (f32[3,10,34,1]{2,3,1,0:T(1,128)S(1)}, f32[3,10,34,1]{2,3,1,0:T(1,128)S(1)}, u32[]{:S(2)}, u32[]{:S(2)}) collective-permute-start(f32[3,10,34,1]{2,3,1,0:T(1,128)S(1)} %copy.8), channel_id=1, source_target_pairs={{1,0},{2,1},{3,2},{0,3},{5,4},{6,5},{7,6},{4,7},{9,8},{10,9},{11,1... | collective-permute-start | bytes 12248 | tf_op jit(solution)/shard_map/ppermute | solution.py:277
  63.3 6.0 %collective-permute-start.11 = (f32[10,34,1]{2,1,0:T(8,128)}, f32[10,34,1]{2,1,0:T(8,128)S(1)}, u32[]{:S(2)}, u32[]{:S(2)}) collective-permute-start(f32[10,34,1]{2,1,0:T(8,128)} %get-tuple-element.32), channel_id=1, source_target_pairs={{0,1},{1,2},{2,3},{3,0},{4,5},{5,6},{6,7},{7,4},{8,9},{9,10},{10,1... | collective-permute-start | bytes 4088 | tf_op jit(solution)/shard_map/ppermute | solution.py:275
  64.2 5.1 %collective-permute-start.10 = (f32[10,34,1]{2,1,0:T(8,128)S(1)}, f32[10,34,1]{2,1,0:T(8,128)}, u32[]{:S(2)}, u32[]{:S(2)}) collective-permute-start(f32[10,34,1]{2,1,0:T(8,128)S(1)} %get-tuple-element.31), channel_id=1, source_target_pairs={{1,0},{2,1},{3,2},{0,3},{5,4},{6,5},{7,6},{4,7},{9,8},{10,9},{11,1... | collective-permute-start | bytes 4088 | tf_op jit(solution)/shard_map/ppermute | solution.py:277
  66.7 3.8 %copy-start.9 = (f32[3,8,32,128]{3,2,1,0:T(8,128)S(1)}, f32[3,8,32,128]{3,2,1,0:T(8,128)}, u32[]{:S(2)}) copy-start(f32[3,8,32,128]{3,2,1,0:T(8,128)} %param.9) | copy-start | bytes 1179652
  72.0 4.4 %collective-permute-start.12 = (f32[3,1,32,128]{3,2,1,0:T(8,128)S(1)}, f32[3,1,32,128]{3,2,1,0:T(8,128)S(1)}, u32[]{:S(2)}, u32[]{:S(2)}) collective-permute-start(f32[3,1,32,128]{3,2,1,0:T(8,128)S(1)} %get-tuple-element.28), channel_id=1, source_target_pairs={{32,0},{64,32},{96,64},{128,96},{160,128},{192,160},{224,192},{0,2... | collective-permute-start | bytes 147464 | tf_op jit(solution)/shard_map/ppermute | solution.py:277
  75.2 4.2 %collective-permute-start.13 = (f32[3,1,32,128]{3,2,1,0:T(8,128)S(1)}, f32[3,1,32,128]{3,2,1,0:T(8,128)S(1)}, u32[]{:S(2)}, u32[]{:S(2)}) collective-permute-start(f32[3,1,32,128]{3,2,1,0:T(8,128)S(1)} %get-tuple-element.27), channel_id=1, source_target_pairs={{0,32},{32,64},{64,96},{96,128},{128,160},{160,192},{192,224},{224... | collective-permute-start | bytes 147464 | tf_op jit(solution)/shard_map/ppermute | solution.py:275
  79.4 6.5 %collective-permute-start.14 = (f32[3,10,1,128]{3,2,1,0:T(1,128)S(1)}, f32[3,10,1,128]{3,2,1,0:T(1,128)S(1)}, u32[]{:S(2)}, u32[]{:S(2)}) collective-permute-start(f32[3,10,1,128]{3,2,1,0:T(1,128)S(1)} %get-tuple-element.20), channel_id=1, source_target_pairs={{4,0},{8,4},{12,8},{16,12},{20,16},{24,20},{28,24},{0,28},{5,1},{9... | collective-permute-start | bytes 46088 | tf_op jit(solution)/shard_map/ppermute | solution.py:277
  84.9 1.2 collective-permute-start.15
  86.7 4.0 %collective-permute-start.17 = (f32[3,10,34,1]{2,3,1,0:T(1,128)S(1)}, f32[3,10,34,1]{2,3,1,0:T(1,128)S(1)}, u32[]{:S(2)}, u32[]{:S(2)}) collective-permute-start(f32[3,10,34,1]{2,3,1,0:T(1,128)S(1)} %copy.14), channel_id=1, source_target_pairs={{0,1},{1,2},{2,3},{3,0},{4,5},{5,6},{6,7},{7,4},{8,9},{9,10},{10,1... | collective-permute-start | bytes 12248 | tf_op jit(solution)/shard_map/ppermute | solution.py:275
  87.7 3.4 %collective-permute-start.16 = (f32[3,10,34,1]{2,3,1,0:T(1,128)S(1)}, f32[3,10,34,1]{2,3,1,0:T(1,128)S(1)}, u32[]{:S(2)}, u32[]{:S(2)}) collective-permute-start(f32[3,10,34,1]{2,3,1,0:T(1,128)S(1)} %copy.12), channel_id=1, source_target_pairs={{1,0},{2,1},{3,2},{0,3},{5,4},{6,5},{7,6},{4,7},{9,8},{10,9},{11,1... | collective-permute-start | bytes 12248 | tf_op jit(solution)/shard_map/ppermute | solution.py:277
  92.0 3.0 %collective-permute-start.18 = (f32[3,1,32,128]{3,2,1,0:T(8,128)S(1)}, f32[3,1,32,128]{3,2,1,0:T(8,128)S(1)}, u32[]{:S(2)}, u32[]{:S(2)}) collective-permute-start(f32[3,1,32,128]{3,2,1,0:T(8,128)S(1)} %get-tuple-element.26), channel_id=1, source_target_pairs={{32,0},{64,32},{96,64},{128,96},{160,128},{192,160},{224,192},{0,2... | collective-permute-start | bytes 147464 | tf_op jit(solution)/shard_map/ppermute | solution.py:277
  92.1 4.2 %collective-permute-start.19 = (f32[3,1,32,128]{3,2,1,0:T(8,128)S(1)}, f32[3,1,32,128]{3,2,1,0:T(8,128)S(1)}, u32[]{:S(2)}, u32[]{:S(2)}) collective-permute-start(f32[3,1,32,128]{3,2,1,0:T(8,128)S(1)} %get-tuple-element.25), channel_id=1, source_target_pairs={{0,32},{32,64},{64,96},{96,128},{128,160},{160,192},{192,224},{224... | collective-permute-start | bytes 147464 | tf_op jit(solution)/shard_map/ppermute | solution.py:275
  96.3 6.5 %collective-permute-start.20 = (f32[3,10,1,128]{3,2,1,0:T(1,128)S(1)}, f32[3,10,1,128]{3,2,1,0:T(1,128)S(1)}, u32[]{:S(2)}, u32[]{:S(2)}) collective-permute-start(f32[3,10,1,128]{3,2,1,0:T(1,128)S(1)} %get-tuple-element.18), channel_id=1, source_target_pairs={{4,0},{8,4},{12,8},{16,12},{20,16},{24,20},{28,24},{0,28},{5,1},{9... | collective-permute-start | bytes 46088 | tf_op jit(solution)/shard_map/ppermute | solution.py:277
  102.0 1.2 collective-permute-start.21
  103.8 3.9 %collective-permute-start.23 = (f32[3,10,34,1]{2,3,1,0:T(1,128)S(1)}, f32[3,10,34,1]{2,3,1,0:T(1,128)S(1)}, u32[]{:S(2)}, u32[]{:S(2)}) collective-permute-start(f32[3,10,34,1]{2,3,1,0:T(1,128)S(1)} %copy.18), channel_id=1, source_target_pairs={{0,1},{1,2},{2,3},{3,0},{4,5},{5,6},{6,7},{7,4},{8,9},{9,10},{10,1... | collective-permute-start | bytes 12248 | tf_op jit(solution)/shard_map/ppermute | solution.py:275
  105.2 2.9 %collective-permute-start.22 = (f32[3,10,34,1]{2,3,1,0:T(1,128)S(1)}, f32[3,10,34,1]{2,3,1,0:T(1,128)S(1)}, u32[]{:S(2)}, u32[]{:S(2)}) collective-permute-start(f32[3,10,34,1]{2,3,1,0:T(1,128)S(1)} %copy.16), channel_id=1, source_target_pairs={{1,0},{2,1},{3,2},{0,3},{5,4},{6,5},{7,6},{4,7},{9,8},{10,9},{11,1... | collective-permute-start | bytes 12248 | tf_op jit(solution)/shard_map/ppermute | solution.py:277
  108.9 3.1 %collective-permute-start.24 = (f32[3,1,32,128]{3,2,1,0:T(8,128)S(1)}, f32[3,1,32,128]{3,2,1,0:T(8,128)S(1)}, u32[]{:S(2)}, u32[]{:S(2)}) collective-permute-start(f32[3,1,32,128]{3,2,1,0:T(8,128)S(1)} %get-tuple-element.24), channel_id=1, source_target_pairs={{32,0},{64,32},{96,64},{128,96},{160,128},{192,160},{224,192},{0,2... | collective-permute-start | bytes 147464 | tf_op jit(solution)/shard_map/ppermute | solution.py:277
  109.0 4.2 %collective-permute-start.25 = (f32[3,1,32,128]{3,2,1,0:T(8,128)S(1)}, f32[3,1,32,128]{3,2,1,0:T(8,128)S(1)}, u32[]{:S(2)}, u32[]{:S(2)}) collective-permute-start(f32[3,1,32,128]{3,2,1,0:T(8,128)S(1)} %get-tuple-element.23), channel_id=1, source_target_pairs={{0,32},{32,64},{64,96},{96,128},{128,160},{160,192},{192,224},{224... | collective-permute-start | bytes 147464 | tf_op jit(solution)/shard_map/ppermute | solution.py:275
  113.3 6.4 %collective-permute-start.26 = (f32[3,10,1,128]{3,2,1,0:T(1,128)S(1)}, f32[3,10,1,128]{3,2,1,0:T(1,128)S(1)}, u32[]{:S(2)}, u32[]{:S(2)}) collective-permute-start(f32[3,10,1,128]{3,2,1,0:T(1,128)S(1)} %get-tuple-element.16), channel_id=1, source_target_pairs={{4,0},{8,4},{12,8},{16,12},{20,16},{24,20},{28,24},{0,28},{5,1},{9... | collective-permute-start | bytes 46088 | tf_op jit(solution)/shard_map/ppermute | solution.py:277
  118.8 1.2 collective-permute-start.27
  120.6 4.1 %collective-permute-start.29 = (f32[3,10,34,1]{2,3,1,0:T(1,128)S(1)}, f32[3,10,34,1]{2,3,1,0:T(1,128)S(1)}, u32[]{:S(2)}, u32[]{:S(2)}) collective-permute-start(f32[3,10,34,1]{2,3,1,0:T(1,128)S(1)} %copy.22), channel_id=1, source_target_pairs={{0,1},{1,2},{2,3},{3,0},{4,5},{5,6},{6,7},{7,4},{8,9},{9,10},{10,1... | collective-permute-start | bytes 12248 | tf_op jit(solution)/shard_map/ppermute | solution.py:275
  122.4 2.9 %collective-permute-start.28 = (f32[3,10,34,1]{2,3,1,0:T(1,128)S(1)}, f32[3,10,34,1]{2,3,1,0:T(1,128)S(1)}, u32[]{:S(2)}, u32[]{:S(2)}) collective-permute-start(f32[3,10,34,1]{2,3,1,0:T(1,128)S(1)} %copy.20), channel_id=1, source_target_pairs={{1,0},{2,1},{3,2},{0,3},{5,4},{6,5},{7,6},{4,7},{9,8},{10,9},{11,1... | collective-permute-start | bytes 12248 | tf_op jit(solution)/shard_map/ppermute | solution.py:277
  125.6 0.9 copy-start.3
  126.2 12.2 %copy-start = (f32[3,8,32,128]{3,2,1,0:T(8,128)}, f32[3,8,32,128]{3,2,1,0:T(8,128)S(1)}, u32[]{:S(2)}) copy-start(f32[3,8,32,128]{3,2,1,0:T(8,128)S(1)} %fusion.5) | copy-start | bytes 1179652
  138.4 21.9 %copy-start.5 = (s32[64,128]{1,0:T(8,128)S(1)}, s32[64,128]{1,0:T(8,128)}, u32[]{:S(2)}) copy-start(s32[64,128]{1,0:T(8,128)} %send_ref.3) | copy-start | bytes 98308

commit v2 on v1

--- a/solution.py
+++ b/solution.py
@@ -6,8 +6,10 @@
 from jax.sharding import PartitionSpec as P
 
 NSWEEP = 4
+WIDE = NSWEEP
 
 time_step = 0.04
+smear_width = 4.0
 rho_liquid = 1.0
 rho_gas = 0.05
 mu_liquid = 2.0
@@ -132,7 +134,7 @@
     )(geom, send, origin)
 
 
-def cell_kernel(tab_ref, near_ref, origin_ref, ind_ref, ten_ref, table_ref):
+def cell_kernel(tab_ref, near_ref, origin_ref, ind_ref, low_ref, high_ref, table_ref):
     sources = tab_ref.shape[0] // 8
     half = sources // 2
     size_x, size_y, _ = near_ref.shape
@@ -158,19 +160,30 @@
         at_x = x.astype(F32) + (0.5 - mid_x)
         at_y = sub + (y.astype(F32) + (0.5 - mid_y))
         distance = found[0] * at_x + found[1] * at_y + found[2] * at_z - found[3]
-        ind_ref[x, pl.ds(y, 8), :] = 0.5 * (1.0 + jnp.tanh(distance / 4.0))
-        ten_ref[x, pl.ds(y, 8), :] = found[4]
+        indicator = 0.5 * (1.0 + jnp.tanh(distance / smear_width))
+        ind_ref[x, pl.ds(y, 8), :] = indicator
+
+        @pl.when(x < WIDE)
+        def _():
+            low_ref[0, x, pl.ds(y, 8), :] = indicator
+            low_ref[1, x, pl.ds(y, 8), :] = found[4]
+
+        @pl.when(x >= WIDE)
+        def _():
+            high_ref[0, x - WIDE, pl.ds(y, 8), :] = indicator
+            high_ref[1, x - WIDE, pl.ds(y, 8), :] = found[4]
 
 
 def cell_fields(tab, near, origin):
     sources = tab.shape[0] // 8
     out = jax.ShapeDtypeStruct(near.shape, F32)
+    side = jax.ShapeDtypeStruct((2, WIDE) + near.shape[1:], F32)
     return pl.pallas_call(
         cell_kernel,
         name="cell_fields",
-        out_shape=(out, out),
+        out_shape=(out, side, side),
         in_specs=[VMEM, VMEM, pl.BlockSpec(memory_space=pltpu.SMEM)],
-        out_specs=(VMEM, VMEM),
+        out_specs=(VMEM, VMEM, VMEM),
         scratch_shapes=[pltpu.VMEM((11 * sources // 2, 2 * LANE), BF16)],
         compiler_params=pltpu.CompilerParams(vmem_limit_bytes=40 << 20),
         cost_estimate=pl.CostEstimate(flops=6 << 40, bytes_accessed=1 << 20, transcendentals=0),
@@ -265,62 +278,199 @@
     )(back, send)
 
 
-def extended(cells, sides, width):
-    for axis, dim in sides:
-        count = lax.axis_size(axis)
-        head = lax.slice_in_dim(cells, 0, width, axis=dim)
-        tail = lax.slice_in_dim(cells, cells.shape[dim] - width, cells.shape[dim], axis=dim)
-        cells = jnp.concatenate(
-            [
-                lax.ppermute(tail, axis, [(i, (i + 1) % count) for i in range(count)]),
-                cells,
-                lax.ppermute(head, axis, [((i + 1) % count, i) for i in range(count)]),
-            ],
-            axis=dim,
-        )
-    return cells
-
-
-def coefficients(padded_ind, tension):
-    gradient = jnp.stack(
-        [
-            (padded_ind[2:, 1:-1, 1:-1] - padded_ind[:-2, 1:-1, 1:-1]) * 0.5,
-            (padded_ind[1:-1, 2:, 1:-1] - padded_ind[1:-1, :-2, 1:-1]) * 0.5,
-            (padded_ind[1:-1, 1:-1, 2:] - padded_ind[1:-1, 1:-1, :-2]) * 0.5,
-        ]
-    )
-    core_ind = padded_ind[1:-1, 1:-1, 1:-1]
-    density = rho_liquid + (rho_gas - rho_liquid) * core_ind
-    viscosity = mu_liquid + (mu_gas - mu_liquid) * core_ind
-    return (viscosity / density, tension * gradient / density)
-
-
-def stencil(padded):
-    laplace = padded[:, 2:, 1:-1, 1:-1] + padded[:, :-2, 1:-1, 1:-1]
-    laplace = laplace + padded[:, 1:-1, 2:, 1:-1] + padded[:, 1:-1, :-2, 1:-1]
-    laplace = laplace + padded[:, 1:-1, 1:-1, 2:] + padded[:, 1:-1, 1:-1, :-2]
-    return laplace - 6.0 * padded[:, 1:-1, 1:-1, 1:-1]
+def pack_y_kernel(low_ref, high_ref, below_ref, above_ref, down_ref, up_ref):
+    size_y = low_ref.shape[2]
+    at = 0
+    for c in range(low_ref.shape[0]):
+        for ref in (below_ref, low_ref, high_ref, above_ref):
+            for x in range(WIDE):
+                down_ref[at:at + WIDE, :] = ref[c, x, 0:WIDE, :]
+                up_ref[at:at + WIDE, :] = ref[c, x, size_y - WIDE:size_y, :]
+                at += WIDE
+
+
+def pack_y(low, high, below, above):
+    out = jax.ShapeDtypeStruct((low.shape[0] * 4 * WIDE * WIDE, LANE), F32)
+    return pl.pallas_call(
+        pack_y_kernel,
+        name="pack_y",
+        out_shape=(out, out),
+        in_specs=[VMEM] * 4,
+        out_specs=(VMEM, VMEM),
+        compiler_params=pltpu.CompilerParams(vmem_limit_bytes=16 << 20),
+        cost_estimate=pl.CostEstimate(flops=1 << 20, bytes_accessed=1 << 20, transcendentals=0),
+    )(low, high, below, above)
+
+
+def pack_z_kernel(*refs):
+    wide_ref, down_ref, up_ref = refs[-3:]
+    lane = lax.broadcasted_iota(I32, (1, LANE), 1)
+    group = lax.shift_right_logical(lane, 2)
+    size_y = refs[0].shape[2]
+    field = 0
+    down = up = None
+    for low_ref, high_ref, below_ref, above_ref, under_ref, over_ref in (refs[0:6], refs[6:12]):
+        at = 0
+        for c in range(low_ref.shape[0]):
+            side = field % 2
+            if side == 0:
+                down = jnp.zeros((size_y + 2 * WIDE, LANE), F32)
+                up = jnp.zeros((size_y + 2 * WIDE, LANE), F32)
+            x = 0
+            for ref in (below_ref, low_ref, high_ref, above_ref):
+                for k in range(WIDE):
+                    plane = jnp.concatenate(
+                        [ref[c, k], over_ref[at:at + WIDE, :], under_ref[at:at + WIDE, :]], axis=0
+                    )
+                    wide_ref[field, x] = plane
+                    slot = x + 4 * WIDE * side
+                    here = group == slot
+                    shift = WIDE * slot
+                    moved = pltpu.roll(plane, shift, 1) if shift else plane
+                    down = jnp.where(here, moved, down)
+                    shift = (shift + WIDE) % LANE
+                    moved = pltpu.roll(plane, shift, 1) if shift else plane
+                    up = jnp.where(here, moved, up)
+                    at += WIDE
+                    x += 1
+            rows = pl.ds((field // 2) * (size_y + 2 * WIDE), size_y + 2 * WIDE)
+            down_ref[rows, :] = down
+            up_ref[rows, :] = up
+            field += 1
+
+
+def pack_z(first, second):
+    fields = first[0].shape[0] + second[0].shape[0]
+    rows = first[0].shape[2] + 2 * WIDE
+    message = jax.ShapeDtypeStruct(((fields + 1) // 2 * rows, LANE), F32)
+    return pl.pallas_call(
+        pack_z_kernel,
+        name="pack_z",
+        out_shape=(jax.ShapeDtypeStruct((fields, 4 * WIDE, rows, LANE), F32), message, message),
+        in_specs=[VMEM] * 12,
+        out_specs=(VMEM,) * 3,
+        compiler_params=pltpu.CompilerParams(vmem_limit_bytes=24 << 20),
+        cost_estimate=pl.CostEstimate(flops=1 << 20, bytes_accessed=1 << 20, transcendentals=0),
+    )(*first, *second)
+
+
+def sweep_kernel(wide_ref, before_ref, after_ref, out_ref, one_ref, two_ref, coef_ref):
+    rows = wide_ref.shape[2]
+    planes = wide_ref.shape[1]
+    size_x = planes - 2 * WIDE
+    size_y = rows - 2 * WIDE
+    lane = lax.broadcasted_iota(I32, (rows, LANE), 1)
+    first, last = lane == 0, lane == LANE - 1
+    main, rim = slice(0, rows), slice(rows, 2 * rows)
+    for field in range(5):
+        pair = slice((field // 2) * rows, (field // 2 + 1) * rows)
+        after, before = after_ref[pair, :], before_ref[pair, :]
+        for x in range(planes):
+            shift = WIDE * (x + planes * (field % 2))
+            near = pltpu.roll(after, (LANE - shift) % LANE, 1) if shift else after
+            far = pltpu.roll(before, LANE - WIDE - shift, 1) if LANE - WIDE - shift else before
+            edge = jnp.where(lane < WIDE, near, jnp.where(lane >= LANE - WIDE, far, 0.0))
+            one_ref[field, x, main] = wide_ref[field, x]
+            one_ref[field, x, rim] = edge
+
+    def along_z(middle, edge):
+        m, e = pltpu.roll(middle, LANE - 1, 1), pltpu.roll(edge, LANE - 1, 1)
+        next_m, next_e = jnp.where(last, e, m), jnp.where(last, m, e)
+        m, e = pltpu.roll(middle, 1, 1), pltpu.roll(edge, 1, 1)
+        return next_m, next_e, jnp.where(first, e, m), jnp.where(first, m, e)
+
+    @pl.loop(1, planes - 1)
+    def _(x):
+        ind = [one_ref[3, x, main], one_ref[3, x, rim]]
+        next_m, next_e, prev_m, prev_e = along_z(ind[0], ind[1])
+        for at, centre, along in ((main, ind[0], next_m - prev_m), (rim, ind[1], next_e - prev_e)):
+            density = rho_liquid + (rho_gas - rho_liquid) * centre
+            viscosity = mu_liquid + (mu_gas - mu_liquid) * centre
+            scale = time_step / density
+            pull = one_ref[4, x, at] * scale * 0.5
+            coef_ref[0, x, at] = viscosity * scale
+            coef_ref[1, x, at] = pull * (one_ref[3, x + 1, at] - one_ref[3, x - 1, at])
+            coef_ref[2, x, at] = pull * (pltpu.roll(centre, rows - 1, 0) - pltpu.roll(centre, 1, 0))
+            coef_ref[3, x, at] = pull * along
+
+    def sweep(source, margin, store):
+        @pl.loop(WIDE - margin, planes - WIDE + margin)
+        def _(x):
+            for c in range(3):
+                middle, edge = source[c, x, main], source[c, x, rim]
+                next_m, next_e, prev_m, prev_e = along_z(middle, edge)
+                parts = [(main, middle, next_m + prev_m)]
+                if margin:
+                    parts.append((rim, edge, next_e + prev_e))
+                for at, centre, along in parts:
+                    laplace = source[c, x + 1, at] + source[c, x - 1, at]
+                    laplace = laplace + pltpu.roll(centre, rows - 1, 0) + pltpu.roll(centre, 1, 0)
+                    laplace = laplace + along - 6.0 * centre
+                    store(c, x, at, centre + (coef_ref[0, x, at] * laplace + coef_ref[1 + c, x, at]))
+
+    def into(ref):
+        def store(c, x, at, value):
+            ref[c, x, at] = value
+        return store
+
+    def into_result(c, x, at, value):
+        out_ref[c, x - WIDE] = value[0:size_y]
+
+    sweep(one_ref, 3, into(two_ref))
+    sweep(two_ref, 2, into(one_ref))
+    sweep(one_ref, 1, into(two_ref))
+    sweep(two_ref, 0, into_result)
+
+
+def swept(wide, before, after):
+    _, planes, rows, _ = wide.shape
+    return pl.pallas_call(
+        sweep_kernel,
+        name="sweeps",
+        out_shape=jax.ShapeDtypeStruct((3, planes - 2 * WIDE, rows - 2 * WIDE, LANE), F32),
+        in_specs=[VMEM] * 3,
+        out_specs=VMEM,
+        scratch_shapes=[
+            pltpu.VMEM((5, planes, 2 * rows, LANE), F32),
+            pltpu.VMEM((3, planes, 2 * rows, LANE), F32),
+            pltpu.VMEM((4, planes, 2 * rows, LANE), F32),
+        ],
+        compiler_params=pltpu.CompilerParams(vmem_limit_bytes=40 << 20),
+        cost_estimate=pl.CostEstimate(flops=1 << 30, bytes_accessed=1 << 20, transcendentals=0),
+    )(wide, before, after)
+
+
+def both_ways(down, up, axis):
+    count = lax.axis_size(axis)
+    above = lax.ppermute(down, axis, [((i + 1) % count, i) for i in range(count)])
+    below = lax.ppermute(up, axis, [(i, (i + 1) % count) for i in range(count)])
+    return below, above
 
 
 def per_device(tri_geom, send_index, near_index, return_cell, velocity):
     size_x, size_y, size_z = near_index.shape
     group_x, group_y = lax.axis_size("gx"), lax.axis_size("gy")
+    vel_low, vel_high = velocity[:, :WIDE], velocity[:, WIDE:]
+    vel_below, vel_above = both_ways(vel_low, vel_high, "gx")
     mid_z = (lax.axis_index("gz") * size_z + size_z // 2).astype(F32)
     mid_x, mid_y = 0.5 * group_x * size_x, 0.5 * group_y * size_y
     outgoing = send_tables(tri_geom, send_index, jnp.stack([jnp.float32(mid_x), jnp.float32(mid_y), mid_z]))
     arrived = lax.all_to_all(
         outgoing.reshape(-1, 8, LANE), ("gx", "gy"), split_axis=0, concat_axis=0, tiled=True
     ).reshape(-1, LANE)
+    vel_down, vel_up = pack_y(vel_low, vel_high, vel_below, vel_above)
+    vel_under, vel_over = both_ways(vel_down, vel_up, "gy")
     own_x = (lax.axis_index("gx") * size_x + size_x // 2).astype(F32) - mid_x
     own_y = (lax.axis_index("gy") * size_y + size_y // 2).astype(F32) - mid_y
-    indicator, tension = cell_fields(arrived, near_index, jnp.stack([own_x, own_y, jnp.float32(0.0)]))
-    padded_ind = extended(indicator, (("gx", 0), ("gy", 1), ("gz", 2)), 1)
-    diffusion, forcing = coefficients(padded_ind, tension)
-    current = velocity
-    for repeat in range(NSWEEP):
-        padded = extended(current, (("gx", 1), ("gy", 2), ("gz", 3)), 1)
-        laplace = stencil(padded)
-        current = current + time_step * (diffusion * laplace + forcing)
+    indicator, low, high = cell_fields(arrived, near_index, jnp.stack([own_x, own_y, jnp.float32(0.0)]))
+    below, above = both_ways(low, high, "gx")
+    down, up = pack_y(low, high, below, above)
+    under, over = both_ways(down, up, "gy")
+    wide, down, up = pack_z(
+        (vel_low, vel_high, vel_below, vel_above, vel_under, vel_over), (low, high, below, above, under, over)
+    )
+    before, after = both_ways(down, up, "gz")
+    current = swept(wide, before, after)
     samples = vertex_samples(current.reshape(3, size_x * size_y, size_z), return_cell)
     returned = lax.all_to_all(
         samples.reshape(-1, 9 * LANE), ("gx", "gy"), split_axis=0, concat_axis=0, tiled=True

time: 169 us -> 118 us (0.70)
  starting transfers between devices: 60.3 us -> 22.7 us
  Pallas kernels: 38.4 us -> 51.2 us
  waiting for transfers between devices: 28.2 us -> 17.2 us
  local copies, waits for them, and re-layouts: 12.8 us -> 3.57 us
  other arithmetic: 5.48 us -> 0.15 us
    ppermute x30 -> x10, starting transfers between devices: 50.4 us -> 9.77 us  [the longest x5 5.22 us: both_ways(): below = lax.ppermute(up, axis, [(i, (i + 1) % count) for i in range(count)])]
    pallas_call x1 -> x5, Pallas kernels: 14 us -> 26.8 us  [the longest x1 14.2 us: cell_fields(): pl.pallas_call(cell_kernel, name='cell_fields', out_shape=(out, side, sid...]
    ppermute x30 -> x10, waiting for transfers between devices: 19.2 us -> 7.76 us  [the longest x5 4.52 us: both_ways(): below = lax.ppermute(up, axis, [(i, (i + 1) % count) for i in range(count)])]
    slice x20 -> x1, local copies, waits for them, and re-layouts: 7.03 us -> 0.76 us  [per_device(): vel_low, vel_high = (velocity[:, :WIDE], velocity[:, WIDE:])]
    add x4 -> x0, other arithmetic: 3.05 us -> none  [per_device(): current = current + time_step * (diffusion * laplace + forcing)]
    all_to_all x1, starting transfers between devices: 9.94 us -> 13 us  [per_device(): lax.all_to_all(outgoing.reshape(-1, 8, LANE), ('gx', 'gy'), split_axis=0,...]
    ppermute x8 -> x0, local copies, waits for them, and re-layouts: 2.69 us -> none  [the longest x4 1.35 us: extended(): lax.ppermute(tail, axis, [(i, (i + 1) % count) for i in range(count)])]
  transfers between devices with their start and end apart: 31 -> 11, of which waited for: 20 -> 7; matrix products, arithmetic and copies ran while one was open for 5% -> 1% of each run, Pallas kernels for 11% -> 13%
where the time goes in v2:
time: 118 us
  Pallas kernels  51.2 us (43%)
  starting transfers between devices  22.7 us (19%)
  blocking collectives  22.5 us (19%)
  waiting for transfers between devices  17.2 us (15%)
  local copies, waits for them, and re-layouts  3.57 us (3%)
    all_to_all x1, blocking collectives, per_device(): lax.all_to_all(samples.reshape(-1, 9 * LANE), ('gx', 'gy'), split_axis=0,...  22.5 us
    pallas_call x1, Pallas kernels, cell_fields(): pl.pallas_call(cell_kernel, name='cell_fields', out_shape=(out, side, sid...  14.2 us
    all_to_all x1, starting transfers between devices, per_device(): lax.all_to_all(outgoing.reshape(-1, 8, LANE), ('gx', 'gy'), split_axis=0,...  13 us
    pallas_call x1, Pallas kernels, vertex_samples(): pl.pallas_call(vertex_kernel, name='vertex_samples', out_shape=jax.ShapeD...  11.9 us
    all_to_all x1, waiting for transfers between devices, per_device(): lax.all_to_all(outgoing.reshape(-1, 8, LANE), ('gx', 'gy'), split_axis=0,...  9.46 us
    pallas_call x1, Pallas kernels, swept(): pl.pallas_call(sweep_kernel, name='sweeps', out_shape=jax.ShapeDtypeStruc...  9.14 us
    pallas_call x1, Pallas kernels, bring_home(): pl.pallas_call(home_kernel, name='bring_home', out_shape=jax.ShapeDtypeSt...  7.69 us
    ppermute x5, starting transfers between devices, both_ways(): below = lax.ppermute(up, axis, [(i, (i + 1) % count) for i in range(count)])  5.22 us
  transfers between devices with their start and end apart: 11, of which 7 were waited for; matrix products, arithmetic and copies ran while one was open for 1% of the time, Pallas kernels for 13%

profile of v2, /device:TPU:1, one launch (start us, length us, event | category | flops | bytes accessed | tf_op | source)
XLA Modules:
  0.0 118.1 jit_solution(2990079851136303863)
XLA Ops:
  0.6 0.1 pad_maximum_fusion.origin_ref
  0.7 0.0 copy-start
  0.7 1.0 copy-done
  1.8 0.0 copy-start.3
  1.8 0.8 copy-done.3
  2.5 0.0 copy-start.6
  2.5 0.0 copy-start.1
  2.5 4.8 %send_tables.1 = f32[512,128]{1,0:T(8,128)} custom-call(f32[10,8192]{1,0:T(8,128)S(1)} %copy-done, s32[64,128]{1,0:T(8,128)S(1)} %copy-done.3, f32[3]{0:T(128)S(1)} %pad_maximum_fusion.origin_ref), custom_call_target="tpu_custom_call" | custom-call | flops 2199023255552 | bytes 1048576 | tf_op jit(solution)/shard_map/send_tables/pallas_call | solution.py:125
  7.3 13.0 %all-to-all-start = ((f32[64,8,128]{2,1,0:T(8,128)}), f32[64,8,128]{2,1,0:T(8,128)S(1)}, u32[]{:S(2)}, u32[]{:S(2)}) async-start(f32[64,8,128]{2,1,0:T(8,128)} %bitcast.1), calls=%async_computation | async-start | bytes 524288 | tf_op jit(solution)/shard_map/all_to_all | solution.py:458
  20.3 0.0 copy-done.6
  20.3 0.8 fusion
  21.1 1.4 %collective-permute-start = (f32[3,4,32,128]{3,2,1,0:T(8,128)}, f32[3,4,32,128]{3,2,1,0:T(8,128)}, u32[]{:S(2)}, u32[]{:S(2)}) collective-permute-start(f32[3,4,32,128]{3,2,1,0:T(8,128)} %get-tuple-element.23.high_ref.refs_1_), channel_id=1, source_target_pairs={{0,32},{32,64},{64,96},{96,128},{128,160},{160,192},{192,224},{224... | collective-permute-start | bytes 589832 | tf_op jit(solution)/shard_map/ppermute | solution.py:446
  22.5 1.5 %collective-permute-start.1 = (f32[3,4,32,128]{3,2,1,0:T(8,128)}, f32[3,4,32,128]{3,2,1,0:T(8,128)}, u32[]{:S(2)}, u32[]{:S(2)}) collective-permute-start(f32[3,4,32,128]{3,2,1,0:T(8,128)} %get-tuple-element.24.low_ref.refs_0_), channel_id=1, source_target_pairs={{32,0},{64,32},{96,64},{128,96},{160,128},{192,160},{224,192},{0,2... | collective-permute-start | bytes 589832 | tf_op jit(solution)/shard_map/ppermute | solution.py:445
  24.0 0.1 pad_maximum_fusion.1.origin_ref
  24.0 9.5 %all-to-all-done = f32[64,8,128]{2,1,0:T(8,128)S(1)} async-done(((f32[64,8,128]{2,1,0:T(8,128)}), f32[64,8,128]{2,1,0:T(8,128)S(1)}, u32[]{:S(2)}, u32[]{:S(2)}) %all-to-all-start) | async-done | bytes 262176 | tf_op jit(solution)/shard_map/all_to_all | solution.py:458
  33.5 0.0 copy-done.1
  33.5 14.2 %cell_fields.1 = (f32[8,32,128]{2,1,0:T(8,128)}, f32[2,4,32,128]{3,2,1,0:T(8,128)S(1)}, f32[2,4,32,128]{3,2,1,0:T(8,128)S(1)}) custom-call(f32[512,128]{1,0:T(8,128)S(1)} %bitcast.10, s32[8,32,128]{2,1,0:T(8,128)S(1)} %copy-done.1, f32[3]{0:T(128)S(1)} %pad_maximum_fusion.1.origin_ref), custom_call_target="tpu_custom_call" | custom-call | flops 6597069766656 | bytes 1048576 | tf_op jit(solution)/shard_map/cell_fields/pallas_call | solution.py:181
  47.7 1.1 collective-permute-start.5
  48.8 0.4 collective-permute-start.4
  49.1 0.0 collective-permute-done.below_ref.refs_2_
  49.1 0.0 collective-permute-done.1.above_ref.refs_3_
  49.1 1.3 %pack_y.2 = (f32[192,128]{1,0:T(8,128)S(1)}, f32[192,128]{1,0:T(8,128)S(1)}) custom-call(f32[3,4,32,128]{3,2,1,0:T(8,128)} %get-tuple-element.24.low_ref.refs_0_, f32[3,4,32,128]{3,2,1,0:T(8,128)} %get-tuple-element.23.high_ref.refs_1_, f32[3,4,32,128]{3,2,1,0:T(8,128)} %collective-permute-done.below_ref.refs_2_, ...), custom_call_target="tpu_custom_call" | custom-call | flops 1048576 | bytes 1048576 | tf_op jit(solution)/shard_map/pack_y/pallas_call | solution.py:294
  50.4 1.3 %collective-permute-start.2 = (f32[192,128]{1,0:T(8,128)S(1)}, f32[192,128]{1,0:T(8,128)S(1)}, u32[]{:S(2)}, u32[]{:S(2)}) collective-permute-start(f32[192,128]{1,0:T(8,128)S(1)} %get-tuple-element.13), channel_id=1, source_target_pairs={{0,4},{4,8},{8,12},{12,16},{16,20},{20,24},{24,28},{28,0},{1,5},{5... | collective-permute-start | bytes 294920 | tf_op jit(solution)/shard_map/ppermute | solution.py:446
  51.7 0.0 collective-permute-start.3
  51.7 0.8 collective-permute-done.5.above_ref.refs_9_
  52.5 2.2 %collective-permute-done.4.below_ref.refs_8_ = f32[2,4,32,128]{3,2,1,0:T(8,128)S(1)} collective-permute-done((f32[2,4,32,128]{3,2,1,0:T(8,128)S(1)}, f32[2,4,32,128]{3,2,1,0:T(8,128)S(1)}, u32[]{:S(2)}, u32[]{:S(2)}) %collective-permute-start.4) | collective-permute-done | bytes 131104 | tf_op jit(solution)/shard_map/ppermute | solution.py:446
  54.7 0.8 collective-permute-start.6
  55.5 0.5 collective-permute-start.7
  55.9 0.0 collective-permute-done.2.refs_4_
  56.0 0.1 collective-permute-done.3.refs_5_
  56.1 0.8 collective-permute-done.6.refs_10_
  56.8 2.4 %collective-permute-done.7.refs_11_ = f32[128,128]{1,0:T(8,128)S(1)} collective-permute-done((f32[128,128]{1,0:T(8,128)S(1)}, f32[128,128]{1,0:T(8,128)S(1)}, u32[]{:S(2)}, u32[]{:S(2)}) %collective-permute-start.7) | collective-permute-done | bytes 65568 | tf_op jit(solution)/shard_map/ppermute | solution.py:445
  59.2 2.2 %pack_z.1 = (f32[5,16,40,128]{3,2,1,0:T(8,128)S(1)}, f32[120,128]{1,0:T(8,128)S(1)}, f32[120,128]{1,0:T(8,128)S(1)}) custom-call(f32[3,4,32,128]{3,2,1,0:T(8,128)} %get-tuple-element.24.low_ref.refs_0_, f32[3,4,32,128]{3,2,1,0:T(8,128)} %get-tuple-element.23.high_ref.refs_1_, f32[3,4,32,128]{3,2,1,0:T(8,128)} %collective-permute-done.below_ref.refs_2_, ...), custom_call_target="tpu_custom_call" | custom-call | flops 1048576 | bytes 1048576 | tf_op jit(solution)/shard_map/pack_z/pallas_call | solution.py:346
  61.4 1.4 %collective-permute-start.8 = (f32[120,128]{1,0:T(8,128)S(1)}, f32[120,128]{1,0:T(8,128)S(1)}, u32[]{:S(2)}, u32[]{:S(2)}) collective-permute-start(f32[120,128]{1,0:T(8,128)S(1)} %get-tuple-element.20), channel_id=1, source_target_pairs={{0,1},{1,2},{2,3},{3,0},{4,5},{5,6},{6,7},{7,4},{8,9},{9,10},{10,1... | collective-permute-start | bytes 184328 | tf_op jit(solution)/shard_map/ppermute | solution.py:446
  62.7 1.5 %collective-permute-start.9 = (f32[120,128]{1,0:T(8,128)S(1)}, f32[120,128]{1,0:T(8,128)S(1)}, u32[]{:S(2)}, u32[]{:S(2)}) collective-permute-start(f32[120,128]{1,0:T(8,128)S(1)} %get-tuple-element.21), channel_id=1, source_target_pairs={{1,0},{2,1},{3,2},{0,3},{5,4},{6,5},{7,6},{4,7},{9,8},{10,9},{11,1... | collective-permute-start | bytes 184328 | tf_op jit(solution)/shard_map/ppermute | solution.py:445
  64.3 1.5 %collective-permute-done.8.before_ref = f32[120,128]{1,0:T(8,128)S(1)} collective-permute-done((f32[120,128]{1,0:T(8,128)S(1)}, f32[120,128]{1,0:T(8,128)S(1)}, u32[]{:S(2)}, u32[]{:S(2)}) %collective-permute-start.8) | collective-permute-done | bytes 61472 | tf_op jit(solution)/shard_map/ppermute | solution.py:446
  65.8 0.0 collective-permute-done.9.after_ref
  65.8 0.0 copy-start.2
  65.8 9.1 %sweeps.1 = f32[3,8,32,128]{3,2,1,0:T(8,128)} custom-call(f32[5,16,40,128]{3,2,1,0:T(8,128)S(1)} %get-tuple-element.19.wide_ref, f32[120,128]{1,0:T(8,128)S(1)} %collective-permute-done.8.before_ref, f32[120,128]{1,0:T(8,128)S(1)} %collective-permute-done.9.after_ref), custom_call_target="tpu_custom_call" | custom-call | flops 1073741824 | bytes 1048576 | tf_op jit(solution)/shard_map/sweeps/pallas_call | solution.py:427
  75.0 0.0 copy-done.2
  75.0 0.0 copy-start.5
  75.0 1.0 copy-done.5
  76.0 0.0 copy-start.4
  76.0 11.9 %vertex_samples.1 = f32[576,128]{1,0:T(8,128)S(1)} custom-call(f32[3,256,128]{2,1,0:T(8,128)S(1)} %bitcast.11, s32[3,8192]{1,0:T(4,128)S(1)} %copy-done.2), custom_call_target="tpu_custom_call" | custom-call | flops 10995116277760 | bytes 1048576 | tf_op jit(solution)/shard_map/vertex_samples/pallas_call | solution.py:216
  87.8 22.5 %all_to_all.14 = f32[64,1,1152]{2,1,0:T(1,128)S(1)} all-to-all(f32[64,1,1152]{2,1,0:T(1,128)S(1)} %bitcast.9), channel_id=1, replica_groups=mesh['gx'=8,'gy'=8,'gz'=4] {'gx','gy'}, dimensions={0} | all-to-all | bytes 589824 | tf_op jit(solution)/shard_map/all_to_all | solution.py:475
  110.4 0.0 copy-done.4
  110.4 7.7 %bring_home.1 = f32[9,8192]{1,0:T(8,128)} custom-call(f32[576,128]{1,0:T(8,128)S(1)} %bitcast.8, s32[64,128]{1,0:T(8,128)S(1)} %copy-done.4), custom_call_target="tpu_custom_call" | custom-call | flops 2199023255552 | bytes 1048576 | tf_op jit(solution)/shard_map/bring_home/pallas_call | solution.py:265
  (1 shorter events, 0.0 us)
Async XLA Ops:
  0.7 1.0 copy-start
  1.8 0.8 copy-start.3
  2.5 17.8 %copy-start.6 = (f32[3,8,32,128]{3,2,1,0:T(8,128)S(1)}, f32[3,8,32,128]{3,2,1,0:T(8,128)}, u32[]{:S(2)}) copy-start(f32[3,8,32,128]{3,2,1,0:T(8,128)} %param.9) | copy-start | bytes 1179652
  2.5 31.0 %copy-start.1 = (s32[8,32,128]{2,1,0:T(8,128)S(1)}, s32[8,32,128]{2,1,0:T(8,128)}, u32[]{:S(2)}) copy-start(s32[8,32,128]{2,1,0:T(8,128)} %near_ref.1) | copy-start | bytes 393220
  7.3 26.2 %all-to-all-start = ((f32[64,8,128]{2,1,0:T(8,128)}), f32[64,8,128]{2,1,0:T(8,128)S(1)}, u32[]{:S(2)}, u32[]{:S(2)}) async-start(f32[64,8,128]{2,1,0:T(8,128)} %bitcast.1), calls=%async_computation | async-start | bytes 524288 | tf_op jit(solution)/shard_map/all_to_all | solution.py:458
  21.1 28.0 %collective-permute-start = (f32[3,4,32,128]{3,2,1,0:T(8,128)}, f32[3,4,32,128]{3,2,1,0:T(8,128)}, u32[]{:S(2)}, u32[]{:S(2)}) collective-permute-start(f32[3,4,32,128]{3,2,1,0:T(8,128)} %get-tuple-element.23.high_ref.refs_1_), channel_id=1, source_target_pairs={{0,32},{32,64},{64,96},{96,128},{128,160},{160,192},{192,224},{224... | collective-permute-start | bytes 589832 | tf_op jit(solution)/shard_map/ppermute | solution.py:446
  22.5 26.7 %collective-permute-start.1 = (f32[3,4,32,128]{3,2,1,0:T(8,128)}, f32[3,4,32,128]{3,2,1,0:T(8,128)}, u32[]{:S(2)}, u32[]{:S(2)}) collective-permute-start(f32[3,4,32,128]{3,2,1,0:T(8,128)} %get-tuple-element.24.low_ref.refs_0_), channel_id=1, source_target_pairs={{32,0},{64,32},{96,64},{128,96},{160,128},{192,160},{224,192},{0,2... | collective-permute-start | bytes 589832 | tf_op jit(solution)/shard_map/ppermute | solution.py:445
  47.7 4.8 %collective-permute-start.5 = (f32[2,4,32,128]{3,2,1,0:T(8,128)S(1)}, f32[2,4,32,128]{3,2,1,0:T(8,128)S(1)}, u32[]{:S(2)}, u32[]{:S(2)}) collective-permute-start(f32[2,4,32,128]{3,2,1,0:T(8,128)S(1)} %get-tuple-element.15.low_ref.refs_6_), channel_id=1, source_target_pairs={{32,0},{64,32},{96,64},{128,96},{160,128},{192,160},{224,192},{0,2... | collective-permute-start | bytes 393224 | tf_op jit(solution)/shard_map/ppermute | solution.py:445
  48.8 5.9 %collective-permute-start.4 = (f32[2,4,32,128]{3,2,1,0:T(8,128)S(1)}, f32[2,4,32,128]{3,2,1,0:T(8,128)S(1)}, u32[]{:S(2)}, u32[]{:S(2)}) collective-permute-start(f32[2,4,32,128]{3,2,1,0:T(8,128)S(1)} %get-tuple-element.16.high_ref.refs_7_), channel_id=1, source_target_pairs={{0,32},{32,64},{64,96},{96,128},{128,160},{160,192},{192,224},{224... | collective-permute-start | bytes 393224 | tf_op jit(solution)/shard_map/ppermute | solution.py:446
  50.4 5.5 %collective-permute-start.2 = (f32[192,128]{1,0:T(8,128)S(1)}, f32[192,128]{1,0:T(8,128)S(1)}, u32[]{:S(2)}, u32[]{:S(2)}) collective-permute-start(f32[192,128]{1,0:T(8,128)S(1)} %get-tuple-element.13), channel_id=1, source_target_pairs={{0,4},{4,8},{8,12},{12,16},{16,20},{20,24},{24,28},{28,0},{1,5},{5... | collective-permute-start | bytes 294920 | tf_op jit(solution)/shard_map/ppermute | solution.py:446
  51.7 4.3 %collective-permute-start.3 = (f32[192,128]{1,0:T(8,128)S(1)}, f32[192,128]{1,0:T(8,128)S(1)}, u32[]{:S(2)}, u32[]{:S(2)}) collective-permute-start(f32[192,128]{1,0:T(8,128)S(1)} %get-tuple-element.14), channel_id=1, source_target_pairs={{4,0},{8,4},{12,8},{16,12},{20,16},{24,20},{28,24},{0,28},{5,1},{9... | collective-permute-start | bytes 294920 | tf_op jit(solution)/shard_map/ppermute | solution.py:445
  54.7 2.1 %collective-permute-start.6 = (f32[128,128]{1,0:T(8,128)S(1)}, f32[128,128]{1,0:T(8,128)S(1)}, u32[]{:S(2)}, u32[]{:S(2)}) collective-permute-start(f32[128,128]{1,0:T(8,128)S(1)} %get-tuple-element.17), channel_id=1, source_target_pairs={{0,4},{4,8},{8,12},{12,16},{16,20},{20,24},{24,28},{28,0},{1,5},{5... | collective-permute-start | bytes 196616 | tf_op jit(solution)/shard_map/ppermute | solution.py:446
  55.5 3.7 %collective-permute-start.7 = (f32[128,128]{1,0:T(8,128)S(1)}, f32[128,128]{1,0:T(8,128)S(1)}, u32[]{:S(2)}, u32[]{:S(2)}) collective-permute-start(f32[128,128]{1,0:T(8,128)S(1)} %get-tuple-element.18), channel_id=1, source_target_pairs={{4,0},{8,4},{12,8},{16,12},{20,16},{24,20},{28,24},{0,28},{5,1},{9... | collective-permute-start | bytes 196616 | tf_op jit(solution)/shard_map/ppermute | solution.py:445
  61.4 4.4 %collective-permute-start.8 = (f32[120,128]{1,0:T(8,128)S(1)}, f32[120,128]{1,0:T(8,128)S(1)}, u32[]{:S(2)}, u32[]{:S(2)}) collective-permute-start(f32[120,128]{1,0:T(8,128)S(1)} %get-tuple-element.20), channel_id=1, source_target_pairs={{0,1},{1,2},{2,3},{3,0},{4,5},{5,6},{6,7},{7,4},{8,9},{9,10},{10,1... | collective-permute-start | bytes 184328 | tf_op jit(solution)/shard_map/ppermute | solution.py:446
  62.7 3.1 %collective-permute-start.9 = (f32[120,128]{1,0:T(8,128)S(1)}, f32[120,128]{1,0:T(8,128)S(1)}, u32[]{:S(2)}, u32[]{:S(2)}) collective-permute-start(f32[120,128]{1,0:T(8,128)S(1)} %get-tuple-element.21), channel_id=1, source_target_pairs={{1,0},{2,1},{3,2},{0,3},{5,4},{6,5},{7,6},{4,7},{9,8},{10,9},{11,1... | collective-permute-start | bytes 184328 | tf_op jit(solution)/shard_map/ppermute | solution.py:445
  65.8 9.1 %copy-start.2 = (s32[3,8192]{1,0:T(4,128)S(1)}, s32[3,8192]{1,0:T(4,128)}, u32[]{:S(2)}) copy-start(s32[3,8192]{1,0:T(4,128)} %cell_ref.1) | copy-start | bytes 294916
  75.0 1.0 copy-start.5
  76.0 34.4 %copy-start.4 = (s32[64,128]{1,0:T(8,128)S(1)}, s32[64,128]{1,0:T(8,128)}, u32[]{:S(2)}) copy-start(s32[64,128]{1,0:T(8,128)} %send_ref.3) | copy-start | bytes 98308

commit v3 on v2

--- a/solution.py
+++ b/solution.py
@@ -17,12 +17,14 @@
 
 F32, BF16, I32 = jnp.float32, jnp.bfloat16, jnp.int32
 LANE = 128
+SPAN = 2
 VMEM = pl.BlockSpec(memory_space=pltpu.VMEM)
 
 
 def one_hot(rows, index):
-    level = lax.broadcasted_iota(I32, (rows, index.shape[1]), 0)
-    return jnp.where(level == index, 1.0, 0.0).astype(BF16)
+    level = lax.broadcasted_iota(I32, (rows, index.shape[1]), 0).astype(F32).astype(BF16)
+    same = level == index.astype(F32).astype(BF16)
+    return jnp.where(same, jnp.ones_like(level), jnp.zeros_like(level))
 
 
 def fold_lines(lines):
@@ -60,13 +62,13 @@
     sub = lax.broadcasted_iota(I32, (8, LANE), 0)
     count = sum(groups)
     found = [[] for _ in groups]
-    for pair in range(4):
-        index = jnp.concatenate([lines[2 * pair], lines[2 * pair + 1]], axis=1)
+    for pair in range(8 // SPAN):
+        index = jnp.concatenate(lines[SPAN * pair:SPAN * (pair + 1)], axis=1)
         row = index >> 7
         hot = one_hot(2 * LANE, ((row >> shift) << 7) + (index & 127))
         product = jnp.dot(table_ref[...], hot, preferred_element_type=F32)
         place = jnp.where(index < 0, -1, row & (half - 1))
-        for side in range(2):
+        for side in range(SPAN):
             here = place[:, side * LANE:(side + 1) * LANE]
             masks = [sub + 8 * t == here for t in range(tiles)]
             picked = []
@@ -111,7 +113,7 @@
     columns += parts_of(offset, 3) + parts_of(geom[9], 2)
     put_table(table_ref, columns, half)
 
-    @pl.loop(0, send_ref.shape[0] // 8)
+    @pl.loop(0, send_ref.shape[0] // 8, unroll=8)
     def _(tile):
         index = send_ref[pl.ds(tile * 8, 8), :]
         found = look_up(table_ref, (2, 2, 2, 3, 2), half, [index[s:s + 1] for s in range(8)])
@@ -151,7 +153,7 @@
     at_z = lax.broadcasted_iota(I32, (8, LANE), 1).astype(F32) + (0.5 - mid_z)
     tiles = size_y // 8
 
-    @pl.loop(0, size_x * tiles)
+    @pl.loop(0, size_x * tiles, unroll=8)
     def _(step):
         x = lax.shift_right_logical(step, tiles.bit_length() - 1)
         y = pl.multiple_of((step & (tiles - 1)) * 8, 8)
@@ -190,16 +192,18 @@
     )(tab, near, origin)
 
 
-def vertex_kernel(field_ref, cell_ref, out_ref, table_ref):
-    comps, rows, _ = field_ref.shape
-    half = rows // 2
-    columns = []
+def sample_vertices(field_ref, cell_ref, out_ref, table_ref):
+    comps, size_x, size_y, _ = field_ref.shape
+    half = size_x * size_y // 2
     for c in range(comps):
-        columns += parts_of(field_ref[c], 2)
-    put_table(table_ref, columns, half)
+        for x in range(size_x):
+            lanes = slice(LANE * (x // (size_x // 2)), LANE * (x // (size_x // 2)) + LANE)
+            for p, part in enumerate(parts_of(field_ref[c, x], 2)):
+                start = (2 * c + p) * half + (x % (size_x // 2)) * size_y
+                table_ref[start:start + size_y, lanes] = part
     sources = cell_ref.shape[1] // LANE
 
-    @pl.loop(0, sources // 8)
+    @pl.loop(0, sources // 8, unroll=8)
     def _(tile):
         for v in range(3):
             lines = [
@@ -210,25 +214,10 @@
                 out_ref[pl.ds(tile * 72 + 3 * c + v, 8, stride=9), :] = found[c]
 
 
-def vertex_samples(field, cells):
-    comps, rows, _ = field.shape
-    sources = cells.shape[1] // LANE
-    return pl.pallas_call(
-        vertex_kernel,
-        name="vertex_samples",
-        out_shape=jax.ShapeDtypeStruct((sources * 9, LANE), F32),
-        in_specs=[VMEM, VMEM],
-        out_specs=VMEM,
-        scratch_shapes=[pltpu.VMEM((6 * rows // 2, 2 * LANE), BF16)],
-        compiler_params=pltpu.CompilerParams(vmem_limit_bytes=40 << 20),
-        cost_estimate=pl.CostEstimate(flops=10 << 40, bytes_accessed=1 << 20, transcendentals=0),
-    )(field, cells)
-
-
-def home_kernel(back_ref, send_ref, out_ref, left_ref, right_ref, total_ref):
+def home_kernel(back_ref, send_ref, out_ref, left_ref, right_ref, total_ref, sum_ref):
     dests = send_ref.shape[0]
     blocks = out_ref.shape[1] // (2 * LANE)
-    chunk = left_ref.shape[1] // (2 * LANE)
+    chunk = right_ref.shape[1] // LANE
     total_ref[...] = jnp.zeros_like(total_ref)
 
     @pl.loop(0, dests // chunk)
@@ -236,32 +225,32 @@
         for line in range(chunk):
             d = step * chunk + line
             index = send_ref[pl.ds(d, 1), :]
-            low = slice(line * LANE, (line + 1) * LANE)
-            high = slice((chunk + line) * LANE, (chunk + line + 1) * LANE)
-            hot = one_hot(2 * LANE, index & (2 * LANE - 1))
-            right_ref[:, low] = hot
-            right_ref[:, high] = hot
-            mine = lax.broadcasted_iota(I32, (blocks, LANE), 0) == (index >> 8)
+            at = slice(line * LANE, (line + 1) * LANE)
+            right_ref[:, at] = one_hot(2 * LANE, index & (2 * LANE - 1))
+            mine = one_hot(blocks, index >> 8)
             for r in range(9):
-                value = back_ref[pl.ds(d * 9 + r, 1), :]
-                head = value.astype(BF16).astype(F32)
-                tail = value - head
-                rows = slice(r * blocks, (r + 1) * blocks)
-                left_ref[rows, low] = jnp.where(mine, head, 0.0).astype(BF16)
-                left_ref[rows, high] = jnp.where(mine, tail, 0.0).astype(BF16)
+                value = jnp.broadcast_to(back_ref[pl.ds(d * 9 + r, 1), :], (blocks, LANE))
+                head = value.astype(BF16)
+                tail = (value - head.astype(F32)).astype(BF16)
+                left_ref[r * blocks:(r + 1) * blocks, at] = mine * head
+                left_ref[(9 + r) * blocks:(10 + r) * blocks, at] = mine * tail
         total_ref[...] += lax.dot_general(
             left_ref[...], right_ref[...], (((1,), (1,)), ((), ())), preferred_element_type=F32
         )
 
-    for r in range(9):
-        for b in range(blocks):
-            at = r * blocks + b
-            out_ref[r:r + 1, b * 2 * LANE:(b + 1) * 2 * LANE] = total_ref[at:at + 1, :]
+    rows = 9 * blocks
+    for side in range(2):
+        lanes = slice(side * LANE, (side + 1) * LANE)
+        sum_ref[side * rows:(side + 1) * rows, :] = total_ref[0:rows, lanes] + total_ref[rows:2 * rows, lanes]
+    for b in range(blocks):
+        for side in range(2):
+            at = (2 * b + side) * LANE
+            out_ref[:, at:at + LANE] = sum_ref[pl.ds(side * rows + b, 9, stride=blocks), :]
 
 
 def bring_home(back, send, triangles):
     blocks = triangles // (2 * LANE)
-    chunk = 4
+    chunk = 16
     return pl.pallas_call(
         home_kernel,
         name="bring_home",
@@ -269,9 +258,10 @@
         in_specs=[VMEM, VMEM],
         out_specs=VMEM,
         scratch_shapes=[
-            pltpu.VMEM((9 * blocks, 2 * chunk * LANE), BF16),
-            pltpu.VMEM((2 * LANE, 2 * chunk * LANE), BF16),
-            pltpu.VMEM((9 * blocks, 2 * LANE), F32),
+            pltpu.VMEM((18 * blocks, chunk * LANE), BF16),
+            pltpu.VMEM((2 * LANE, chunk * LANE), BF16),
+            pltpu.VMEM((18 * blocks, 2 * LANE), F32),
+            pltpu.VMEM((18 * blocks, LANE), F32),
         ],
         compiler_params=pltpu.CompilerParams(vmem_limit_bytes=40 << 20),
         cost_estimate=pl.CostEstimate(flops=2 << 40, bytes_accessed=1 << 20, transcendentals=0),
@@ -319,10 +309,10 @@
             x = 0
             for ref in (below_ref, low_ref, high_ref, above_ref):
                 for k in range(WIDE):
-                    plane = jnp.concatenate(
-                        [ref[c, k], over_ref[at:at + WIDE, :], under_ref[at:at + WIDE, :]], axis=0
-                    )
-                    wide_ref[field, x] = plane
+                    wide_ref[field, x, 0:WIDE] = under_ref[at:at + WIDE, :]
+                    wide_ref[field, x, WIDE:WIDE + size_y] = ref[c, k]
+                    wide_ref[field, x, WIDE + size_y:] = over_ref[at:at + WIDE, :]
+                    plane = wide_ref[field, x]
                     slot = x + 4 * WIDE * side
                     here = group == slot
                     shift = WIDE * slot
@@ -354,14 +344,19 @@
     )(*first, *second)
 
 
-def sweep_kernel(wide_ref, before_ref, after_ref, out_ref, one_ref, two_ref, coef_ref):
-    rows = wide_ref.shape[2]
-    planes = wide_ref.shape[1]
-    size_x = planes - 2 * WIDE
+SPARE = 8
+
+
+def sweep_kernel(wide_ref, before_ref, after_ref, cell_ref, out_ref, sample_ref, one_ref, two_ref, coef_ref, table_ref):
+    planes, rows = wide_ref.shape[1:3]
     size_y = rows - 2 * WIDE
+    stride = rows + 2 * SPARE
+
+    def ends(count):
+        lane = lax.broadcasted_iota(I32, (count, LANE), 1)
+        return lane == 0, lane == LANE - 1
+
     lane = lax.broadcasted_iota(I32, (rows, LANE), 1)
-    first, last = lane == 0, lane == LANE - 1
-    main, rim = slice(0, rows), slice(rows, 2 * rows)
     for field in range(5):
         pair = slice((field // 2) * rows, (field // 2 + 1) * rows)
         after, before = after_ref[pair, :], before_ref[pair, :]
@@ -370,74 +365,86 @@
             near = pltpu.roll(after, (LANE - shift) % LANE, 1) if shift else after
             far = pltpu.roll(before, LANE - WIDE - shift, 1) if LANE - WIDE - shift else before
             edge = jnp.where(lane < WIDE, near, jnp.where(lane >= LANE - WIDE, far, 0.0))
-            one_ref[field, x, main] = wide_ref[field, x]
-            one_ref[field, x, rim] = edge
-
-    def along_z(middle, edge):
-        m, e = pltpu.roll(middle, LANE - 1, 1), pltpu.roll(edge, LANE - 1, 1)
-        next_m, next_e = jnp.where(last, e, m), jnp.where(last, m, e)
-        m, e = pltpu.roll(middle, 1, 1), pltpu.roll(edge, 1, 1)
-        return next_m, next_e, jnp.where(first, e, m), jnp.where(first, m, e)
-
-    @pl.loop(1, planes - 1)
+            one_ref[field, x, SPARE:SPARE + rows] = wide_ref[field, x]
+            one_ref[field, x, stride + SPARE:stride + SPARE + rows] = edge
+
+    def neighbours(middle, edge):
+        first, last = ends(middle.shape[0])
+        return (
+            pltpu.roll(jnp.where(first, edge, middle), LANE - 1, 1),
+            pltpu.roll(jnp.where(last, edge, middle), 1, 1),
+        )
+
+    @pl.loop(1, planes - 1, unroll=2)
     def _(x):
-        ind = [one_ref[3, x, main], one_ref[3, x, rim]]
-        next_m, next_e, prev_m, prev_e = along_z(ind[0], ind[1])
-        for at, centre, along in ((main, ind[0], next_m - prev_m), (rim, ind[1], next_e - prev_e)):
+        for at in (SPARE, stride + SPARE):
+            other = SPARE if at > SPARE else stride + SPARE
+            here = pl.ds(at, rows)
+            centre = one_ref[3, x, here]
+            later, sooner = neighbours(centre, one_ref[3, x, pl.ds(other, rows)])
             density = rho_liquid + (rho_gas - rho_liquid) * centre
             viscosity = mu_liquid + (mu_gas - mu_liquid) * centre
             scale = time_step / density
-            pull = one_ref[4, x, at] * scale * 0.5
-            coef_ref[0, x, at] = viscosity * scale
-            coef_ref[1, x, at] = pull * (one_ref[3, x + 1, at] - one_ref[3, x - 1, at])
-            coef_ref[2, x, at] = pull * (pltpu.roll(centre, rows - 1, 0) - pltpu.roll(centre, 1, 0))
-            coef_ref[3, x, at] = pull * along
-
-    def sweep(source, margin, store):
-        @pl.loop(WIDE - margin, planes - WIDE + margin)
+            pull = one_ref[4, x, here] * scale * 0.5
+            coef_ref[0, x, here] = viscosity * scale
+            coef_ref[1, x, here] = pull * (one_ref[3, x + 1, here] - one_ref[3, x - 1, here])
+            coef_ref[2, x, here] = pull * (one_ref[3, x, pl.ds(at + 1, rows)] - one_ref[3, x, pl.ds(at - 1, rows)])
+            coef_ref[3, x, here] = pull * (later - sooner)
+
+    def sweep(source, margin, offset, count, store):
+        starts = (offset, stride + offset) if margin else (offset,)
+
+        @pl.loop(WIDE - margin, planes - WIDE + margin, unroll=2)
         def _(x):
             for c in range(3):
-                middle, edge = source[c, x, main], source[c, x, rim]
-                next_m, next_e, prev_m, prev_e = along_z(middle, edge)
-                parts = [(main, middle, next_m + prev_m)]
-                if margin:
-                    parts.append((rim, edge, next_e + prev_e))
-                for at, centre, along in parts:
-                    laplace = source[c, x + 1, at] + source[c, x - 1, at]
-                    laplace = laplace + pltpu.roll(centre, rows - 1, 0) + pltpu.roll(centre, 1, 0)
-                    laplace = laplace + along - 6.0 * centre
-                    store(c, x, at, centre + (coef_ref[0, x, at] * laplace + coef_ref[1 + c, x, at]))
+                planes_here = [source[c, x, pl.ds(stride * k + offset, count)] for k in range(2)]
+                for k, at in enumerate(starts):
+                    here = pl.ds(at, count)
+                    centre = planes_here[k]
+                    later, sooner = neighbours(centre, planes_here[1 - k])
+                    laplace = source[c, x + 1, here] + source[c, x - 1, here]
+                    laplace = laplace + source[c, x, pl.ds(at + 1, count)] + source[c, x, pl.ds(at - 1, count)]
+                    laplace = laplace + later + sooner - 6.0 * centre
+                    store(c, x, here, centre + (coef_ref[0, x, here] * laplace + coef_ref[1 + c, x, here]))
 
     def into(ref):
-        def store(c, x, at, value):
-            ref[c, x, at] = value
+        def store(c, x, here, value):
+            ref[c, x, here] = value
         return store
 
-    def into_result(c, x, at, value):
-        out_ref[c, x - WIDE] = value[0:size_y]
-
-    sweep(one_ref, 3, into(two_ref))
-    sweep(two_ref, 2, into(one_ref))
-    sweep(one_ref, 1, into(two_ref))
-    sweep(two_ref, 0, into_result)
-
-
-def swept(wide, before, after):
+    def into_result(c, x, here, value):
+        out_ref[c, x - WIDE] = value
+
+    sweep(one_ref, 3, SPARE, rows, into(two_ref))
+    sweep(two_ref, 2, SPARE, rows, into(one_ref))
+    sweep(one_ref, 1, SPARE, rows, into(two_ref))
+    sweep(two_ref, 0, SPARE + WIDE, size_y, into_result)
+    sample_vertices(out_ref, cell_ref, sample_ref, table_ref)
+
+
+def swept(wide, before, after, cells):
     _, planes, rows, _ = wide.shape
+    size_x, size_y = planes - 2 * WIDE, rows - 2 * WIDE
+    sources = cells.shape[1] // LANE
+    stride = rows + 2 * SPARE
     return pl.pallas_call(
         sweep_kernel,
         name="sweeps",
-        out_shape=jax.ShapeDtypeStruct((3, planes - 2 * WIDE, rows - 2 * WIDE, LANE), F32),
-        in_specs=[VMEM] * 3,
-        out_specs=VMEM,
+        out_shape=(
+            jax.ShapeDtypeStruct((3, size_x, size_y, LANE), F32),
+            jax.ShapeDtypeStruct((sources * 9, LANE), F32),
+        ),
+        in_specs=[VMEM] * 4,
+        out_specs=(VMEM, VMEM),
         scratch_shapes=[
-            pltpu.VMEM((5, planes, 2 * rows, LANE), F32),
-            pltpu.VMEM((3, planes, 2 * rows, LANE), F32),
-            pltpu.VMEM((4, planes, 2 * rows, LANE), F32),
+            pltpu.VMEM((5, planes, 2 * stride, LANE), F32),
+            pltpu.VMEM((3, planes, 2 * stride, LANE), F32),
+            pltpu.VMEM((4, planes, 2 * stride, LANE), F32),
+            pltpu.VMEM((6 * size_x * size_y // 2, 2 * LANE), BF16),
         ],
         compiler_params=pltpu.CompilerParams(vmem_limit_bytes=40 << 20),
-        cost_estimate=pl.CostEstimate(flops=1 << 30, bytes_accessed=1 << 20, transcendentals=0),
-    )(wide, before, after)
+        cost_estimate=pl.CostEstimate(flops=10 << 40, bytes_accessed=1 << 20, transcendentals=0),
+    )(wide, before, after, cells)
 
 
 def both_ways(down, up, axis):
@@ -460,6 +467,7 @@
     ).reshape(-1, LANE)
     vel_down, vel_up = pack_y(vel_low, vel_high, vel_below, vel_above)
     vel_under, vel_over = both_ways(vel_down, vel_up, "gy")
+    arrived, vel_under, vel_over = lax.optimization_barrier((arrived, vel_under, vel_over))
     own_x = (lax.axis_index("gx") * size_x + size_x // 2).astype(F32) - mid_x
     own_y = (lax.axis_index("gy") * size_y + size_y // 2).astype(F32) - mid_y
     indicator, low, high = cell_fields(arrived, near_index, jnp.stack([own_x, own_y, jnp.float32(0.0)]))
@@ -470,8 +478,7 @@
         (vel_low, vel_high, vel_below, vel_above, vel_under, vel_over), (low, high, below, above, under, over)
     )
     before, after = both_ways(down, up, "gz")
-    current = swept(wide, before, after)
-    samples = vertex_samples(current.reshape(3, size_x * size_y, size_z), return_cell)
+    current, samples = swept(wide, before, after, return_cell)
     returned = lax.all_to_all(
         samples.reshape(-1, 9 * LANE), ("gx", "gy"), split_axis=0, concat_axis=0, tiled=True
     ).reshape(-1, LANE)

time: 118 us -> 115 us (0.975)
  Pallas kernels: 51.2 us -> 39.1 us
  waiting for transfers between devices: 17.2 us -> 23.8 us
  starting transfers between devices: 22.7 us -> 25.7 us
    ppermute x5, waiting for transfers between devices: 4.52 us -> 16.9 us  [both_ways(): below = lax.ppermute(up, axis, [(i, (i + 1) % count) for i in range(count)])]
    all_to_all x1, waiting for transfers between devices: 9.46 us -> 0.01 us  [per_device(): lax.all_to_all(outgoing.reshape(-1, 8, LANE), ('gx', 'gy'), split_axis=0,...]
    pallas_call x2 -> x1, Pallas kernels: 21 us -> 16.5 us  [swept(): pl.pallas_call(sweep_kernel, name='sweeps', out_shape=(jax.ShapeDtypeStru...]
    ppermute x5, waiting for transfers between devices: 3.24 us -> 6.91 us  [both_ways(): lax.ppermute(down, axis, [((i + 1) % count, i) for i in range(count)])]
    ppermute x5, starting transfers between devices: 5.22 us -> 8.33 us  [both_ways(): below = lax.ppermute(up, axis, [(i, (i + 1) % count) for i in range(count)])]
    pallas_call x1, Pallas kernels: 7.69 us -> 5.04 us  [bring_home(): pl.pallas_call(home_kernel, name='bring_home', out_shape=jax.ShapeDtypeSt...]
    pallas_call x1, Pallas kernels: 4.82 us -> 3.22 us  [send_tables(): pl.pallas_call(send_kernel, name='send_tables', out_shape=jax.ShapeDtypeS...]
    pallas_call x2, Pallas kernels: 1.28 us -> 0.06 us  [pack_y(): pl.pallas_call(pack_y_kernel, name='pack_y', out_shape=(out, out), in_spe...]
  transfers between devices with their start and end apart: 11 -> 11, of which waited for: 7 -> 8; matrix products, arithmetic and copies ran while one was open for 1% -> 0% of each run, Pallas kernels for 13% -> 0%
where the time goes in v3:
time: 115 us
  Pallas kernels  39.1 us (34%)
  starting transfers between devices  25.7 us (22%)
  waiting for transfers between devices  23.8 us (21%)
  blocking collectives  22.4 us (19%)
  local copies, waits for them, and re-layouts  3.12 us (3%)
    all_to_all x1, blocking collectives, per_device(): lax.all_to_all(samples.reshape(-1, 9 * LANE), ('gx', 'gy'), split_axis=0,...  22.4 us
    ppermute x5, waiting for transfers between devices, both_ways(): below = lax.ppermute(up, axis, [(i, (i + 1) % count) for i in range(count)])  16.9 us
    pallas_call x1, Pallas kernels, swept(): pl.pallas_call(sweep_kernel, name='sweeps', out_shape=(jax.ShapeDtypeStru...  16.5 us
    pallas_call x1, Pallas kernels, cell_fields(): pl.pallas_call(cell_kernel, name='cell_fields', out_shape=(out, side, sid...  13.3 us
    all_to_all x1, starting transfers between devices, per_device(): lax.all_to_all(outgoing.reshape(-1, 8, LANE), ('gx', 'gy'), split_axis=0,...  13.1 us
    ppermute x5, starting transfers between devices, both_ways(): below = lax.ppermute(up, axis, [(i, (i + 1) % count) for i in range(count)])  8.33 us
    ppermute x5, waiting for transfers between devices, both_ways(): lax.ppermute(down, axis, [((i + 1) % count, i) for i in range(count)])  6.91 us
    pallas_call x1, Pallas kernels, bring_home(): pl.pallas_call(home_kernel, name='bring_home', out_shape=jax.ShapeDtypeSt...  5.04 us
  transfers between devices with their start and end apart: 11, of which 8 were waited for; matrix products, arithmetic and copies ran while one was open for 0% of the time, Pallas kernels for 0%

profile of v3, /device:TPU:1, one launch (start us, length us, event | category | flops | bytes accessed | tf_op | source)
XLA Modules:
  0.0 115.0 jit_solution(10421715151994071040)
XLA Ops:
  0.6 0.1 pad_maximum_fusion.origin_ref
  0.7 0.0 copy-start.4
  0.7 1.0 copy-done.4
  1.8 0.0 copy-start.7
  1.8 0.8 copy-done.7
  2.5 0.0 copy-start.9
  2.5 3.2 %send_tables.1 = f32[512,128]{1,0:T(8,128)} custom-call(f32[10,8192]{1,0:T(8,128)S(1)} %copy-done.4, s32[64,128]{1,0:T(8,128)S(1)} %copy-done.7, f32[3]{0:T(128)S(1)} %pad_maximum_fusion.origin_ref), custom_call_target="tpu_custom_call" | custom-call | flops 2199023255552 | bytes 1048576 | tf_op jit(solution)/shard_map/send_tables/pallas_call | solution.py:127
  5.7 0.0 copy-start.5
  5.7 13.1 %all-to-all-start = ((f32[64,8,128]{2,1,0:T(8,128)}), f32[64,8,128]{2,1,0:T(8,128)S(1)}, u32[]{:S(2)}, u32[]{:S(2)}) async-start(f32[64,8,128]{2,1,0:T(8,128)} %bitcast.1), calls=%async_computation | async-start | bytes 524288 | tf_op jit(solution)/shard_map/all_to_all | solution.py:465
  18.9 0.0 copy-done.9
  18.9 1.5 %collective-permute-start = (f32[3,4,32,128]{3,2,1,0:T(8,128)S(1)}, f32[3,4,32,128]{3,2,1,0:T(8,128)S(1)}, u32[]{:S(2)}, u32[]{:S(2)}) collective-permute-start(f32[3,4,32,128]{3,2,1,0:T(8,128)S(1)} %get-tuple-element.33.high_ref.refs_1_), channel_id=1, source_target_pairs={{0,32},{32,64},{64,96},{96,128},{128,160},{160,192},{192,224},{224... | collective-permute-start | bytes 589832 | tf_op jit(solution)/shard_map/ppermute | solution.py:453
  20.4 1.6 %collective-permute-start.1 = (f32[3,4,32,128]{3,2,1,0:T(8,128)S(1)}, f32[3,4,32,128]{3,2,1,0:T(8,128)S(1)}, u32[]{:S(2)}, u32[]{:S(2)}) collective-permute-start(f32[3,4,32,128]{3,2,1,0:T(8,128)S(1)} %get-tuple-element.34.low_ref.refs_0_), channel_id=1, source_target_pairs={{32,0},{64,32},{96,64},{128,96},{160,128},{192,160},{224,192},{0,2... | collective-permute-start | bytes 589832 | tf_op jit(solution)/shard_map/ppermute | solution.py:452
  21.9 10.2 %collective-permute-done.below_ref.refs_2_ = f32[3,4,32,128]{3,2,1,0:T(8,128)S(1)} collective-permute-done((f32[3,4,32,128]{3,2,1,0:T(8,128)S(1)}, f32[3,4,32,128]{3,2,1,0:T(8,128)S(1)}, u32[]{:S(2)}, u32[]{:S(2)}) %collective-permute-start) | collective-permute-done | bytes 196640 | tf_op jit(solution)/shard_map/ppermute | solution.py:453
  32.2 0.0 collective-permute-done.1.above_ref.refs_3_
  32.2 2.0 %collective-permute-start.2 = (f32[192,128]{1,0:T(8,128)S(1)}, f32[192,128]{1,0:T(8,128)S(1)}, u32[]{:S(2)}, u32[]{:S(2)}) collective-permute-start(f32[192,128]{1,0:T(8,128)S(1)} %get-tuple-element.18), channel_id=1, source_target_pairs={{0,4},{4,8},{8,12},{12,16},{16,20},{20,24},{24,28},{28,0},{1,5},{5... | collective-permute-start | bytes 294920 | tf_op jit(solution)/shard_map/ppermute | solution.py:453
  34.2 0.0 collective-permute-start.3
  34.2 0.1 pad_maximum_fusion.1.origin_ref
  34.2 1.6 %collective-permute-done.2.refs_4_ = f32[192,128]{1,0:T(8,128)S(1)} collective-permute-done((f32[192,128]{1,0:T(8,128)S(1)}, f32[192,128]{1,0:T(8,128)S(1)}, u32[]{:S(2)}, u32[]{:S(2)}) %collective-permute-start.2) | collective-permute-done | bytes 98336 | tf_op jit(solution)/shard_map/ppermute | solution.py:453
  35.8 0.0 copy-start
  35.8 0.6 copy-done
  36.4 1.8 %collective-permute-done.3.refs_5_ = f32[192,128]{1,0:T(8,128)S(1)} collective-permute-done((f32[192,128]{1,0:T(8,128)S(1)}, f32[192,128]{1,0:T(8,128)S(1)}, u32[]{:S(2)}, u32[]{:S(2)}) %collective-permute-start.3) | collective-permute-done | bytes 98336 | tf_op jit(solution)/shard_map/ppermute | solution.py:452
  38.2 0.0 copy-start.2
  38.2 0.6 copy-done.2
  38.8 0.0 all-to-all-done
  38.8 0.0 copy-done.5
  38.8 0.0 copy-start.1
  38.8 0.0 copy-start.3
  38.9 13.3 %cell_fields.1 = (f32[8,32,128]{2,1,0:T(8,128)}, f32[2,4,32,128]{3,2,1,0:T(8,128)S(1)}, f32[2,4,32,128]{3,2,1,0:T(8,128)S(1)}) custom-call(f32[512,128]{1,0:T(8,128)S(1)} %bitcast.9, s32[8,32,128]{2,1,0:T(8,128)S(1)} %copy-done.5, f32[3]{0:T(128)S(1)} %pad_maximum_fusion.1.origin_ref), custom_call_target="tpu_custom_call" | custom-call | flops 6597069766656 | bytes 1048576 | tf_op jit(solution)/shard_map/cell_fields/pallas_call | solution.py:183
  52.1 0.0 copy-start.6
  52.1 1.1 collective-permute-start.5
  53.2 0.3 collective-permute-start.4
  53.6 2.8 %collective-permute-done.5.above_ref.refs_9_ = f32[2,4,32,128]{3,2,1,0:T(8,128)S(1)} collective-permute-done((f32[2,4,32,128]{3,2,1,0:T(8,128)S(1)}, f32[2,4,32,128]{3,2,1,0:T(8,128)S(1)}, u32[]{:S(2)}, u32[]{:S(2)}) %collective-permute-start.5) | collective-permute-done | bytes 131104 | tf_op jit(solution)/shard_map/ppermute | solution.py:452
  56.4 1.9 %collective-permute-done.4.below_ref.refs_8_ = f32[2,4,32,128]{3,2,1,0:T(8,128)S(1)} collective-permute-done((f32[2,4,32,128]{3,2,1,0:T(8,128)S(1)}, f32[2,4,32,128]{3,2,1,0:T(8,128)S(1)}, u32[]{:S(2)}, u32[]{:S(2)}) %collective-permute-start.4) | collective-permute-done | bytes 131104 | tf_op jit(solution)/shard_map/ppermute | solution.py:453
  58.3 3.2 %collective-permute-start.6 = (f32[128,128]{1,0:T(8,128)S(1)}, f32[128,128]{1,0:T(8,128)S(1)}, u32[]{:S(2)}, u32[]{:S(2)}) collective-permute-start(f32[128,128]{1,0:T(8,128)S(1)} %get-tuple-element.25), channel_id=1, source_target_pairs={{0,4},{4,8},{8,12},{12,16},{16,20},{20,24},{24,28},{28,0},{1,5},{5... | collective-permute-start | bytes 196616 | tf_op jit(solution)/shard_map/ppermute | solution.py:453
  61.5 0.0 collective-permute-start.7
  61.5 1.3 %collective-permute-done.6.refs_10_ = f32[128,128]{1,0:T(8,128)S(1)} collective-permute-done((f32[128,128]{1,0:T(8,128)S(1)}, f32[128,128]{1,0:T(8,128)S(1)}, u32[]{:S(2)}, u32[]{:S(2)}) %collective-permute-start.6) | collective-permute-done | bytes 65568 | tf_op jit(solution)/shard_map/ppermute | solution.py:453
  62.8 2.4 %collective-permute-done.7.refs_11_ = f32[128,128]{1,0:T(8,128)S(1)} collective-permute-done((f32[128,128]{1,0:T(8,128)S(1)}, f32[128,128]{1,0:T(8,128)S(1)}, u32[]{:S(2)}, u32[]{:S(2)}) %collective-permute-start.7) | collective-permute-done | bytes 65568 | tf_op jit(solution)/shard_map/ppermute | solution.py:452
  65.2 0.0 copy-done.1
  65.2 0.0 copy-done.3
  65.2 1.0 pack_z.1
  66.2 1.4 %collective-permute-start.8 = (f32[120,128]{1,0:T(8,128)S(1)}, f32[120,128]{1,0:T(8,128)S(1)}, u32[]{:S(2)}, u32[]{:S(2)}) collective-permute-start(f32[120,128]{1,0:T(8,128)S(1)} %get-tuple-element.28), channel_id=1, source_target_pairs={{0,1},{1,2},{2,3},{3,0},{4,5},{5,6},{6,7},{7,4},{8,9},{9,10},{10,1... | collective-permute-start | bytes 184328 | tf_op jit(solution)/shard_map/ppermute | solution.py:453
  67.5 1.5 %collective-permute-start.9 = (f32[120,128]{1,0:T(8,128)S(1)}, f32[120,128]{1,0:T(8,128)S(1)}, u32[]{:S(2)}, u32[]{:S(2)}) collective-permute-start(f32[120,128]{1,0:T(8,128)S(1)} %get-tuple-element.29), channel_id=1, source_target_pairs={{1,0},{2,1},{3,2},{0,3},{5,4},{6,5},{7,6},{4,7},{9,8},{10,9},{11,1... | collective-permute-start | bytes 184328 | tf_op jit(solution)/shard_map/ppermute | solution.py:452
  69.1 1.9 %collective-permute-done.8.before_ref = f32[120,128]{1,0:T(8,128)S(1)} collective-permute-done((f32[120,128]{1,0:T(8,128)S(1)}, f32[120,128]{1,0:T(8,128)S(1)}, u32[]{:S(2)}, u32[]{:S(2)}) %collective-permute-start.8) | collective-permute-done | bytes 61472 | tf_op jit(solution)/shard_map/ppermute | solution.py:453
  70.9 0.0 collective-permute-done.9.after_ref
  70.9 0.0 copy-done.6
  71.0 0.0 copy-start.8
  71.0 16.5 %sweeps.1 = (f32[3,8,32,128]{3,2,1,0:T(8,128)}, f32[576,128]{1,0:T(8,128)S(1)}) custom-call(f32[5,16,40,128]{3,2,1,0:T(8,128)S(1)} %get-tuple-element.27.wide_ref, f32[120,128]{1,0:T(8,128)S(1)} %collective-permute-done.8.before_ref, f32[120,128]{1,0:T(8,128)S(1)} %collective-permute-done.9.after_ref, s32[3,8192]{1,0:T(4,128)S(1)} %copy-done.6), custom_call_target="tpu_custom_call" | custom-call | flops 10995116277760 | bytes 1048576 | tf_op jit(solution)/shard_map/sweeps/pallas_call | solution.py:430
  87.5 22.4 %all_to_all.14 = f32[64,1,1152]{2,1,0:T(1,128)S(1)} all-to-all(f32[64,1,1152]{2,1,0:T(1,128)S(1)} %bitcast.7), channel_id=1, replica_groups=mesh['gx'=8,'gy'=8,'gz'=4] {'gx','gy'}, dimensions={0} | all-to-all | bytes 589824 | tf_op jit(solution)/shard_map/all_to_all | solution.py:482
  109.9 0.0 copy-done.8
  109.9 5.0 %bring_home.1 = f32[9,8192]{1,0:T(8,128)} custom-call(f32[576,128]{1,0:T(8,128)S(1)} %bitcast.8, s32[64,128]{1,0:T(8,128)S(1)} %copy-done.8), custom_call_target="tpu_custom_call" | custom-call | flops 2199023255552 | bytes 1048576 | tf_op jit(solution)/shard_map/bring_home/pallas_call | solution.py:254
  (3 shorter events, 0.1 us)
Async XLA Ops:
  0.7 1.0 copy-start.4
  1.8 0.8 copy-start.7
  2.5 16.3 %copy-start.9 = (f32[3,8,32,128]{3,2,1,0:T(8,128)S(1)}, f32[3,8,32,128]{3,2,1,0:T(8,128)}, u32[]{:S(2)}) copy-start(f32[3,8,32,128]{3,2,1,0:T(8,128)} %param.9) | copy-start | bytes 1179652
  5.7 33.1 %copy-start.5 = (s32[8,32,128]{2,1,0:T(8,128)S(1)}, s32[8,32,128]{2,1,0:T(8,128)}, u32[]{:S(2)}) copy-start(s32[8,32,128]{2,1,0:T(8,128)} %near_ref.1) | copy-start | bytes 393220
  5.7 33.1 %all-to-all-start = ((f32[64,8,128]{2,1,0:T(8,128)}), f32[64,8,128]{2,1,0:T(8,128)S(1)}, u32[]{:S(2)}, u32[]{:S(2)}) async-start(f32[64,8,128]{2,1,0:T(8,128)} %bitcast.1), calls=%async_computation | async-start | bytes 524288 | tf_op jit(solution)/shard_map/all_to_all | solution.py:465
  18.9 13.3 %collective-permute-start = (f32[3,4,32,128]{3,2,1,0:T(8,128)S(1)}, f32[3,4,32,128]{3,2,1,0:T(8,128)S(1)}, u32[]{:S(2)}, u32[]{:S(2)}) collective-permute-start(f32[3,4,32,128]{3,2,1,0:T(8,128)S(1)} %get-tuple-element.33.high_ref.refs_1_), channel_id=1, source_target_pairs={{0,32},{32,64},{64,96},{96,128},{128,160},{160,192},{192,224},{224... | collective-permute-start | bytes 589832 | tf_op jit(solution)/shard_map/ppermute | solution.py:453
  20.4 11.8 %collective-permute-start.1 = (f32[3,4,32,128]{3,2,1,0:T(8,128)S(1)}, f32[3,4,32,128]{3,2,1,0:T(8,128)S(1)}, u32[]{:S(2)}, u32[]{:S(2)}) collective-permute-start(f32[3,4,32,128]{3,2,1,0:T(8,128)S(1)} %get-tuple-element.34.low_ref.refs_0_), channel_id=1, source_target_pairs={{32,0},{64,32},{96,64},{128,96},{160,128},{192,160},{224,192},{0,2... | collective-permute-start | bytes 589832 | tf_op jit(solution)/shard_map/ppermute | solution.py:452
  32.2 3.6 %collective-permute-start.2 = (f32[192,128]{1,0:T(8,128)S(1)}, f32[192,128]{1,0:T(8,128)S(1)}, u32[]{:S(2)}, u32[]{:S(2)}) collective-permute-start(f32[192,128]{1,0:T(8,128)S(1)} %get-tuple-element.18), channel_id=1, source_target_pairs={{0,4},{4,8},{8,12},{12,16},{16,20},{20,24},{24,28},{28,0},{1,5},{5... | collective-permute-start | bytes 294920 | tf_op jit(solution)/shard_map/ppermute | solution.py:453
  34.2 4.0 %collective-permute-start.3 = (f32[192,128]{1,0:T(8,128)S(1)}, f32[192,128]{1,0:T(8,128)S(1)}, u32[]{:S(2)}, u32[]{:S(2)}) collective-permute-start(f32[192,128]{1,0:T(8,128)S(1)} %get-tuple-element.19), channel_id=1, source_target_pairs={{4,0},{8,4},{12,8},{16,12},{20,16},{24,20},{28,24},{0,28},{5,1},{9... | collective-permute-start | bytes 294920 | tf_op jit(solution)/shard_map/ppermute | solution.py:452
  35.8 0.6 copy-start
  38.2 0.6 copy-start.2
  38.8 26.3 %copy-start.1 = (f32[192,128]{1,0:T(8,128)S(1)}, f32[192,128]{1,0:T(8,128)}, u32[]{:S(2)}) copy-start(f32[192,128]{1,0:T(8,128)} %copy-done) | copy-start | bytes 294916
  38.8 26.3 %copy-start.3 = (f32[192,128]{1,0:T(8,128)S(1)}, f32[192,128]{1,0:T(8,128)}, u32[]{:S(2)}) copy-start(f32[192,128]{1,0:T(8,128)} %copy-done.2) | copy-start | bytes 294916
  52.1 18.8 %copy-start.6 = (s32[3,8192]{1,0:T(4,128)S(1)}, s32[3,8192]{1,0:T(4,128)}, u32[]{:S(2)}) copy-start(s32[3,8192]{1,0:T(4,128)} %cell_ref.1) | copy-start | bytes 294916
  52.1 4.2 %collective-permute-start.5 = (f32[2,4,32,128]{3,2,1,0:T(8,128)S(1)}, f32[2,4,32,128]{3,2,1,0:T(8,128)S(1)}, u32[]{:S(2)}, u32[]{:S(2)}) collective-permute-start(f32[2,4,32,128]{3,2,1,0:T(8,128)S(1)} %get-tuple-element.23.low_ref.refs_6_), channel_id=1, source_target_pairs={{32,0},{64,32},{96,64},{128,96},{160,128},{192,160},{224,192},{0,2... | collective-permute-start | bytes 393224 | tf_op jit(solution)/shard_map/ppermute | solution.py:452
  53.2 5.0 %collective-permute-start.4 = (f32[2,4,32,128]{3,2,1,0:T(8,128)S(1)}, f32[2,4,32,128]{3,2,1,0:T(8,128)S(1)}, u32[]{:S(2)}, u32[]{:S(2)}) collective-permute-start(f32[2,4,32,128]{3,2,1,0:T(8,128)S(1)} %get-tuple-element.24.high_ref.refs_7_), channel_id=1, source_target_pairs={{0,32},{32,64},{64,96},{96,128},{128,160},{160,192},{192,224},{224... | collective-permute-start | bytes 393224 | tf_op jit(solution)/shard_map/ppermute | solution.py:453
  58.3 4.5 %collective-permute-start.6 = (f32[128,128]{1,0:T(8,128)S(1)}, f32[128,128]{1,0:T(8,128)S(1)}, u32[]{:S(2)}, u32[]{:S(2)}) collective-permute-start(f32[128,128]{1,0:T(8,128)S(1)} %get-tuple-element.25), channel_id=1, source_target_pairs={{0,4},{4,8},{8,12},{12,16},{16,20},{20,24},{24,28},{28,0},{1,5},{5... | collective-permute-start | bytes 196616 | tf_op jit(solution)/shard_map/ppermute | solution.py:453
  61.5 3.7 %collective-permute-start.7 = (f32[128,128]{1,0:T(8,128)S(1)}, f32[128,128]{1,0:T(8,128)S(1)}, u32[]{:S(2)}, u32[]{:S(2)}) collective-permute-start(f32[128,128]{1,0:T(8,128)S(1)} %get-tuple-element.26), channel_id=1, source_target_pairs={{4,0},{8,4},{12,8},{16,12},{20,16},{24,20},{28,24},{0,28},{5,1},{9... | collective-permute-start | bytes 196616 | tf_op jit(solution)/shard_map/ppermute | solution.py:452
  66.2 4.8 %collective-permute-start.8 = (f32[120,128]{1,0:T(8,128)S(1)}, f32[120,128]{1,0:T(8,128)S(1)}, u32[]{:S(2)}, u32[]{:S(2)}) collective-permute-start(f32[120,128]{1,0:T(8,128)S(1)} %get-tuple-element.28), channel_id=1, source_target_pairs={{0,1},{1,2},{2,3},{3,0},{4,5},{5,6},{6,7},{7,4},{8,9},{9,10},{10,1... | collective-permute-start | bytes 184328 | tf_op jit(solution)/shard_map/ppermute | solution.py:453
  67.5 3.4 %collective-permute-start.9 = (f32[120,128]{1,0:T(8,128)S(1)}, f32[120,128]{1,0:T(8,128)S(1)}, u32[]{:S(2)}, u32[]{:S(2)}) collective-permute-start(f32[120,128]{1,0:T(8,128)S(1)} %get-tuple-element.29), channel_id=1, source_target_pairs={{1,0},{2,1},{3,2},{0,3},{5,4},{6,5},{7,6},{4,7},{9,8},{10,9},{11,1... | collective-permute-start | bytes 184328 | tf_op jit(solution)/shard_map/ppermute | solution.py:452
  71.0 39.0 %copy-start.8 = (s32[64,128]{1,0:T(8,128)S(1)}, s32[64,128]{1,0:T(8,128)}, u32[]{:S(2)}) copy-start(s32[64,128]{1,0:T(8,128)} %send_ref.3) | copy-start | bytes 98308

commit v4 on v3

--- a/solution.py
+++ b/solution.py
@@ -153,27 +153,21 @@
     at_z = lax.broadcasted_iota(I32, (8, LANE), 1).astype(F32) + (0.5 - mid_z)
     tiles = size_y // 8
 
-    @pl.loop(0, size_x * tiles, unroll=8)
-    def _(step):
-        x = lax.shift_right_logical(step, tiles.bit_length() - 1)
-        y = pl.multiple_of((step & (tiles - 1)) * 8, 8)
-        index = near_ref[x, pl.ds(y, 8), :]
-        found = look_up(table_ref, (2, 2, 2, 3, 2), half, [index[s:s + 1] for s in range(8)])
-        at_x = x.astype(F32) + (0.5 - mid_x)
-        at_y = sub + (y.astype(F32) + (0.5 - mid_y))
-        distance = found[0] * at_x + found[1] * at_y + found[2] * at_z - found[3]
-        indicator = 0.5 * (1.0 + jnp.tanh(distance / smear_width))
-        ind_ref[x, pl.ds(y, 8), :] = indicator
-
-        @pl.when(x < WIDE)
-        def _():
-            low_ref[0, x, pl.ds(y, 8), :] = indicator
-            low_ref[1, x, pl.ds(y, 8), :] = found[4]
-
-        @pl.when(x >= WIDE)
-        def _():
-            high_ref[0, x - WIDE, pl.ds(y, 8), :] = indicator
-            high_ref[1, x - WIDE, pl.ds(y, 8), :] = found[4]
+    for side_ref, start in ((low_ref, 0), (high_ref, WIDE)):
+
+        @pl.loop(0, WIDE * tiles, unroll=8)
+        def _(step):
+            x = lax.shift_right_logical(step, tiles.bit_length() - 1)
+            y = pl.multiple_of((step & (tiles - 1)) * 8, 8)
+            index = near_ref[start + x, pl.ds(y, 8), :]
+            found = look_up(table_ref, (2, 2, 2, 3, 2), half, [index[s:s + 1] for s in range(8)])
+            at_x = x.astype(F32) + (start + 0.5 - mid_x)
+            at_y = sub + (y.astype(F32) + (0.5 - mid_y))
+            distance = found[0] * at_x + found[1] * at_y + found[2] * at_z - found[3]
+            indicator = 0.5 * (1.0 + jnp.tanh(distance / smear_width))
+            ind_ref[start + x, pl.ds(y, 8), :] = indicator
+            side_ref[0, x, pl.ds(y, 8), :] = indicator
+            side_ref[1, x, pl.ds(y, 8), :] = found[4]
 
 
 def cell_fields(tab, near, origin):
@@ -467,7 +461,6 @@
     ).reshape(-1, LANE)
     vel_down, vel_up = pack_y(vel_low, vel_high, vel_below, vel_above)
     vel_under, vel_over = both_ways(vel_down, vel_up, "gy")
-    arrived, vel_under, vel_over = lax.optimization_barrier((arrived, vel_under, vel_over))
     own_x = (lax.axis_index("gx") * size_x + size_x // 2).astype(F32) - mid_x
     own_y = (lax.axis_index("gy") * size_y + size_y // 2).astype(F32) - mid_y
     indicator, low, high = cell_fields(arrived, near_index, jnp.stack([own_x, own_y, jnp.float32(0.0)]))

time: 115 us -> 103 us (0.90)
  waiting for transfers between devices: 23.8 us -> 17.2 us
  starting transfers between devices: 25.7 us -> 22.7 us
  Pallas kernels: 39.1 us -> 36.4 us
    ppermute x5, waiting for transfers between devices: 16.9 us -> 4.53 us  [both_ways(): below = lax.ppermute(up, axis, [(i, (i + 1) % count) for i in range(count)])]
    all_to_all x1, waiting for transfers between devices: 0.01 us -> 9.46 us  [per_device(): lax.all_to_all(outgoing.reshape(-1, 8, LANE), ('gx', 'gy'), split_axis=0,...]
    pallas_call x1, Pallas kernels: 13.3 us -> 8.18 us  [cell_fields(): pl.pallas_call(cell_kernel, name='cell_fields', out_shape=(out, side, sid...]
    ppermute x5, waiting for transfers between devices: 6.91 us -> 3.24 us  [both_ways(): lax.ppermute(down, axis, [((i + 1) % count, i) for i in range(count)])]
    ppermute x5, starting transfers between devices: 8.33 us -> 5.22 us  [both_ways(): below = lax.ppermute(up, axis, [(i, (i + 1) % count) for i in range(count)])]
    unnamed x20 -> x12, local copies, waits for them, and re-layouts: 3.09 us -> 1.82 us
    pallas_call x2, Pallas kernels: 0.06 us -> 1.28 us  [pack_y(): pl.pallas_call(pack_y_kernel, name='pack_y', out_shape=(out, out), in_spe...]
    pallas_call x1, Pallas kernels: 0.97 us -> 2.19 us  [pack_z(): pl.pallas_call(pack_z_kernel, name='pack_z', out_shape=(jax.ShapeDtypeStr...]
  transfers between devices with their start and end apart: 11 -> 11, of which waited for: 8 -> 7; matrix products, arithmetic and copies ran while one was open for 0% -> 1% of each run, Pallas kernels for 0% -> 9%
where the time goes in v4:
time: 103 us; the launch traced here: 102 us
  Pallas kernels  36.4 us (35%)
  starting transfers between devices  22.7 us (22%)
  blocking collectives  22.5 us (22%)
  waiting for transfers between devices  17.2 us (17%)
  local copies, waits for them, and re-layouts  2.57 us (2%)
    all_to_all x1, blocking collectives, per_device(): lax.all_to_all(samples.reshape(-1, 9 * LANE), ('gx', 'gy'), split_axis=0,...  22.5 us
    pallas_call x1, Pallas kernels, swept(): pl.pallas_call(sweep_kernel, name='sweeps', out_shape=(jax.ShapeDtypeStru...  16.5 us
    all_to_all x1, starting transfers between devices, per_device(): lax.all_to_all(outgoing.reshape(-1, 8, LANE), ('gx', 'gy'), split_axis=0,...  13 us
    all_to_all x1, waiting for transfers between devices, per_device(): lax.all_to_all(outgoing.reshape(-1, 8, LANE), ('gx', 'gy'), split_axis=0,...  9.46 us
    pallas_call x1, Pallas kernels, cell_fields(): pl.pallas_call(cell_kernel, name='cell_fields', out_shape=(out, side, sid...  8.18 us
    ppermute x5, starting transfers between devices, both_ways(): below = lax.ppermute(up, axis, [(i, (i + 1) % count) for i in range(count)])  5.22 us
    pallas_call x1, Pallas kernels, bring_home(): pl.pallas_call(home_kernel, name='bring_home', out_shape=jax.ShapeDtypeSt...  5.04 us
    ppermute x5, starting transfers between devices, both_ways(): lax.ppermute(down, axis, [((i + 1) % count, i) for i in range(count)])  4.54 us
  transfers between devices with their start and end apart: 11, of which 7 were waited for; matrix products, arithmetic and copies ran while one was open for 1% of the time, Pallas kernels for 9%

profile of v4, /device:TPU:1, one launch (start us, length us, event | category | flops | bytes accessed | tf_op | source)
XLA Modules:
  0.0 102.4 jit_solution(1045749063702420937)
XLA Ops:
  0.6 0.1 pad_maximum_fusion.origin_ref
  0.7 0.0 copy-start
  0.7 1.0 %copy-done = f32[10,8192]{1,0:T(8,128)S(1)} copy-done((f32[10,8192]{1,0:T(8,128)S(1)}, f32[10,8192]{1,0:T(8,128)}, u32[]{:S(2)}) %copy-start) | copy-done | bytes 327704
  1.8 0.0 copy-start.3
  1.8 0.8 copy-done.3
  2.5 0.0 copy-start.5
  2.5 0.0 copy-start.1
  2.5 3.2 %send_tables.1 = f32[512,128]{1,0:T(8,128)} custom-call(f32[10,8192]{1,0:T(8,128)S(1)} %copy-done, s32[64,128]{1,0:T(8,128)S(1)} %copy-done.3, f32[3]{0:T(128)S(1)} %pad_maximum_fusion.origin_ref), custom_call_target="tpu_custom_call" | custom-call | flops 2199023255552 | bytes 1048576 | tf_op jit(solution)/shard_map/send_tables/pallas_call | solution.py:127
  5.7 13.0 %all-to-all-start = ((f32[64,8,128]{2,1,0:T(8,128)}), f32[64,8,128]{2,1,0:T(8,128)S(1)}, u32[]{:S(2)}, u32[]{:S(2)}) async-start(f32[64,8,128]{2,1,0:T(8,128)} %bitcast.1), calls=%async_computation | async-start | bytes 524288 | tf_op jit(solution)/shard_map/all_to_all | solution.py:459
  18.7 0.0 copy-done.5
  18.7 0.8 fusion
  19.5 1.4 %collective-permute-start = (f32[3,4,32,128]{3,2,1,0:T(8,128)}, f32[3,4,32,128]{3,2,1,0:T(8,128)}, u32[]{:S(2)}, u32[]{:S(2)}) collective-permute-start(f32[3,4,32,128]{3,2,1,0:T(8,128)} %get-tuple-element.27.high_ref.refs_1_), channel_id=1, source_target_pairs={{0,32},{32,64},{64,96},{96,128},{128,160},{160,192},{192,224},{224... | collective-permute-start | bytes 589832 | tf_op jit(solution)/shard_map/ppermute | solution.py:447
  20.9 1.5 %collective-permute-start.1 = (f32[3,4,32,128]{3,2,1,0:T(8,128)}, f32[3,4,32,128]{3,2,1,0:T(8,128)}, u32[]{:S(2)}, u32[]{:S(2)}) collective-permute-start(f32[3,4,32,128]{3,2,1,0:T(8,128)} %get-tuple-element.28.low_ref.refs_0_), channel_id=1, source_target_pairs={{32,0},{64,32},{96,64},{128,96},{160,128},{192,160},{224,192},{0,2... | collective-permute-start | bytes 589832 | tf_op jit(solution)/shard_map/ppermute | solution.py:446
  22.4 0.1 pad_maximum_fusion.1.origin_ref
  22.4 9.5 %all-to-all-done = f32[64,8,128]{2,1,0:T(8,128)S(1)} async-done(((f32[64,8,128]{2,1,0:T(8,128)}), f32[64,8,128]{2,1,0:T(8,128)S(1)}, u32[]{:S(2)}, u32[]{:S(2)}) %all-to-all-start) | async-done | bytes 262176 | tf_op jit(solution)/shard_map/all_to_all | solution.py:459
  31.9 0.0 copy-done.1
  31.9 8.2 %cell_fields.1 = (f32[8,32,128]{2,1,0:T(8,128)}, f32[2,4,32,128]{3,2,1,0:T(8,128)S(1)}, f32[2,4,32,128]{3,2,1,0:T(8,128)S(1)}) custom-call(f32[512,128]{1,0:T(8,128)S(1)} %bitcast.9, s32[8,32,128]{2,1,0:T(8,128)S(1)} %copy-done.1, f32[3]{0:T(128)S(1)} %pad_maximum_fusion.1.origin_ref), custom_call_target="tpu_custom_call" | custom-call | flops 6597069766656 | bytes 1048576 | tf_op jit(solution)/shard_map/cell_fields/pallas_call | solution.py:177
  40.1 0.0 copy-start.2
  40.1 1.1 %collective-permute-start.5 = (f32[2,4,32,128]{3,2,1,0:T(8,128)S(1)}, f32[2,4,32,128]{3,2,1,0:T(8,128)S(1)}, u32[]{:S(2)}, u32[]{:S(2)}) collective-permute-start(f32[2,4,32,128]{3,2,1,0:T(8,128)S(1)} %get-tuple-element.17.low_ref.refs_6_), channel_id=1, source_target_pairs={{32,0},{64,32},{96,64},{128,96},{160,128},{192,160},{224,192},{0,2... | collective-permute-start | bytes 393224 | tf_op jit(solution)/shard_map/ppermute | solution.py:446
  41.2 0.4 collective-permute-start.4
  41.5 0.0 collective-permute-done.below_ref.refs_2_
  41.5 0.0 collective-permute-done.1.above_ref.refs_3_
  41.5 1.3 %pack_y.2 = (f32[192,128]{1,0:T(8,128)S(1)}, f32[192,128]{1,0:T(8,128)S(1)}) custom-call(f32[3,4,32,128]{3,2,1,0:T(8,128)} %get-tuple-element.28.low_ref.refs_0_, f32[3,4,32,128]{3,2,1,0:T(8,128)} %get-tuple-element.27.high_ref.refs_1_, f32[3,4,32,128]{3,2,1,0:T(8,128)} %collective-permute-done.below_ref.refs_2_, ...), custom_call_target="tpu_custom_call" | custom-call | flops 1048576 | bytes 1048576 | tf_op jit(solution)/shard_map/pack_y/pallas_call | solution.py:278
  42.8 1.3 %collective-permute-start.2 = (f32[192,128]{1,0:T(8,128)S(1)}, f32[192,128]{1,0:T(8,128)S(1)}, u32[]{:S(2)}, u32[]{:S(2)}) collective-permute-start(f32[192,128]{1,0:T(8,128)S(1)} %get-tuple-element.15), channel_id=1, source_target_pairs={{0,4},{4,8},{8,12},{12,16},{16,20},{20,24},{24,28},{28,0},{1,5},{5... | collective-permute-start | bytes 294920 | tf_op jit(solution)/shard_map/ppermute | solution.py:447
  44.1 0.0 collective-permute-start.3
  44.1 0.8 collective-permute-done.5.above_ref.refs_9_
  44.9 2.2 %collective-permute-done.4.below_ref.refs_8_ = f32[2,4,32,128]{3,2,1,0:T(8,128)S(1)} collective-permute-done((f32[2,4,32,128]{3,2,1,0:T(8,128)S(1)}, f32[2,4,32,128]{3,2,1,0:T(8,128)S(1)}, u32[]{:S(2)}, u32[]{:S(2)}) %collective-permute-start.4) | collective-permute-done | bytes 131104 | tf_op jit(solution)/shard_map/ppermute | solution.py:447
  47.1 0.8 collective-permute-start.6
  47.9 0.5 collective-permute-start.7
  48.3 0.0 collective-permute-done.2.refs_4_
  48.4 0.1 collective-permute-done.3.refs_5_
  48.4 0.8 collective-permute-done.6.refs_10_
  49.2 2.4 %collective-permute-done.7.refs_11_ = f32[128,128]{1,0:T(8,128)S(1)} collective-permute-done((f32[128,128]{1,0:T(8,128)S(1)}, f32[128,128]{1,0:T(8,128)S(1)}, u32[]{:S(2)}, u32[]{:S(2)}) %collective-permute-start.7) | collective-permute-done | bytes 65568 | tf_op jit(solution)/shard_map/ppermute | solution.py:446
  51.6 2.2 %pack_z.1 = (f32[5,16,40,128]{3,2,1,0:T(8,128)S(1)}, f32[120,128]{1,0:T(8,128)S(1)}, f32[120,128]{1,0:T(8,128)S(1)}) custom-call(f32[3,4,32,128]{3,2,1,0:T(8,128)} %get-tuple-element.28.low_ref.refs_0_, f32[3,4,32,128]{3,2,1,0:T(8,128)} %get-tuple-element.27.high_ref.refs_1_, f32[3,4,32,128]{3,2,1,0:T(8,128)} %collective-permute-done.below_ref.refs_2_, ...), custom_call_target="tpu_custom_call" | custom-call | flops 1048576 | bytes 1048576 | tf_op jit(solution)/shard_map/pack_z/pallas_call | solution.py:330
  53.8 1.4 %collective-permute-start.8 = (f32[120,128]{1,0:T(8,128)S(1)}, f32[120,128]{1,0:T(8,128)S(1)}, u32[]{:S(2)}, u32[]{:S(2)}) collective-permute-start(f32[120,128]{1,0:T(8,128)S(1)} %get-tuple-element.22), channel_id=1, source_target_pairs={{0,1},{1,2},{2,3},{3,0},{4,5},{5,6},{6,7},{7,4},{8,9},{9,10},{10,1... | collective-permute-start | bytes 184328 | tf_op jit(solution)/shard_map/ppermute | solution.py:447
  55.2 1.5 %collective-permute-start.9 = (f32[120,128]{1,0:T(8,128)S(1)}, f32[120,128]{1,0:T(8,128)S(1)}, u32[]{:S(2)}, u32[]{:S(2)}) collective-permute-start(f32[120,128]{1,0:T(8,128)S(1)} %get-tuple-element.23), channel_id=1, source_target_pairs={{1,0},{2,1},{3,2},{0,3},{5,4},{6,5},{7,6},{4,7},{9,8},{10,9},{11,1... | collective-permute-start | bytes 184328 | tf_op jit(solution)/shard_map/ppermute | solution.py:446
  56.7 1.5 %collective-permute-done.8.before_ref = f32[120,128]{1,0:T(8,128)S(1)} collective-permute-done((f32[120,128]{1,0:T(8,128)S(1)}, f32[120,128]{1,0:T(8,128)S(1)}, u32[]{:S(2)}, u32[]{:S(2)}) %collective-permute-start.8) | collective-permute-done | bytes 61472 | tf_op jit(solution)/shard_map/ppermute | solution.py:447
  58.2 0.0 collective-permute-done.9.after_ref
  58.2 0.0 copy-done.2
  58.2 0.0 copy-start.4
  58.2 16.5 %sweeps.1 = (f32[3,8,32,128]{3,2,1,0:T(8,128)}, f32[576,128]{1,0:T(8,128)S(1)}) custom-call(f32[5,16,40,128]{3,2,1,0:T(8,128)S(1)} %get-tuple-element.21.wide_ref, f32[120,128]{1,0:T(8,128)S(1)} %collective-permute-done.8.before_ref, f32[120,128]{1,0:T(8,128)S(1)} %collective-permute-done.9.after_ref, s32[3,8192]{1,0:T(4,128)S(1)} %copy-done.2), custom_call_target="tpu_custom_call" | custom-call | flops 10995116277760 | bytes 1048576 | tf_op jit(solution)/shard_map/sweeps/pallas_call | solution.py:424
  74.8 22.5 %all_to_all.14 = f32[64,1,1152]{2,1,0:T(1,128)S(1)} all-to-all(f32[64,1,1152]{2,1,0:T(1,128)S(1)} %bitcast.7), channel_id=1, replica_groups=mesh['gx'=8,'gy'=8,'gz'=4] {'gx','gy'}, dimensions={0} | all-to-all | bytes 589824 | tf_op jit(solution)/shard_map/all_to_all | solution.py:475
  97.3 0.0 copy-done.4
  97.3 5.0 %bring_home.1 = f32[9,8192]{1,0:T(8,128)} custom-call(f32[576,128]{1,0:T(8,128)S(1)} %bitcast.8, s32[64,128]{1,0:T(8,128)S(1)} %copy-done.4), custom_call_target="tpu_custom_call" | custom-call | flops 2199023255552 | bytes 1048576 | tf_op jit(solution)/shard_map/bring_home/pallas_call | solution.py:248
  (1 shorter events, 0.0 us)
Async XLA Ops:
  0.7 1.0 %copy-start = (f32[10,8192]{1,0:T(8,128)S(1)}, f32[10,8192]{1,0:T(8,128)}, u32[]{:S(2)}) copy-start(f32[10,8192]{1,0:T(8,128)} %geom_ref.1) | copy-start | bytes 983044
  1.8 0.8 copy-start.3
  2.5 16.2 %copy-start.5 = (f32[3,8,32,128]{3,2,1,0:T(8,128)S(1)}, f32[3,8,32,128]{3,2,1,0:T(8,128)}, u32[]{:S(2)}) copy-start(f32[3,8,32,128]{3,2,1,0:T(8,128)} %param.9) | copy-start | bytes 1179652
  2.5 29.4 %copy-start.1 = (s32[8,32,128]{2,1,0:T(8,128)S(1)}, s32[8,32,128]{2,1,0:T(8,128)}, u32[]{:S(2)}) copy-start(s32[8,32,128]{2,1,0:T(8,128)} %near_ref.1) | copy-start | bytes 393220
  5.7 26.2 %all-to-all-start = ((f32[64,8,128]{2,1,0:T(8,128)}), f32[64,8,128]{2,1,0:T(8,128)S(1)}, u32[]{:S(2)}, u32[]{:S(2)}) async-start(f32[64,8,128]{2,1,0:T(8,128)} %bitcast.1), calls=%async_computation | async-start | bytes 524288 | tf_op jit(solution)/shard_map/all_to_all | solution.py:459
  19.5 22.0 %collective-permute-start = (f32[3,4,32,128]{3,2,1,0:T(8,128)}, f32[3,4,32,128]{3,2,1,0:T(8,128)}, u32[]{:S(2)}, u32[]{:S(2)}) collective-permute-start(f32[3,4,32,128]{3,2,1,0:T(8,128)} %get-tuple-element.27.high_ref.refs_1_), channel_id=1, source_target_pairs={{0,32},{32,64},{64,96},{96,128},{128,160},{160,192},{192,224},{224... | collective-permute-start | bytes 589832 | tf_op jit(solution)/shard_map/ppermute | solution.py:447
  20.9 20.7 %collective-permute-start.1 = (f32[3,4,32,128]{3,2,1,0:T(8,128)}, f32[3,4,32,128]{3,2,1,0:T(8,128)}, u32[]{:S(2)}, u32[]{:S(2)}) collective-permute-start(f32[3,4,32,128]{3,2,1,0:T(8,128)} %get-tuple-element.28.low_ref.refs_0_), channel_id=1, source_target_pairs={{32,0},{64,32},{96,64},{128,96},{160,128},{192,160},{224,192},{0,2... | collective-permute-start | bytes 589832 | tf_op jit(solution)/shard_map/ppermute | solution.py:446
  40.1 18.2 %copy-start.2 = (s32[3,8192]{1,0:T(4,128)S(1)}, s32[3,8192]{1,0:T(4,128)}, u32[]{:S(2)}) copy-start(s32[3,8192]{1,0:T(4,128)} %cell_ref.1) | copy-start | bytes 294916
  40.1 4.8 %collective-permute-start.5 = (f32[2,4,32,128]{3,2,1,0:T(8,128)S(1)}, f32[2,4,32,128]{3,2,1,0:T(8,128)S(1)}, u32[]{:S(2)}, u32[]{:S(2)}) collective-permute-start(f32[2,4,32,128]{3,2,1,0:T(8,128)S(1)} %get-tuple-element.17.low_ref.refs_6_), channel_id=1, source_target_pairs={{32,0},{64,32},{96,64},{128,96},{160,128},{192,160},{224,192},{0,2... | collective-permute-start | bytes 393224 | tf_op jit(solution)/shard_map/ppermute | solution.py:446
  41.2 5.9 %collective-permute-start.4 = (f32[2,4,32,128]{3,2,1,0:T(8,128)S(1)}, f32[2,4,32,128]{3,2,1,0:T(8,128)S(1)}, u32[]{:S(2)}, u32[]{:S(2)}) collective-permute-start(f32[2,4,32,128]{3,2,1,0:T(8,128)S(1)} %get-tuple-element.18.high_ref.refs_7_), channel_id=1, source_target_pairs={{0,32},{32,64},{64,96},{96,128},{128,160},{160,192},{192,224},{224... | collective-permute-start | bytes 393224 | tf_op jit(solution)/shard_map/ppermute | solution.py:447
  42.8 5.5 %collective-permute-start.2 = (f32[192,128]{1,0:T(8,128)S(1)}, f32[192,128]{1,0:T(8,128)S(1)}, u32[]{:S(2)}, u32[]{:S(2)}) collective-permute-start(f32[192,128]{1,0:T(8,128)S(1)} %get-tuple-element.15), channel_id=1, source_target_pairs={{0,4},{4,8},{8,12},{12,16},{16,20},{20,24},{24,28},{28,0},{1,5},{5... | collective-permute-start | bytes 294920 | tf_op jit(solution)/shard_map/ppermute | solution.py:447
  44.1 4.3 %collective-permute-start.3 = (f32[192,128]{1,0:T(8,128)S(1)}, f32[192,128]{1,0:T(8,128)S(1)}, u32[]{:S(2)}, u32[]{:S(2)}) collective-permute-start(f32[192,128]{1,0:T(8,128)S(1)} %get-tuple-element.16), channel_id=1, source_target_pairs={{4,0},{8,4},{12,8},{16,12},{20,16},{24,20},{28,24},{0,28},{5,1},{9... | collective-permute-start | bytes 294920 | tf_op jit(solution)/shard_map/ppermute | solution.py:446
  47.1 2.1 %collective-permute-start.6 = (f32[128,128]{1,0:T(8,128)S(1)}, f32[128,128]{1,0:T(8,128)S(1)}, u32[]{:S(2)}, u32[]{:S(2)}) collective-permute-start(f32[128,128]{1,0:T(8,128)S(1)} %get-tuple-element.19), channel_id=1, source_target_pairs={{0,4},{4,8},{8,12},{12,16},{16,20},{20,24},{24,28},{28,0},{1,5},{5... | collective-permute-start | bytes 196616 | tf_op jit(solution)/shard_map/ppermute | solution.py:447
  47.9 3.7 %collective-permute-start.7 = (f32[128,128]{1,0:T(8,128)S(1)}, f32[128,128]{1,0:T(8,128)S(1)}, u32[]{:S(2)}, u32[]{:S(2)}) collective-permute-start(f32[128,128]{1,0:T(8,128)S(1)} %get-tuple-element.20), channel_id=1, source_target_pairs={{4,0},{8,4},{12,8},{16,12},{20,16},{24,20},{28,24},{0,28},{5,1},{9... | collective-permute-start | bytes 196616 | tf_op jit(solution)/shard_map/ppermute | solution.py:446
  53.8 4.4 %collective-permute-start.8 = (f32[120,128]{1,0:T(8,128)S(1)}, f32[120,128]{1,0:T(8,128)S(1)}, u32[]{:S(2)}, u32[]{:S(2)}) collective-permute-start(f32[120,128]{1,0:T(8,128)S(1)} %get-tuple-element.22), channel_id=1, source_target_pairs={{0,1},{1,2},{2,3},{3,0},{4,5},{5,6},{6,7},{7,4},{8,9},{9,10},{10,1... | collective-permute-start | bytes 184328 | tf_op jit(solution)/shard_map/ppermute | solution.py:447
  55.2 3.1 %collective-permute-start.9 = (f32[120,128]{1,0:T(8,128)S(1)}, f32[120,128]{1,0:T(8,128)S(1)}, u32[]{:S(2)}, u32[]{:S(2)}) collective-permute-start(f32[120,128]{1,0:T(8,128)S(1)} %get-tuple-element.23), channel_id=1, source_target_pairs={{1,0},{2,1},{3,2},{0,3},{5,4},{6,5},{7,6},{4,7},{9,8},{10,9},{11,1... | collective-permute-start | bytes 184328 | tf_op jit(solution)/shard_map/ppermute | solution.py:446
  58.2 39.1 %copy-start.4 = (s32[64,128]{1,0:T(8,128)S(1)}, s32[64,128]{1,0:T(8,128)}, u32[]{:S(2)}) copy-start(s32[64,128]{1,0:T(8,128)} %send_ref.3) | copy-start | bytes 98308

commit v5 on v4

--- a/solution.py
+++ b/solution.py
@@ -118,7 +118,7 @@
         index = send_ref[pl.ds(tile * 8, 8), :]
         found = look_up(table_ref, (2, 2, 2, 3, 2), half, [index[s:s + 1] for s in range(8)])
         for q, value in enumerate(found):
-            out_ref[pl.ds(tile * 64 + q, 8, stride=8), :] = value
+            out_ref[pl.ds(tile * 40 + q, 8, stride=5), :] = value
 
 
 def send_tables(geom, send, origin):
@@ -127,7 +127,7 @@
     return pl.pallas_call(
         send_kernel,
         name="send_tables",
-        out_shape=jax.ShapeDtypeStruct((dests * 8, LANE), F32),
+        out_shape=jax.ShapeDtypeStruct((dests * 5, LANE), F32),
         in_specs=[VMEM, VMEM, pl.BlockSpec(memory_space=pltpu.SMEM)],
         out_specs=VMEM,
         scratch_shapes=[pltpu.VMEM((10 * rows, LANE), F32), pltpu.VMEM((11 * rows // 2, 2 * LANE), BF16)],
@@ -137,10 +137,10 @@
 
 
 def cell_kernel(tab_ref, near_ref, origin_ref, ind_ref, low_ref, high_ref, table_ref):
-    sources = tab_ref.shape[0] // 8
+    sources = tab_ref.shape[0] // 5
     half = sources // 2
     size_x, size_y, _ = near_ref.shape
-    value = [tab_ref[pl.ds(q, sources, stride=8), :] for q in range(5)]
+    value = [tab_ref[pl.ds(q, sources, stride=5), :] for q in range(5)]
     columns = []
     offset = value[3]
     for a in range(3):
@@ -171,7 +171,7 @@
 
 
 def cell_fields(tab, near, origin):
-    sources = tab.shape[0] // 8
+    sources = tab.shape[0] // 5
     out = jax.ShapeDtypeStruct(near.shape, F32)
     side = jax.ShapeDtypeStruct((2, WIDE) + near.shape[1:], F32)
     return pl.pallas_call(
@@ -457,7 +457,7 @@
     mid_x, mid_y = 0.5 * group_x * size_x, 0.5 * group_y * size_y
     outgoing = send_tables(tri_geom, send_index, jnp.stack([jnp.float32(mid_x), jnp.float32(mid_y), mid_z]))
     arrived = lax.all_to_all(
-        outgoing.reshape(-1, 8, LANE), ("gx", "gy"), split_axis=0, concat_axis=0, tiled=True
+        outgoing.reshape(-1, 5 * LANE), ("gx", "gy"), split_axis=0, concat_axis=0, tiled=True
     ).reshape(-1, LANE)
     vel_down, vel_up = pack_y(vel_low, vel_high, vel_below, vel_above)
     vel_under, vel_over = both_ways(vel_down, vel_up, "gy")

time: 103 us -> 101 us (0.981)
  waiting for transfers between devices: 17.2 us -> 15 us
    all_to_all x1, waiting for transfers between devices: 9.46 us -> 7.95 us  [per_device(): lax.all_to_all(outgoing.reshape(-1, 5 * LANE), ('gx', 'gy'), split_axis=0...]
where the time goes in v5:
time: 101 us; the launch traced here: 100 us
  Pallas kernels  36.4 us (36%)
  starting transfers between devices  23 us (23%)
  blocking collectives  22.5 us (22%)
  waiting for transfers between devices  15 us (15%)
  local copies, waits for them, and re-layouts  2.58 us (3%)
    all_to_all x1, blocking collectives, per_device(): lax.all_to_all(samples.reshape(-1, 9 * LANE), ('gx', 'gy'), split_axis=0,...  22.5 us
    pallas_call x1, Pallas kernels, swept(): pl.pallas_call(sweep_kernel, name='sweeps', out_shape=(jax.ShapeDtypeStru...  16.5 us
    all_to_all x1, starting transfers between devices, per_device(): lax.all_to_all(outgoing.reshape(-1, 5 * LANE), ('gx', 'gy'), split_axis=0...  13 us
    pallas_call x1, Pallas kernels, cell_fields(): pl.pallas_call(cell_kernel, name='cell_fields', out_shape=(out, side, sid...  8.17 us
    all_to_all x1, waiting for transfers between devices, per_device(): lax.all_to_all(outgoing.reshape(-1, 5 * LANE), ('gx', 'gy'), split_axis=0...  7.95 us
    ppermute x5, starting transfers between devices, both_ways(): below = lax.ppermute(up, axis, [(i, (i + 1) % count) for i in range(count)])  5.6 us
    pallas_call x1, Pallas kernels, bring_home(): pl.pallas_call(home_kernel, name='bring_home', out_shape=jax.ShapeDtypeSt...  5.04 us
    ppermute x5, starting transfers between devices, both_ways(): lax.ppermute(down, axis, [((i + 1) % count, i) for i in range(count)])  4.37 us
  transfers between devices with their start and end apart: 11, of which 7 were waited for; matrix products, arithmetic and copies ran while one was open for 1% of the time, Pallas kernels for 9%

profile of v5, /device:TPU:1, one launch (start us, length us, event | category | flops | bytes accessed | tf_op | source)
XLA Modules:
  0.0 100.3 jit_solution(1067229525053744145)
XLA Ops:
  0.6 0.1 pad_maximum_fusion.origin_ref
  0.7 0.0 copy-start
  0.7 1.0 %copy-done = f32[10,8192]{1,0:T(8,128)S(1)} copy-done((f32[10,8192]{1,0:T(8,128)S(1)}, f32[10,8192]{1,0:T(8,128)}, u32[]{:S(2)}) %copy-start) | copy-done | bytes 327704
  1.8 0.0 copy-start.3
  1.8 0.8 copy-done.3
  2.5 0.0 copy-start.5
  2.5 0.0 copy-start.1
  2.5 3.2 %send_tables.1 = f32[320,128]{1,0:T(8,128)} custom-call(f32[10,8192]{1,0:T(8,128)S(1)} %copy-done, s32[64,128]{1,0:T(8,128)S(1)} %copy-done.3, f32[3]{0:T(128)S(1)} %pad_maximum_fusion.origin_ref), custom_call_target="tpu_custom_call" | custom-call | flops 2199023255552 | bytes 1048576 | tf_op jit(solution)/shard_map/send_tables/pallas_call | solution.py:127
  5.7 13.0 %all-to-all-start = ((f32[64,1,640]{2,1,0:T(1,128)}), f32[64,1,640]{2,1,0:T(1,128)S(1)}, u32[]{:S(2)}, u32[]{:S(2)}) async-start(f32[64,1,640]{2,1,0:T(1,128)} %bitcast.1), calls=%async_computation | async-start | bytes 327680 | tf_op jit(solution)/shard_map/all_to_all | solution.py:459
  18.7 0.0 copy-done.5
  18.7 0.8 fusion
  19.5 1.4 %collective-permute-start = (f32[3,4,32,128]{3,2,1,0:T(8,128)}, f32[3,4,32,128]{3,2,1,0:T(8,128)}, u32[]{:S(2)}, u32[]{:S(2)}) collective-permute-start(f32[3,4,32,128]{3,2,1,0:T(8,128)} %get-tuple-element.27.high_ref.refs_1_), channel_id=1, source_target_pairs={{0,32},{32,64},{64,96},{96,128},{128,160},{160,192},{192,224},{224... | collective-permute-start | bytes 589832 | tf_op jit(solution)/shard_map/ppermute | solution.py:447
  20.9 1.5 %collective-permute-start.1 = (f32[3,4,32,128]{3,2,1,0:T(8,128)}, f32[3,4,32,128]{3,2,1,0:T(8,128)}, u32[]{:S(2)}, u32[]{:S(2)}) collective-permute-start(f32[3,4,32,128]{3,2,1,0:T(8,128)} %get-tuple-element.28.low_ref.refs_0_), channel_id=1, source_target_pairs={{32,0},{64,32},{96,64},{128,96},{160,128},{192,160},{224,192},{0,2... | collective-permute-start | bytes 589832 | tf_op jit(solution)/shard_map/ppermute | solution.py:446
  22.3 0.1 pad_maximum_fusion.1.origin_ref
  22.4 7.9 %all-to-all-done = f32[64,1,640]{2,1,0:T(1,128)S(1)} async-done(((f32[64,1,640]{2,1,0:T(1,128)}), f32[64,1,640]{2,1,0:T(1,128)S(1)}, u32[]{:S(2)}, u32[]{:S(2)}) %all-to-all-start) | async-done | bytes 163872 | tf_op jit(solution)/shard_map/all_to_all | solution.py:459
  30.4 0.0 copy-done.1
  30.4 8.2 %cell_fields.1 = (f32[8,32,128]{2,1,0:T(8,128)}, f32[2,4,32,128]{3,2,1,0:T(8,128)S(1)}, f32[2,4,32,128]{3,2,1,0:T(8,128)S(1)}) custom-call(f32[320,128]{1,0:T(8,128)S(1)} %bitcast.9, s32[8,32,128]{2,1,0:T(8,128)S(1)} %copy-done.1, f32[3]{0:T(128)S(1)} %pad_maximum_fusion.1.origin_ref), custom_call_target="tpu_custom_call" | custom-call | flops 6597069766656 | bytes 1048576 | tf_op jit(solution)/shard_map/cell_fields/pallas_call | solution.py:177
  38.5 0.0 copy-start.2
  38.5 0.8 collective-permute-start.5
  39.3 0.7 collective-permute-start.4
  40.0 0.0 collective-permute-done.below_ref.refs_2_
  40.0 0.0 collective-permute-done.1.above_ref.refs_3_
  40.0 1.3 %pack_y.2 = (f32[192,128]{1,0:T(8,128)S(1)}, f32[192,128]{1,0:T(8,128)S(1)}) custom-call(f32[3,4,32,128]{3,2,1,0:T(8,128)} %get-tuple-element.28.low_ref.refs_0_, f32[3,4,32,128]{3,2,1,0:T(8,128)} %get-tuple-element.27.high_ref.refs_1_, f32[3,4,32,128]{3,2,1,0:T(8,128)} %collective-permute-done.below_ref.refs_2_, ...), custom_call_target="tpu_custom_call" | custom-call | flops 1048576 | bytes 1048576 | tf_op jit(solution)/shard_map/pack_y/pallas_call | solution.py:278
  41.3 1.1 %collective-permute-start.2 = (f32[192,128]{1,0:T(8,128)S(1)}, f32[192,128]{1,0:T(8,128)S(1)}, u32[]{:S(2)}, u32[]{:S(2)}) collective-permute-start(f32[192,128]{1,0:T(8,128)S(1)} %get-tuple-element.15), channel_id=1, source_target_pairs={{0,4},{4,8},{8,12},{12,16},{16,20},{20,24},{24,28},{28,0},{1,5},{5... | collective-permute-start | bytes 294920 | tf_op jit(solution)/shard_map/ppermute | solution.py:447
  42.4 0.0 collective-permute-start.3
  42.4 0.8 collective-permute-done.5.above_ref.refs_9_
  43.2 1.7 %collective-permute-done.4.below_ref.refs_8_ = f32[2,4,32,128]{3,2,1,0:T(8,128)S(1)} collective-permute-done((f32[2,4,32,128]{3,2,1,0:T(8,128)S(1)}, f32[2,4,32,128]{3,2,1,0:T(8,128)S(1)}, u32[]{:S(2)}, u32[]{:S(2)}) %collective-permute-start.4) | collective-permute-done | bytes 131104 | tf_op jit(solution)/shard_map/ppermute | solution.py:447
  44.9 1.0 collective-permute-start.6
  45.9 0.6 collective-permute-start.7
  46.5 0.0 collective-permute-done.2.refs_4_
  46.5 0.3 collective-permute-done.3.refs_5_
  46.7 0.5 collective-permute-done.6.refs_10_
  47.2 2.4 %collective-permute-done.7.refs_11_ = f32[128,128]{1,0:T(8,128)S(1)} collective-permute-done((f32[128,128]{1,0:T(8,128)S(1)}, f32[128,128]{1,0:T(8,128)S(1)}, u32[]{:S(2)}, u32[]{:S(2)}) %collective-permute-start.7) | collective-permute-done | bytes 65568 | tf_op jit(solution)/shard_map/ppermute | solution.py:446
  49.6 2.2 %pack_z.1 = (f32[5,16,40,128]{3,2,1,0:T(8,128)S(1)}, f32[120,128]{1,0:T(8,128)S(1)}, f32[120,128]{1,0:T(8,128)S(1)}) custom-call(f32[3,4,32,128]{3,2,1,0:T(8,128)} %get-tuple-element.28.low_ref.refs_0_, f32[3,4,32,128]{3,2,1,0:T(8,128)} %get-tuple-element.27.high_ref.refs_1_, f32[3,4,32,128]{3,2,1,0:T(8,128)} %collective-permute-done.below_ref.refs_2_, ...), custom_call_target="tpu_custom_call" | custom-call | flops 1048576 | bytes 1048576 | tf_op jit(solution)/shard_map/pack_z/pallas_call | solution.py:330
  51.8 1.4 %collective-permute-start.8 = (f32[120,128]{1,0:T(8,128)S(1)}, f32[120,128]{1,0:T(8,128)S(1)}, u32[]{:S(2)}, u32[]{:S(2)}) collective-permute-start(f32[120,128]{1,0:T(8,128)S(1)} %get-tuple-element.22), channel_id=1, source_target_pairs={{0,1},{1,2},{2,3},{3,0},{4,5},{5,6},{6,7},{7,4},{8,9},{9,10},{10,1... | collective-permute-start | bytes 184328 | tf_op jit(solution)/shard_map/ppermute | solution.py:447
  53.1 1.5 %collective-permute-start.9 = (f32[120,128]{1,0:T(8,128)S(1)}, f32[120,128]{1,0:T(8,128)S(1)}, u32[]{:S(2)}, u32[]{:S(2)}) collective-permute-start(f32[120,128]{1,0:T(8,128)S(1)} %get-tuple-element.23), channel_id=1, source_target_pairs={{1,0},{2,1},{3,2},{0,3},{5,4},{6,5},{7,6},{4,7},{9,8},{10,9},{11,1... | collective-permute-start | bytes 184328 | tf_op jit(solution)/shard_map/ppermute | solution.py:446
  54.7 1.5 %collective-permute-done.8.before_ref = f32[120,128]{1,0:T(8,128)S(1)} collective-permute-done((f32[120,128]{1,0:T(8,128)S(1)}, f32[120,128]{1,0:T(8,128)S(1)}, u32[]{:S(2)}, u32[]{:S(2)}) %collective-permute-start.8) | collective-permute-done | bytes 61472 | tf_op jit(solution)/shard_map/ppermute | solution.py:447
  56.2 0.0 collective-permute-done.9.after_ref
  56.2 0.0 copy-done.2
  56.2 0.0 copy-start.4
  56.2 16.5 %sweeps.1 = (f32[3,8,32,128]{3,2,1,0:T(8,128)}, f32[576,128]{1,0:T(8,128)S(1)}) custom-call(f32[5,16,40,128]{3,2,1,0:T(8,128)S(1)} %get-tuple-element.21.wide_ref, f32[120,128]{1,0:T(8,128)S(1)} %collective-permute-done.8.before_ref, f32[120,128]{1,0:T(8,128)S(1)} %collective-permute-done.9.after_ref, s32[3,8192]{1,0:T(4,128)S(1)} %copy-done.2), custom_call_target="tpu_custom_call" | custom-call | flops 10995116277760 | bytes 1048576 | tf_op jit(solution)/shard_map/sweeps/pallas_call | solution.py:424
  72.7 22.5 %all_to_all.18 = f32[64,1,1152]{2,1,0:T(1,128)S(1)} all-to-all(f32[64,1,1152]{2,1,0:T(1,128)S(1)} %bitcast.7), channel_id=1, replica_groups=mesh['gx'=8,'gy'=8,'gz'=4] {'gx','gy'}, dimensions={0} | all-to-all | bytes 589824 | tf_op jit(solution)/shard_map/all_to_all | solution.py:475
  95.2 0.0 copy-done.4
  95.3 5.0 %bring_home.1 = f32[9,8192]{1,0:T(8,128)} custom-call(f32[576,128]{1,0:T(8,128)S(1)} %bitcast.8, s32[64,128]{1,0:T(8,128)S(1)} %copy-done.4), custom_call_target="tpu_custom_call" | custom-call | flops 2199023255552 | bytes 1048576 | tf_op jit(solution)/shard_map/bring_home/pallas_call | solution.py:248
  (1 shorter events, 0.0 us)
Async XLA Ops:
  0.7 1.0 %copy-start = (f32[10,8192]{1,0:T(8,128)S(1)}, f32[10,8192]{1,0:T(8,128)}, u32[]{:S(2)}) copy-start(f32[10,8192]{1,0:T(8,128)} %geom_ref.1) | copy-start | bytes 983044
  1.8 0.8 copy-start.3
  2.5 16.2 %copy-start.5 = (f32[3,8,32,128]{3,2,1,0:T(8,128)S(1)}, f32[3,8,32,128]{3,2,1,0:T(8,128)}, u32[]{:S(2)}) copy-start(f32[3,8,32,128]{3,2,1,0:T(8,128)} %param.9) | copy-start | bytes 1179652
  2.5 27.8 %copy-start.1 = (s32[8,32,128]{2,1,0:T(8,128)S(1)}, s32[8,32,128]{2,1,0:T(8,128)}, u32[]{:S(2)}) copy-start(s32[8,32,128]{2,1,0:T(8,128)} %near_ref.1) | copy-start | bytes 393220
  5.7 24.7 %all-to-all-start = ((f32[64,1,640]{2,1,0:T(1,128)}), f32[64,1,640]{2,1,0:T(1,128)S(1)}, u32[]{:S(2)}, u32[]{:S(2)}) async-start(f32[64,1,640]{2,1,0:T(1,128)} %bitcast.1), calls=%async_computation | async-start | bytes 327680 | tf_op jit(solution)/shard_map/all_to_all | solution.py:459
  19.5 20.5 %collective-permute-start = (f32[3,4,32,128]{3,2,1,0:T(8,128)}, f32[3,4,32,128]{3,2,1,0:T(8,128)}, u32[]{:S(2)}, u32[]{:S(2)}) collective-permute-start(f32[3,4,32,128]{3,2,1,0:T(8,128)} %get-tuple-element.27.high_ref.refs_1_), channel_id=1, source_target_pairs={{0,32},{32,64},{64,96},{96,128},{128,160},{160,192},{192,224},{224... | collective-permute-start | bytes 589832 | tf_op jit(solution)/shard_map/ppermute | solution.py:447
  20.9 19.1 %collective-permute-start.1 = (f32[3,4,32,128]{3,2,1,0:T(8,128)}, f32[3,4,32,128]{3,2,1,0:T(8,128)}, u32[]{:S(2)}, u32[]{:S(2)}) collective-permute-start(f32[3,4,32,128]{3,2,1,0:T(8,128)} %get-tuple-element.28.low_ref.refs_0_), channel_id=1, source_target_pairs={{32,0},{64,32},{96,64},{128,96},{160,128},{192,160},{224,192},{0,2... | collective-permute-start | bytes 589832 | tf_op jit(solution)/shard_map/ppermute | solution.py:446
  38.5 17.7 %copy-start.2 = (s32[3,8192]{1,0:T(4,128)S(1)}, s32[3,8192]{1,0:T(4,128)}, u32[]{:S(2)}) copy-start(s32[3,8192]{1,0:T(4,128)} %cell_ref.1) | copy-start | bytes 294916
  38.5 4.7 %collective-permute-start.5 = (f32[2,4,32,128]{3,2,1,0:T(8,128)S(1)}, f32[2,4,32,128]{3,2,1,0:T(8,128)S(1)}, u32[]{:S(2)}, u32[]{:S(2)}) collective-permute-start(f32[2,4,32,128]{3,2,1,0:T(8,128)S(1)} %get-tuple-element.17.low_ref.refs_6_), channel_id=1, source_target_pairs={{32,0},{64,32},{96,64},{128,96},{160,128},{192,160},{224,192},{0,2... | collective-permute-start | bytes 393224 | tf_op jit(solution)/shard_map/ppermute | solution.py:446
  39.3 5.6 %collective-permute-start.4 = (f32[2,4,32,128]{3,2,1,0:T(8,128)S(1)}, f32[2,4,32,128]{3,2,1,0:T(8,128)S(1)}, u32[]{:S(2)}, u32[]{:S(2)}) collective-permute-start(f32[2,4,32,128]{3,2,1,0:T(8,128)S(1)} %get-tuple-element.18.high_ref.refs_7_), channel_id=1, source_target_pairs={{0,32},{32,64},{64,96},{96,128},{128,160},{160,192},{192,224},{224... | collective-permute-start | bytes 393224 | tf_op jit(solution)/shard_map/ppermute | solution.py:447
  41.3 5.2 %collective-permute-start.2 = (f32[192,128]{1,0:T(8,128)S(1)}, f32[192,128]{1,0:T(8,128)S(1)}, u32[]{:S(2)}, u32[]{:S(2)}) collective-permute-start(f32[192,128]{1,0:T(8,128)S(1)} %get-tuple-element.15), channel_id=1, source_target_pairs={{0,4},{4,8},{8,12},{12,16},{16,20},{20,24},{24,28},{28,0},{1,5},{5... | collective-permute-start | bytes 294920 | tf_op jit(solution)/shard_map/ppermute | solution.py:447
  42.4 4.3 %collective-permute-start.3 = (f32[192,128]{1,0:T(8,128)S(1)}, f32[192,128]{1,0:T(8,128)S(1)}, u32[]{:S(2)}, u32[]{:S(2)}) collective-permute-start(f32[192,128]{1,0:T(8,128)S(1)} %get-tuple-element.16), channel_id=1, source_target_pairs={{4,0},{8,4},{12,8},{16,12},{20,16},{24,20},{28,24},{0,28},{5,1},{9... | collective-permute-start | bytes 294920 | tf_op jit(solution)/shard_map/ppermute | solution.py:446
  44.9 2.3 %collective-permute-start.6 = (f32[128,128]{1,0:T(8,128)S(1)}, f32[128,128]{1,0:T(8,128)S(1)}, u32[]{:S(2)}, u32[]{:S(2)}) collective-permute-start(f32[128,128]{1,0:T(8,128)S(1)} %get-tuple-element.19), channel_id=1, source_target_pairs={{0,4},{4,8},{8,12},{12,16},{16,20},{20,24},{24,28},{28,0},{1,5},{5... | collective-permute-start | bytes 196616 | tf_op jit(solution)/shard_map/ppermute | solution.py:447
  45.9 3.7 %collective-permute-start.7 = (f32[128,128]{1,0:T(8,128)S(1)}, f32[128,128]{1,0:T(8,128)S(1)}, u32[]{:S(2)}, u32[]{:S(2)}) collective-permute-start(f32[128,128]{1,0:T(8,128)S(1)} %get-tuple-element.20), channel_id=1, source_target_pairs={{4,0},{8,4},{12,8},{16,12},{20,16},{24,20},{28,24},{0,28},{5,1},{9... | collective-permute-start | bytes 196616 | tf_op jit(solution)/shard_map/ppermute | solution.py:446
  51.8 4.4 %collective-permute-start.8 = (f32[120,128]{1,0:T(8,128)S(1)}, f32[120,128]{1,0:T(8,128)S(1)}, u32[]{:S(2)}, u32[]{:S(2)}) collective-permute-start(f32[120,128]{1,0:T(8,128)S(1)} %get-tuple-element.22), channel_id=1, source_target_pairs={{0,1},{1,2},{2,3},{3,0},{4,5},{5,6},{6,7},{7,4},{8,9},{9,10},{10,1... | collective-permute-start | bytes 184328 | tf_op jit(solution)/shard_map/ppermute | solution.py:447
  53.1 3.1 %collective-permute-start.9 = (f32[120,128]{1,0:T(8,128)S(1)}, f32[120,128]{1,0:T(8,128)S(1)}, u32[]{:S(2)}, u32[]{:S(2)}) collective-permute-start(f32[120,128]{1,0:T(8,128)S(1)} %get-tuple-element.23), channel_id=1, source_target_pairs={{1,0},{2,1},{3,2},{0,3},{5,4},{6,5},{7,6},{4,7},{9,8},{10,9},{11,1... | collective-permute-start | bytes 184328 | tf_op jit(solution)/shard_map/ppermute | solution.py:446
  56.2 39.0 %copy-start.4 = (s32[64,128]{1,0:T(8,128)S(1)}, s32[64,128]{1,0:T(8,128)}, u32[]{:S(2)}) copy-start(s32[64,128]{1,0:T(8,128)} %send_ref.3) | copy-start | bytes 98308

commit v6 on v5

--- a/solution.py
+++ b/solution.py
@@ -286,62 +286,64 @@
     )(low, high, below, above)
 
 
-def pack_z_kernel(*refs):
+def pack_z_kernel(first, refs):
+    low_ref, high_ref, below_ref, above_ref, under_ref, over_ref = refs[0:6]
     wide_ref, down_ref, up_ref = refs[-3:]
     lane = lax.broadcasted_iota(I32, (1, LANE), 1)
     group = lax.shift_right_logical(lane, 2)
-    size_y = refs[0].shape[2]
-    field = 0
-    down = up = None
-    for low_ref, high_ref, below_ref, above_ref, under_ref, over_ref in (refs[0:6], refs[6:12]):
-        at = 0
-        for c in range(low_ref.shape[0]):
-            side = field % 2
-            if side == 0:
-                down = jnp.zeros((size_y + 2 * WIDE, LANE), F32)
-                up = jnp.zeros((size_y + 2 * WIDE, LANE), F32)
-            x = 0
-            for ref in (below_ref, low_ref, high_ref, above_ref):
-                for k in range(WIDE):
-                    wide_ref[field, x, 0:WIDE] = under_ref[at:at + WIDE, :]
-                    wide_ref[field, x, WIDE:WIDE + size_y] = ref[c, k]
-                    wide_ref[field, x, WIDE + size_y:] = over_ref[at:at + WIDE, :]
-                    plane = wide_ref[field, x]
-                    slot = x + 4 * WIDE * side
-                    here = group == slot
-                    shift = WIDE * slot
-                    moved = pltpu.roll(plane, shift, 1) if shift else plane
-                    down = jnp.where(here, moved, down)
-                    shift = (shift + WIDE) % LANE
-                    moved = pltpu.roll(plane, shift, 1) if shift else plane
-                    up = jnp.where(here, moved, up)
-                    at += WIDE
-                    x += 1
-            rows = pl.ds((field // 2) * (size_y + 2 * WIDE), size_y + 2 * WIDE)
-            down_ref[rows, :] = down
-            up_ref[rows, :] = up
-            field += 1
-
-
-def pack_z(first, second):
-    fields = first[0].shape[0] + second[0].shape[0]
-    rows = first[0].shape[2] + 2 * WIDE
-    message = jax.ShapeDtypeStruct(((fields + 1) // 2 * rows, LANE), F32)
-    return pl.pallas_call(
-        pack_z_kernel,
+    size_y = low_ref.shape[2]
+    height = size_y + 2 * WIDE
+    if len(refs) > 9:
+        done = (first + 1) // 2 * height
+        down_ref[0:done, :] = refs[6][...]
+        up_ref[0:done, :] = refs[7][...]
+    at = 0
+    for c in range(low_ref.shape[0]):
+        field = first + c
+        side = field % 2
+        rows = slice((field // 2) * height, (field // 2 + 1) * height)
+        down = down_ref[rows, :] if side else jnp.zeros((height, LANE), F32)
+        up = up_ref[rows, :] if side else jnp.zeros((height, LANE), F32)
+        x = 0
+        for ref in (below_ref, low_ref, high_ref, above_ref):
+            for k in range(WIDE):
+                wide_ref[c, x, 0:WIDE] = under_ref[at:at + WIDE, :]
+                wide_ref[c, x, WIDE:WIDE + size_y] = ref[c, k]
+                wide_ref[c, x, WIDE + size_y:] = over_ref[at:at + WIDE, :]
+                plane = wide_ref[c, x]
+                slot = x + 4 * WIDE * side
+                here = group == slot
+                shift = WIDE * slot
+                moved = pltpu.roll(plane, shift, 1) if shift else plane
+                down = jnp.where(here, moved, down)
+                shift = (shift + WIDE) % LANE
+                moved = pltpu.roll(plane, shift, 1) if shift else plane
+                up = jnp.where(here, moved, up)
+                at += WIDE
+                x += 1
+        down_ref[rows, :] = down
+        up_ref[rows, :] = up
+
+
+def pack_z(first, planes, begun=()):
+    fields, _, size_y, _ = planes[0].shape
+    height = size_y + 2 * WIDE
+    message = jax.ShapeDtypeStruct(((first + fields + 1) // 2 * height, LANE), F32)
+    return pl.pallas_call(
+        lambda *refs: pack_z_kernel(first, refs),
         name="pack_z",
-        out_shape=(jax.ShapeDtypeStruct((fields, 4 * WIDE, rows, LANE), F32), message, message),
-        in_specs=[VMEM] * 12,
+        out_shape=(jax.ShapeDtypeStruct((fields, 4 * WIDE, height, LANE), F32), message, message),
+        in_specs=[VMEM] * (6 + len(begun)),
         out_specs=(VMEM,) * 3,
         compiler_params=pltpu.CompilerParams(vmem_limit_bytes=24 << 20),
         cost_estimate=pl.CostEstimate(flops=1 << 20, bytes_accessed=1 << 20, transcendentals=0),
-    )(*first, *second)
+    )(*planes, *begun)
 
 
 SPARE = 8
 
 
-def sweep_kernel(wide_ref, before_ref, after_ref, cell_ref, out_ref, sample_ref, one_ref, two_ref, coef_ref, table_ref):
+def sweep_kernel(wide_ref, more_ref, before_ref, after_ref, cell_ref, out_ref, sample_ref, one_ref, two_ref, coef_ref, table_ref):
     planes, rows = wide_ref.shape[1:3]
     size_y = rows - 2 * WIDE
     stride = rows + 2 * SPARE
@@ -359,7 +361,7 @@
             near = pltpu.roll(after, (LANE - shift) % LANE, 1) if shift else after
             far = pltpu.roll(before, LANE - WIDE - shift, 1) if LANE - WIDE - shift else before
             edge = jnp.where(lane < WIDE, near, jnp.where(lane >= LANE - WIDE, far, 0.0))
-            one_ref[field, x, SPARE:SPARE + rows] = wide_ref[field, x]
+            one_ref[field, x, SPARE:SPARE + rows] = wide_ref[field, x] if field < 3 else more_ref[field - 3, x]
             one_ref[field, x, stride + SPARE:stride + SPARE + rows] = edge
 
     def neighbours(middle, edge):
@@ -416,7 +418,7 @@
     sample_vertices(out_ref, cell_ref, sample_ref, table_ref)
 
 
-def swept(wide, before, after, cells):
+def swept(wide, more, before, after, cells):
     _, planes, rows, _ = wide.shape
     size_x, size_y = planes - 2 * WIDE, rows - 2 * WIDE
     sources = cells.shape[1] // LANE
@@ -428,7 +430,7 @@
             jax.ShapeDtypeStruct((3, size_x, size_y, LANE), F32),
             jax.ShapeDtypeStruct((sources * 9, LANE), F32),
         ),
-        in_specs=[VMEM] * 4,
+        in_specs=[VMEM] * 5,
         out_specs=(VMEM, VMEM),
         scratch_shapes=[
             pltpu.VMEM((5, planes, 2 * stride, LANE), F32),
@@ -438,7 +440,7 @@
         ],
         compiler_params=pltpu.CompilerParams(vmem_limit_bytes=40 << 20),
         cost_estimate=pl.CostEstimate(flops=10 << 40, bytes_accessed=1 << 20, transcendentals=0),
-    )(wide, before, after, cells)
+    )(wide, more, before, after, cells)
 
 
 def both_ways(down, up, axis):
@@ -467,11 +469,10 @@
     below, above = both_ways(low, high, "gx")
     down, up = pack_y(low, high, below, above)
     under, over = both_ways(down, up, "gy")
-    wide, down, up = pack_z(
-        (vel_low, vel_high, vel_below, vel_above, vel_under, vel_over), (low, high, below, above, under, over)
-    )
+    wide, *begun = pack_z(0, (vel_low, vel_high, vel_below, vel_above, vel_under, vel_over))
+    more, down, up = pack_z(3, (low, high, below, above, under, over), begun)
     before, after = both_ways(down, up, "gz")
-    current, samples = swept(wide, before, after, return_cell)
+    current, samples = swept(wide, more, before, after, return_cell)
     returned = lax.all_to_all(
         samples.reshape(-1, 9 * LANE), ("gx", "gy"), split_axis=0, concat_axis=0, tiled=True
     ).reshape(-1, LANE)

time: 101 us -> 98.2 us (0.972)
  waiting for transfers between devices: 15 us -> 10.7 us
  starting transfers between devices: 23 us -> 24.6 us
  local copies, waits for them, and re-layouts: 2.58 us -> 3.66 us
    ppermute x5, waiting for transfers between devices: 3.44 us -> 1.49 us  [both_ways(): lax.ppermute(down, axis, [((i + 1) % count, i) for i in range(count)])]
    ppermute x5, starting transfers between devices: 4.37 us -> 5.76 us  [both_ways(): lax.ppermute(down, axis, [((i + 1) % count, i) for i in range(count)])]
    ppermute x5, waiting for transfers between devices: 3.64 us -> 2.35 us  [both_ways(): below = lax.ppermute(up, axis, [(i, (i + 1) % count) for i in range(count)])]
    slice x1, local copies, waits for them, and re-layouts: 0.77 us -> 1.84 us  [per_device(): vel_low, vel_high = (velocity[:, :WIDE], velocity[:, WIDE:])]
    all_to_all x1, waiting for transfers between devices: 7.95 us -> 6.9 us  [per_device(): lax.all_to_all(outgoing.reshape(-1, 5 * LANE), ('gx', 'gy'), split_axis=0...]
    pallas_call x1 -> x2, Pallas kernels: 2.19 us -> 2.22 us  [pack_z(): pl.pallas_call(lambda *refs: pack_z_kernel(first, refs), name='pack_z', o...]
  transfers between devices with their start and end apart: 11 -> 11, of which waited for: 7 -> 4; matrix products, arithmetic and copies ran while one was open for 1% -> 2% of each run, Pallas kernels for 9% -> 12%
where the time goes in v6:
time: 98.2 us; the launch traced here: 97.8 us
  Pallas kernels  36.4 us (37%)
  starting transfers between devices  24.6 us (25%)
  blocking collectives  21.5 us (22%)
  waiting for transfers between devices  10.7 us (11%)
  local copies, waits for them, and re-layouts  3.66 us (4%)
    all_to_all x1, blocking collectives, per_device(): lax.all_to_all(samples.reshape(-1, 9 * LANE), ('gx', 'gy'), split_axis=0,...  21.5 us
    pallas_call x1, Pallas kernels, swept(): pl.pallas_call(sweep_kernel, name='sweeps', out_shape=(jax.ShapeDtypeStru...  16.5 us
    all_to_all x1, starting transfers between devices, per_device(): lax.all_to_all(outgoing.reshape(-1, 5 * LANE), ('gx', 'gy'), split_axis=0...  13 us
    pallas_call x1, Pallas kernels, cell_fields(): pl.pallas_call(cell_kernel, name='cell_fields', out_shape=(out, side, sid...  8.17 us
    all_to_all x1, waiting for transfers between devices, per_device(): lax.all_to_all(outgoing.reshape(-1, 5 * LANE), ('gx', 'gy'), split_axis=0...  6.9 us
    ppermute x5, starting transfers between devices, both_ways(): below = lax.ppermute(up, axis, [(i, (i + 1) % count) for i in range(count)])  5.82 us
    ppermute x5, starting transfers between devices, both_ways(): lax.ppermute(down, axis, [((i + 1) % count, i) for i in range(count)])  5.76 us
    pallas_call x1, Pallas kernels, bring_home(): pl.pallas_call(home_kernel, name='bring_home', out_shape=jax.ShapeDtypeSt...  5.04 us
  transfers between devices with their start and end apart: 11, of which 4 were waited for; matrix products, arithmetic and copies ran while one was open for 2% of the time, Pallas kernels for 12%

profile of v6, /device:TPU:1, one launch (start us, length us, event | category | flops | bytes accessed | tf_op | source)
XLA Modules:
  0.0 97.8 jit_solution(16121246593387910430)
XLA Ops:
  0.6 0.1 pad_maximum_fusion.origin_ref
  0.7 0.0 copy-start
  0.7 1.0 %copy-done = f32[10,8192]{1,0:T(8,128)S(1)} copy-done((f32[10,8192]{1,0:T(8,128)S(1)}, f32[10,8192]{1,0:T(8,128)}, u32[]{:S(2)}) %copy-start) | copy-done | bytes 327704
  1.8 0.0 copy-start.3
  1.8 0.8 copy-done.3
  2.5 3.2 %send_tables.1 = f32[320,128]{1,0:T(8,128)} custom-call(f32[10,8192]{1,0:T(8,128)S(1)} %copy-done, s32[64,128]{1,0:T(8,128)S(1)} %copy-done.3, f32[3]{0:T(128)S(1)} %pad_maximum_fusion.origin_ref), custom_call_target="tpu_custom_call" | custom-call | flops 2199023255552 | bytes 1048576 | tf_op jit(solution)/shard_map/send_tables/pallas_call | solution.py:127
  5.7 13.0 %all-to-all-start = ((f32[64,1,640]{2,1,0:T(1,128)}), f32[64,1,640]{2,1,0:T(1,128)S(1)}, u32[]{:S(2)}, u32[]{:S(2)}) async-start(f32[64,1,640]{2,1,0:T(1,128)} %bitcast.1), calls=%async_computation | async-start | bytes 327680 | tf_op jit(solution)/shard_map/all_to_all | solution.py:461
  18.7 0.0 copy-start.1
  18.7 1.8 %fusion = (f32[3,4,32,128]{3,2,1,0:T(8,128)}, f32[3,4,32,128]{3,2,1,0:T(8,128)}) fusion(f32[3,8,32,128]{3,2,1,0:T(8,128)} %param.9), kind=kLoop, calls=%fused_computation.2 | loop fusion | bytes 786432 | tf_op jit(solution)/shard_map/slice | solution.py:456
  20.5 1.4 %collective-permute-start = (f32[3,4,32,128]{3,2,1,0:T(8,128)}, f32[3,4,32,128]{3,2,1,0:T(8,128)}, u32[]{:S(2)}, u32[]{:S(2)}) collective-permute-start(f32[3,4,32,128]{3,2,1,0:T(8,128)} %get-tuple-element.33.high_ref.refs_1_), channel_id=1, source_target_pairs={{0,32},{32,64},{64,96},{96,128},{128,160},{160,192},{192,224},{224... | collective-permute-start | bytes 589832 | tf_op jit(solution)/shard_map/ppermute | solution.py:449
  21.9 1.5 %collective-permute-start.1 = (f32[3,4,32,128]{3,2,1,0:T(8,128)}, f32[3,4,32,128]{3,2,1,0:T(8,128)}, u32[]{:S(2)}, u32[]{:S(2)}) collective-permute-start(f32[3,4,32,128]{3,2,1,0:T(8,128)} %get-tuple-element.34.low_ref.refs_0_), channel_id=1, source_target_pairs={{32,0},{64,32},{96,64},{128,96},{160,128},{192,160},{224,192},{0,2... | collective-permute-start | bytes 589832 | tf_op jit(solution)/shard_map/ppermute | solution.py:448
  23.4 0.1 pad_maximum_fusion.1.origin_ref
  23.5 6.9 %all-to-all-done = f32[64,1,640]{2,1,0:T(1,128)S(1)} async-done(((f32[64,1,640]{2,1,0:T(1,128)}), f32[64,1,640]{2,1,0:T(1,128)S(1)}, u32[]{:S(2)}, u32[]{:S(2)}) %all-to-all-start) | async-done | bytes 163872 | tf_op jit(solution)/shard_map/all_to_all | solution.py:461
  30.4 0.0 copy-done.1
  30.4 8.2 %cell_fields.1 = (f32[8,32,128]{2,1,0:T(8,128)}, f32[2,4,32,128]{3,2,1,0:T(8,128)S(1)}, f32[2,4,32,128]{3,2,1,0:T(8,128)S(1)}) custom-call(f32[320,128]{1,0:T(8,128)S(1)} %bitcast.9, s32[8,32,128]{2,1,0:T(8,128)S(1)} %copy-done.1, f32[3]{0:T(128)S(1)} %pad_maximum_fusion.1.origin_ref), custom_call_target="tpu_custom_call" | custom-call | flops 6597069766656 | bytes 1048576 | tf_op jit(solution)/shard_map/cell_fields/pallas_call | solution.py:177
  38.6 0.5 collective-permute-start.4
  39.1 2.1 %collective-permute-start.5 = (f32[2,4,32,128]{3,2,1,0:T(8,128)S(1)}, f32[2,4,32,128]{3,2,1,0:T(8,128)S(1)}, u32[]{:S(2)}, u32[]{:S(2)}) collective-permute-start(f32[2,4,32,128]{3,2,1,0:T(8,128)S(1)} %get-tuple-element.21.low_ref.refs_0_), channel_id=1, source_target_pairs={{32,0},{64,32},{96,64},{128,96},{160,128},{192,160},{224,192},{0,2... | collective-permute-start | bytes 393224 | tf_op jit(solution)/shard_map/ppermute | solution.py:448
  41.2 0.0 collective-permute-done.below_ref.refs_2_
  41.2 0.0 collective-permute-done.1.above_ref.refs_3_
  41.2 1.3 %pack_y.2 = (f32[192,128]{1,0:T(8,128)S(1)}, f32[192,128]{1,0:T(8,128)S(1)}) custom-call(f32[3,4,32,128]{3,2,1,0:T(8,128)} %get-tuple-element.34.low_ref.refs_0_, f32[3,4,32,128]{3,2,1,0:T(8,128)} %get-tuple-element.33.high_ref.refs_1_, f32[3,4,32,128]{3,2,1,0:T(8,128)} %collective-permute-done.below_ref.refs_2_, ...), custom_call_target="tpu_custom_call" | custom-call | flops 1048576 | bytes 1048576 | tf_op jit(solution)/shard_map/pack_y/pallas_call | solution.py:278
  42.5 1.1 %collective-permute-start.2 = (f32[192,128]{1,0:T(8,128)S(1)}, f32[192,128]{1,0:T(8,128)S(1)}, u32[]{:S(2)}, u32[]{:S(2)}) collective-permute-start(f32[192,128]{1,0:T(8,128)S(1)} %get-tuple-element.18), channel_id=1, source_target_pairs={{0,4},{4,8},{8,12},{12,16},{16,20},{20,24},{24,28},{28,0},{1,5},{5... | collective-permute-start | bytes 294920 | tf_op jit(solution)/shard_map/ppermute | solution.py:449
  43.6 0.0 collective-permute-start.3
  43.6 0.8 collective-permute-done.4.below_ref.refs_2_
  44.4 0.0 collective-permute-done.5.above_ref.refs_3_
  44.5 1.4 %collective-permute-start.6 = (f32[128,128]{1,0:T(8,128)S(1)}, f32[128,128]{1,0:T(8,128)S(1)}, u32[]{:S(2)}, u32[]{:S(2)}) collective-permute-start(f32[128,128]{1,0:T(8,128)S(1)} %get-tuple-element.23), channel_id=1, source_target_pairs={{0,4},{4,8},{8,12},{12,16},{16,20},{20,24},{24,28},{28,0},{1,5},{5... | collective-permute-start | bytes 196616 | tf_op jit(solution)/shard_map/ppermute | solution.py:449
  45.9 0.6 collective-permute-start.7
  46.5 0.0 collective-permute-done.2.refs_4_
  46.5 1.5 %collective-permute-done.3.refs_5_ = f32[192,128]{1,0:T(8,128)S(1)} collective-permute-done((f32[192,128]{1,0:T(8,128)S(1)}, f32[192,128]{1,0:T(8,128)S(1)}, u32[]{:S(2)}, u32[]{:S(2)}) %collective-permute-start.3) | collective-permute-done | bytes 98336 | tf_op jit(solution)/shard_map/ppermute | solution.py:448
  47.9 1.8 %pack_z.2 = (f32[3,16,40,128]{3,2,1,0:T(8,128)S(1)}, f32[80,128]{1,0:T(8,128)S(1)}, f32[80,128]{1,0:T(8,128)S(1)}) custom-call(f32[3,4,32,128]{3,2,1,0:T(8,128)} %get-tuple-element.34.low_ref.refs_0_, f32[3,4,32,128]{3,2,1,0:T(8,128)} %get-tuple-element.33.high_ref.refs_1_, f32[3,4,32,128]{3,2,1,0:T(8,128)} %collective-permute-done.below_ref.refs_2_, ...), custom_call_target="tpu_custom_call" | custom-call | flops 1048576 | bytes 1048576 | tf_op jit(solution)/shard_map/pack_z/pallas_call | solution.py:332
  49.8 0.0 collective-permute-done.6.refs_4_
  49.8 0.0 collective-permute-done.7.refs_5_
  49.8 0.0 copy-start.2
  49.8 0.4 pack_z.3
  50.2 1.4 %collective-permute-start.8 = (f32[120,128]{1,0:T(8,128)S(1)}, f32[120,128]{1,0:T(8,128)S(1)}, u32[]{:S(2)}, u32[]{:S(2)}) collective-permute-start(f32[120,128]{1,0:T(8,128)S(1)} %get-tuple-element.28), channel_id=1, source_target_pairs={{0,1},{1,2},{2,3},{3,0},{4,5},{5,6},{6,7},{7,4},{8,9},{9,10},{10,1... | collective-permute-start | bytes 184328 | tf_op jit(solution)/shard_map/ppermute | solution.py:449
  51.6 1.5 %collective-permute-start.9 = (f32[120,128]{1,0:T(8,128)S(1)}, f32[120,128]{1,0:T(8,128)S(1)}, u32[]{:S(2)}, u32[]{:S(2)}) collective-permute-start(f32[120,128]{1,0:T(8,128)S(1)} %get-tuple-element.29), channel_id=1, source_target_pairs={{1,0},{2,1},{3,2},{0,3},{5,4},{6,5},{7,6},{4,7},{9,8},{10,9},{11,1... | collective-permute-start | bytes 184328 | tf_op jit(solution)/shard_map/ppermute | solution.py:448
  53.1 1.5 %collective-permute-done.8.before_ref = f32[120,128]{1,0:T(8,128)S(1)} collective-permute-done((f32[120,128]{1,0:T(8,128)S(1)}, f32[120,128]{1,0:T(8,128)S(1)}, u32[]{:S(2)}, u32[]{:S(2)}) %collective-permute-start.8) | collective-permute-done | bytes 61472 | tf_op jit(solution)/shard_map/ppermute | solution.py:449
  54.6 0.0 collective-permute-done.9.after_ref
  54.7 0.0 copy-done.2
  54.7 16.5 %sweeps.1 = (f32[3,8,32,128]{3,2,1,0:T(8,128)}, f32[576,128]{1,0:T(8,128)S(1)}) custom-call(f32[3,16,40,128]{3,2,1,0:T(8,128)S(1)} %get-tuple-element.20.wide_ref, f32[2,16,40,128]{3,2,1,0:T(8,128)S(1)} %get-tuple-element.27.more_ref, f32[120,128]{1,0:T(8,128)S(1)} %collective-permute-done.8.before_ref, f32[120,128]{1,0:T(8,128)S(1)} %collective-permute-done.9.after_ref, ...), custom_call_target="tpu_custom_call" | custom-call | flops 10995116277760 | bytes 1048576 | tf_op jit(solution)/shard_map/sweeps/pallas_call | solution.py:426
  71.2 0.0 copy-start.4
  71.2 21.5 %all_to_all.18 = f32[64,1,1152]{2,1,0:T(1,128)S(1)} all-to-all(f32[64,1,1152]{2,1,0:T(1,128)S(1)} %bitcast.7), channel_id=1, replica_groups=mesh['gx'=8,'gy'=8,'gz'=4] {'gx','gy'}, dimensions={0} | all-to-all | bytes 589824 | tf_op jit(solution)/shard_map/all_to_all | solution.py:476
  92.7 0.0 copy-done.4
  92.7 5.0 %bring_home.1 = f32[9,8192]{1,0:T(8,128)} custom-call(f32[576,128]{1,0:T(8,128)S(1)} %bitcast.8, s32[64,128]{1,0:T(8,128)S(1)} %copy-done.4), custom_call_target="tpu_custom_call" | custom-call | flops 2199023255552 | bytes 1048576 | tf_op jit(solution)/shard_map/bring_home/pallas_call | solution.py:248
  (1 shorter events, 0.0 us)
Async XLA Ops:
  0.7 1.0 %copy-start = (f32[10,8192]{1,0:T(8,128)S(1)}, f32[10,8192]{1,0:T(8,128)}, u32[]{:S(2)}) copy-start(f32[10,8192]{1,0:T(8,128)} %geom_ref.1) | copy-start | bytes 983044
  1.8 0.8 copy-start.3
  5.7 24.7 %all-to-all-start = ((f32[64,1,640]{2,1,0:T(1,128)}), f32[64,1,640]{2,1,0:T(1,128)S(1)}, u32[]{:S(2)}, u32[]{:S(2)}) async-start(f32[64,1,640]{2,1,0:T(1,128)} %bitcast.1), calls=%async_computation | async-start | bytes 327680 | tf_op jit(solution)/shard_map/all_to_all | solution.py:461
  18.7 11.7 %copy-start.1 = (s32[8,32,128]{2,1,0:T(8,128)S(1)}, s32[8,32,128]{2,1,0:T(8,128)}, u32[]{:S(2)}) copy-start(s32[8,32,128]{2,1,0:T(8,128)} %near_ref.1) | copy-start | bytes 393220
  20.5 20.7 %collective-permute-start = (f32[3,4,32,128]{3,2,1,0:T(8,128)}, f32[3,4,32,128]{3,2,1,0:T(8,128)}, u32[]{:S(2)}, u32[]{:S(2)}) collective-permute-start(f32[3,4,32,128]{3,2,1,0:T(8,128)} %get-tuple-element.33.high_ref.refs_1_), channel_id=1, source_target_pairs={{0,32},{32,64},{64,96},{96,128},{128,160},{160,192},{192,224},{224... | collective-permute-start | bytes 589832 | tf_op jit(solution)/shard_map/ppermute | solution.py:449
  21.9 19.3 %collective-permute-start.1 = (f32[3,4,32,128]{3,2,1,0:T(8,128)}, f32[3,4,32,128]{3,2,1,0:T(8,128)}, u32[]{:S(2)}, u32[]{:S(2)}) collective-permute-start(f32[3,4,32,128]{3,2,1,0:T(8,128)} %get-tuple-element.34.low_ref.refs_0_), channel_id=1, source_target_pairs={{32,0},{64,32},{96,64},{128,96},{160,128},{192,160},{224,192},{0,2... | collective-permute-start | bytes 589832 | tf_op jit(solution)/shard_map/ppermute | solution.py:448
  38.6 5.9 %collective-permute-start.4 = (f32[2,4,32,128]{3,2,1,0:T(8,128)S(1)}, f32[2,4,32,128]{3,2,1,0:T(8,128)S(1)}, u32[]{:S(2)}, u32[]{:S(2)}) collective-permute-start(f32[2,4,32,128]{3,2,1,0:T(8,128)S(1)} %get-tuple-element.22.high_ref.refs_1_), channel_id=1, source_target_pairs={{0,32},{32,64},{64,96},{96,128},{128,160},{160,192},{192,224},{224... | collective-permute-start | bytes 393224 | tf_op jit(solution)/shard_map/ppermute | solution.py:449
  39.1 5.3 %collective-permute-start.5 = (f32[2,4,32,128]{3,2,1,0:T(8,128)S(1)}, f32[2,4,32,128]{3,2,1,0:T(8,128)S(1)}, u32[]{:S(2)}, u32[]{:S(2)}) collective-permute-start(f32[2,4,32,128]{3,2,1,0:T(8,128)S(1)} %get-tuple-element.21.low_ref.refs_0_), channel_id=1, source_target_pairs={{32,0},{64,32},{96,64},{128,96},{160,128},{192,160},{224,192},{0,2... | collective-permute-start | bytes 393224 | tf_op jit(solution)/shard_map/ppermute | solution.py:448
  42.5 4.0 %collective-permute-start.2 = (f32[192,128]{1,0:T(8,128)S(1)}, f32[192,128]{1,0:T(8,128)S(1)}, u32[]{:S(2)}, u32[]{:S(2)}) collective-permute-start(f32[192,128]{1,0:T(8,128)S(1)} %get-tuple-element.18), channel_id=1, source_target_pairs={{0,4},{4,8},{8,12},{12,16},{16,20},{20,24},{24,28},{28,0},{1,5},{5... | collective-permute-start | bytes 294920 | tf_op jit(solution)/shard_map/ppermute | solution.py:449
  43.6 4.3 %collective-permute-start.3 = (f32[192,128]{1,0:T(8,128)S(1)}, f32[192,128]{1,0:T(8,128)S(1)}, u32[]{:S(2)}, u32[]{:S(2)}) collective-permute-start(f32[192,128]{1,0:T(8,128)S(1)} %get-tuple-element.19), channel_id=1, source_target_pairs={{4,0},{8,4},{12,8},{16,12},{20,16},{24,20},{28,24},{0,28},{5,1},{9... | collective-permute-start | bytes 294920 | tf_op jit(solution)/shard_map/ppermute | solution.py:448
  44.5 5.3 %collective-permute-start.6 = (f32[128,128]{1,0:T(8,128)S(1)}, f32[128,128]{1,0:T(8,128)S(1)}, u32[]{:S(2)}, u32[]{:S(2)}) collective-permute-start(f32[128,128]{1,0:T(8,128)S(1)} %get-tuple-element.23), channel_id=1, source_target_pairs={{0,4},{4,8},{8,12},{12,16},{16,20},{20,24},{24,28},{28,0},{1,5},{5... | collective-permute-start | bytes 196616 | tf_op jit(solution)/shard_map/ppermute | solution.py:449
  45.9 3.9 %collective-permute-start.7 = (f32[128,128]{1,0:T(8,128)S(1)}, f32[128,128]{1,0:T(8,128)S(1)}, u32[]{:S(2)}, u32[]{:S(2)}) collective-permute-start(f32[128,128]{1,0:T(8,128)S(1)} %get-tuple-element.24), channel_id=1, source_target_pairs={{4,0},{8,4},{12,8},{16,12},{20,16},{24,20},{28,24},{0,28},{5,1},{9... | collective-permute-start | bytes 196616 | tf_op jit(solution)/shard_map/ppermute | solution.py:448
  49.8 4.9 %copy-start.2 = (s32[3,8192]{1,0:T(4,128)S(1)}, s32[3,8192]{1,0:T(4,128)}, u32[]{:S(2)}) copy-start(s32[3,8192]{1,0:T(4,128)} %cell_ref.1) | copy-start | bytes 294916
  50.2 4.4 %collective-permute-start.8 = (f32[120,128]{1,0:T(8,128)S(1)}, f32[120,128]{1,0:T(8,128)S(1)}, u32[]{:S(2)}, u32[]{:S(2)}) collective-permute-start(f32[120,128]{1,0:T(8,128)S(1)} %get-tuple-element.28), channel_id=1, source_target_pairs={{0,1},{1,2},{2,3},{3,0},{4,5},{5,6},{6,7},{7,4},{8,9},{9,10},{10,1... | collective-permute-start | bytes 184328 | tf_op jit(solution)/shard_map/ppermute | solution.py:449
  51.6 3.1 %collective-permute-start.9 = (f32[120,128]{1,0:T(8,128)S(1)}, f32[120,128]{1,0:T(8,128)S(1)}, u32[]{:S(2)}, u32[]{:S(2)}) collective-permute-start(f32[120,128]{1,0:T(8,128)S(1)} %get-tuple-element.29), channel_id=1, source_target_pairs={{1,0},{2,1},{3,2},{0,3},{5,4},{6,5},{7,6},{4,7},{9,8},{10,9},{11,1... | collective-permute-start | bytes 184328 | tf_op jit(solution)/shard_map/ppermute | solution.py:448
  71.2 21.5 %copy-start.4 = (s32[64,128]{1,0:T(8,128)S(1)}, s32[64,128]{1,0:T(8,128)}, u32[]{:S(2)}) copy-start(s32[64,128]{1,0:T(8,128)} %send_ref.3) | copy-start | bytes 98308
